TPU v7x, 32 devices: a whole 2x2x4 slice. The times are simulated.
32 devices in a mesh: fsdp: 8 (over z, y), dp: 4 (over x, core).
Axes of the slice: x: 2, y: 2, z: 4, core: 2. Of those that a mesh axis runs over, the one named last changes fastest.
Arguments:
- tokens: bfloat16 [32768, 1024], P(('fsdp', 'dp')), may hold values from -6 to 6
- time_index: int32 [256], P(('fsdp', 'dp')), may hold values from 0 to 127
- time_table: bfloat16 [128, 1024], P(None, 'fsdp'), may hold values from -2.5 to 2.5
- ln1_gain: bfloat16 [1024], P('fsdp'), may hold values from 0.5 to 1.5
- ln1_bias: bfloat16 [1024], P('fsdp'), may hold values from -1.75 to 1.75
- w_qkv: bfloat16 [1024, 3072], P('fsdp'), may hold values from -0.1875 to 0.1875
- w_out: bfloat16 [1024, 1024], P('fsdp'), may hold values from -0.75 to 0.75
- b_out: bfloat16 [1024], P('fsdp'), may hold values from -1.75 to 1.75
- ln2_gain: bfloat16 [1024], P('fsdp'), may hold values from 0.5 to 1.5
- ln2_bias: bfloat16 [1024], P('fsdp'), may hold values from -1.75 to 1.75
- w_up: bfloat16 [1024, 4096], P('fsdp'), may hold values from -0.1875 to 0.1875
- b_up: bfloat16 [4096], P('fsdp'), may hold values from -3 to 3
- w_down: bfloat16 [4096, 1024], P('fsdp'), may hold values from -0.09375 to 0.09375
- b_down: bfloat16 [1024], P('fsdp'), may hold values from -1.75 to 1.75
- cotangent: bfloat16 [32768, 1024], P(('fsdp', 'dp')), may hold values from -6 to 6
Outputs:
- block_out: bfloat16 [32768, 1024], P(('fsdp', 'dp'))
- grad_tokens: bfloat16 [32768, 1024], P(('fsdp', 'dp'))
- grad_table: float32 [128, 1024], P(None, 'fsdp')
- grad_ln1_gain: float32 [1024], P('fsdp')
- grad_ln1_bias: float32 [1024], P('fsdp')
- grad_qkv: float32 [1024, 3072], P('fsdp')
- grad_out_w: float32 [1024, 1024], P('fsdp')
- grad_out_b: float32 [1024], P('fsdp')
- grad_ln2_gain: float32 [1024], P('fsdp')
- grad_ln2_bias: float32 [1024], P('fsdp')
- grad_up: float32 [1024, 4096], P('fsdp')
- grad_up_b: float32 [4096], P('fsdp')
- grad_down: float32 [4096, 1024], P('fsdp')
- grad_down_b: float32 [1024], P('fsdp')
All inputs are finite; a program needn't handle non-finite values.
Results may differ from a plain program's by a relative error of at most 0.012.
Values may be sent and summed in bfloat16 or wider, within the bound.
No kernel may reach another device: no remote copies, remote signals or barrier semaphores. Data moves between devices by JAX's collectives and lax.ppermute only.
A program may use at most 256 MiB of HBM per device.

v0:
```python
import jax
import jax.numpy as jnp
from jax import lax
from jax.sharding import PartitionSpec as P

HEADS = 16


def normalize(values):
    centred = values - jnp.mean(values, axis=-1, keepdims=True)
    spread = jnp.mean(centred * centred, axis=-1, keepdims=True)
    return centred * lax.rsqrt(spread + 1e-05)


def scaled_norm(values, gain):
    return normalize(values) * gain


def exact_gelu(values):
    return jax.nn.gelu(values, approximate=False)


def local(
    tokens,
    time_index,
    time_table,
    ln1_gain,
    ln1_bias,
    w_qkv,
    w_out,
    b_out,
    ln2_gain,
    ln2_bias,
    w_up,
    b_up,
    w_down,
    b_down,
    cotangent,
):
    table_all, gain_one, bias_one, qkv_w, out_w, out_b = (
        lax.all_gather(time_table, "fsdp", axis=1, tiled=True),
        lax.all_gather(ln1_gain, "fsdp", axis=0, tiled=True),
        lax.all_gather(ln1_bias, "fsdp", axis=0, tiled=True),
        lax.all_gather(w_qkv, "fsdp", axis=0, tiled=True),
        lax.all_gather(w_out, "fsdp", axis=0, tiled=True),
        lax.all_gather(b_out, "fsdp", axis=0, tiled=True),
    )
    gain_two, bias_two, up_w, up_b, down_w, down_b = (
        lax.all_gather(ln2_gain, "fsdp", axis=0, tiled=True),
        lax.all_gather(ln2_bias, "fsdp", axis=0, tiled=True),
        lax.all_gather(w_up, "fsdp", axis=0, tiled=True),
        lax.all_gather(b_up, "fsdp", axis=0, tiled=True),
        lax.all_gather(w_down, "fsdp", axis=0, tiled=True),
        lax.all_gather(b_down, "fsdp", axis=0, tiled=True),
    )
    row_count, model_width = tokens.shape
    seq_count = time_index.shape[0]
    length = row_count // seq_count
    head_dim = model_width // HEADS
    factor = head_dim ** (-0.5)
    levels = table_all.shape[0]
    gain_one_f = gain_one.astype(jnp.float32)
    gain_two_f = gain_two.astype(jnp.float32)
    one_hot = time_index[:, None] == jnp.arange(levels, dtype=jnp.int32)[None, :]
    embedding = jnp.dot(one_hot.astype(jnp.bfloat16), table_all, preferred_element_type=jnp.float32)
    scale_seq = (1.0 + embedding)[:, None, :]
    inputs = tokens.astype(jnp.float32)
    normed = (normalize(inputs) * gain_one_f + bias_one.astype(jnp.float32)).reshape(
        seq_count, length, model_width
    )
    scaled = (normed * scale_seq).astype(jnp.bfloat16).reshape(row_count, model_width)
    packed = jnp.dot(scaled, qkv_w, preferred_element_type=jnp.float32).astype(jnp.bfloat16)
    packed = packed.reshape(seq_count, length, 3, HEADS, head_dim)
    queries = packed[:, :, 0]
    key_heads = packed[:, :, 1]
    value_heads = packed[:, :, 2]
    scores = (
        jnp.einsum("sqhd,skhd->shqk", queries, key_heads, preferred_element_type=jnp.float32)
        * factor
    )
    attn_probs = jax.nn.softmax(scores, axis=-1)
    probs_low = attn_probs.astype(jnp.bfloat16)
    attn_mix = jnp.einsum(
        "shqk,skhd->sqhd", probs_low, value_heads, preferred_element_type=jnp.float32
    )
    attn_mix = attn_mix.astype(jnp.bfloat16).reshape(row_count, model_width)
    middle = (
        inputs
        + jnp.dot(attn_mix, out_w, preferred_element_type=jnp.float32)
        + out_b.astype(jnp.float32)
    )
    hidden_in = (normalize(middle) * gain_two_f + bias_two.astype(jnp.float32)).astype(jnp.bfloat16)
    pre_act = jnp.dot(hidden_in, up_w, preferred_element_type=jnp.float32) + up_b.astype(
        jnp.float32
    )
    activated = exact_gelu(pre_act).astype(jnp.bfloat16)
    block_out = (
        middle
        + jnp.dot(activated, down_w, preferred_element_type=jnp.float32)
        + down_b.astype(jnp.float32)
    ).astype(jnp.bfloat16)
    qkv_w, out_w, up_w, down_w = (
        lax.all_gather(w_qkv, "fsdp", axis=0, tiled=True),
        lax.all_gather(w_out, "fsdp", axis=0, tiled=True),
        lax.all_gather(w_up, "fsdp", axis=0, tiled=True),
        lax.all_gather(w_down, "fsdp", axis=0, tiled=True),
    )
    upstream = cotangent.astype(jnp.float32)
    grad_down = jnp.einsum("ti,td->id", activated, cotangent, preferred_element_type=jnp.float32)
    grad_down_b = jnp.sum(upstream, axis=0)
    d_act = jnp.einsum("td,id->ti", cotangent, down_w, preferred_element_type=jnp.float32)
    gelu_pull = jax.vjp(exact_gelu, pre_act)[1]
    d_pre = gelu_pull(d_act)[0].astype(jnp.bfloat16)
    grad_up = jnp.einsum("ti,tf->if", hidden_in, d_pre, preferred_element_type=jnp.float32)
    grad_up_b = jnp.sum(d_pre.astype(jnp.float32), axis=0)
    d_hidden = jnp.einsum("tf,if->ti", d_pre, up_w, preferred_element_type=jnp.float32)
    grad_ln2_bias = jnp.sum(d_hidden, axis=0)
    second_pull = jax.vjp(scaled_norm, middle, gain_two_f)[1]
    d_mid_part, grad_ln2_gain = second_pull(d_hidden)
    d_middle = upstream + d_mid_part
    d_mid_low = d_middle.astype(jnp.bfloat16)
    grad_out_w = jnp.einsum("ti,td->id", attn_mix, d_mid_low, preferred_element_type=jnp.float32)
    grad_out_b = jnp.sum(d_mid_low.astype(jnp.float32), axis=0)
    d_mix = jnp.einsum("td,id->ti", d_mid_low, out_w, preferred_element_type=jnp.float32)
    d_mix = d_mix.astype(jnp.bfloat16).reshape(seq_count, length, HEADS, head_dim)
    d_probs = jnp.einsum("sqhd,skhd->shqk", d_mix, value_heads, preferred_element_type=jnp.float32)
    d_values = jnp.einsum("shqk,sqhd->skhd", probs_low, d_mix, preferred_element_type=jnp.float32)
    d_scores = (
        attn_probs * (d_probs - jnp.sum(d_probs * attn_probs, axis=-1, keepdims=True))
    ).astype(jnp.bfloat16)
    d_queries = (
        jnp.einsum("shqk,skhd->sqhd", d_scores, key_heads, preferred_element_type=jnp.float32)
        * factor
    )
    d_keys = (
        jnp.einsum("shqk,sqhd->skhd", d_scores, queries, preferred_element_type=jnp.float32)
        * factor
    )
    d_packed = (
        jnp.stack([d_queries, d_keys, d_values], axis=2)
        .astype(jnp.bfloat16)
        .reshape(row_count, 3 * model_width)
    )
    grad_qkv = jnp.einsum("ti,tf->if", scaled, d_packed, preferred_element_type=jnp.float32)
    d_scaled = jnp.einsum("tf,if->ti", d_packed, qkv_w, preferred_element_type=jnp.float32).reshape(
        seq_count, length, model_width
    )
    d_normed = d_scaled * scale_seq
    grad_ln1_bias = jnp.sum(d_normed, axis=(0, 1))
    d_embedding = jnp.sum(d_scaled * normed, axis=1)
    grad_table = jnp.einsum(
        "sn,sd->nd", one_hot.astype(jnp.float32), d_embedding, precision=lax.Precision.HIGHEST
    )
    first_pull = jax.vjp(scaled_norm, inputs, gain_one_f)[1]
    d_in_part, grad_ln1_gain = first_pull(d_normed.reshape(row_count, model_width))
    grad_tokens = (d_middle + d_in_part).astype(jnp.bfloat16)
    all_shares = (
        lax.psum_scatter(grad_table, "fsdp", scatter_dimension=1, tiled=True),
        lax.psum_scatter(grad_ln1_gain, "fsdp", scatter_dimension=0, tiled=True),
        lax.psum_scatter(grad_ln1_bias, "fsdp", scatter_dimension=0, tiled=True),
        lax.psum_scatter(grad_qkv, "fsdp", scatter_dimension=0, tiled=True),
        lax.psum_scatter(grad_out_w, "fsdp", scatter_dimension=0, tiled=True),
        lax.psum_scatter(grad_out_b, "fsdp", scatter_dimension=0, tiled=True),
        lax.psum_scatter(grad_ln2_gain, "fsdp", scatter_dimension=0, tiled=True),
        lax.psum_scatter(grad_ln2_bias, "fsdp", scatter_dimension=0, tiled=True),
        lax.psum_scatter(grad_up, "fsdp", scatter_dimension=0, tiled=True),
        lax.psum_scatter(grad_up_b, "fsdp", scatter_dimension=0, tiled=True),
        lax.psum_scatter(grad_down, "fsdp", scatter_dimension=0, tiled=True),
        lax.psum_scatter(grad_down_b, "fsdp", scatter_dimension=0, tiled=True),
    )
    (
        share_table,
        share_gain_one,
        share_bias_one,
        share_qkv,
        share_out_w,
        share_out_b,
        share_gain_two,
        share_bias_two,
        share_up,
        share_up_b,
        share_down,
        share_down_b,
    ) = all_shares
    summed = lax.psum(
        (
            share_table,
            share_gain_one,
            share_bias_one,
            share_qkv,
            share_out_w,
            share_out_b,
            share_gain_two,
            share_bias_two,
            share_up,
            share_up_b,
            share_down,
            share_down_b,
        ),
        "dp",
    )
    return (
        block_out,
        grad_tokens,
        summed[0],
        summed[1],
        summed[2],
        summed[3],
        summed[4],
        summed[5],
        summed[6],
        summed[7],
        summed[8],
        summed[9],
        summed[10],
        summed[11],
    )


def solution(mesh):
    in_specs = (
        P(("fsdp", "dp"), None),
        P(("fsdp", "dp")),
        P(None, "fsdp"),
        P("fsdp"),
        P("fsdp"),
        P("fsdp", None),
        P("fsdp", None),
        P("fsdp"),
        P("fsdp"),
        P("fsdp"),
        P("fsdp", None),
        P("fsdp"),
        P("fsdp", None),
        P("fsdp"),
        P(("fsdp", "dp"), None),
    )
    out_specs = (
        P(("fsdp", "dp"), None),
        P(("fsdp", "dp"), None),
        P(None, "fsdp"),
        P("fsdp"),
        P("fsdp"),
        P("fsdp", None),
        P("fsdp", None),
        P("fsdp"),
        P("fsdp"),
        P("fsdp"),
        P("fsdp", None),
        P("fsdp"),
        P("fsdp", None),
        P("fsdp"),
    )
    return jax.shard_map(local, mesh=mesh, in_specs=in_specs, out_specs=out_specs, check_vma=False)
```

profile of v0, /device:TPU:1, one launch (start us, length us, event | category | flops | bytes accessed | tf_op | source)
XLA Modules:
  0.0 1620.3 jit_solution(10055201754899174732)
XLA Ops:
  10.7 18.2 %all-gather = bf16[8,1,128]{2,1,0:T(2,128)(2,1)S(1)} all-gather(bf16[1,1,128]{2,1,0:T(2,128)(2,1)} %bitcast.124), channel_id=1, replica_groups=mesh['fsdp'=8,'dp'=4] {'fsdp'}, dimensions={0}, use_global_device_ids=true | all-gather | bytes 2304 | tf_op jit(solution)/shard_map/all_gather | solution.py:42
  28.9 13.1 all-gather.1
  42.0 15.0 all-gather.2
  57.0 13.1 all-gather.3
  70.1 15.5 all-gather.4
  85.6 22.5 %all-gather.5 = bf16[8,1,512]{2,1,0:T(2,128)(2,1)S(1)} all-gather(bf16[1,1,512]{2,1,0:T(2,128)(2,1)S(1)} %reshape.133), channel_id=1, replica_groups=mesh['fsdp'=8,'dp'=4] {'fsdp'}, dimensions={0}, use_global_device_ids=true | all-gather | bytes 9216 | tf_op jit(solution)/shard_map/all_gather | solution.py:52
  108.2 2.9 copy.73
  111.0 4.6 copy.82
  115.7 22.8 %all_gather.42 = bf16[128,1024]{1,0:T(8,128)(2,1)S(1)} all-gather(bf16[128,128]{1,0:T(8,128)(2,1)S(1)} %copy-done.50), channel_id=1, replica_groups=mesh['fsdp'=8,'dp'=4] {'fsdp'}, dimensions={1}, use_global_device_ids=true | all-gather | bytes 294912 | tf_op jit(solution)/shard_map/all_gather | solution.py:41
  139.3 2.5 mul.197
  141.7 5.4 copy.104
  149.3 3.3 fusion.21
  152.6 5.4 copy.106
  158.1 11.3 convolution_convert_fusion
  169.4 16.2 reshape.152
  185.5 9.2 fusion.64
  194.7 5.8 copy.112
  200.5 5.8 copy.111
  206.3 5.8 copy.113
  212.1 3.6 fusion.33
  215.6 8.3 fusion.65
  225.2 2.0 copy-done.9
  227.3 3.1 copy.80
  230.4 4.9 fusion.66
  235.4 2.0 copy-done.6
  238.4 51.1 %all-gather.16.cloned.1.call-done = bf16[1024,4096]{1,0:T(8,128)(2,1)} async-done(((bf16[128,4096]{1,0:T(8,128)(2,1)}), bf16[1024,4096]{1,0:T(8,128)(2,1)}) %all-gather.16.cloned.1.call-update) | async-done | bytes 8388624 | tf_op jit(solution)/shard_map/all_gather | solution.py:51
  289.5 16.9 %fusion.59 = f32[1024,4096]{1,0:T(8,128)} fusion(bf16[1024,4096]{1,0:T(8,128)(2,1)} %all-gather.16.cloned.1.call-done, f32[1024,1024]{0,1:T(8,128)} %copy-done.6, f32[1024]{0:T(1024)S(1)} %bitcast.120, f32[1024]{0:T(1024)S(1)} %bitcast.115, f32[1024]{0:T(1024)S(1)} %fusion.54, f32[1024]{0:T(1024)S(1)} %broadcast_multiply_fusion.1), kind=kOutput, calls=%fused_computation.102 | convolution fusion | flops 8595177472 | bytes 29376512 | tf_op jit(solution)/shard_map/dot_general | solution.py:93
  306.4 108.2 %all-gather.18.cloned.1.call-done = bf16[4096,1024]{1,0:T(8,128)(2,1)} async-done(((bf16[512,1024]{1,0:T(8,128)(2,1)}), bf16[4096,1024]{1,0:T(8,128)(2,1)}) %all-gather.18.cloned.1.call-update) | async-done | bytes 8388624 | tf_op jit(solution)/shard_map/all_gather | solution.py:53
  414.6 51.7 %convert_reduce_fusion = (f32[4096]{0:T(1024)}, bf16[1024,4096]{1,0:T(8,128)(2,1)S(1)}, f32[1024,4096]{1,0:T(8,128)}) fusion(f32[1024,4096]{1,0:T(8,128)} %fusion.59, f32[4096]{0:T(1024)S(1)} %bitcast.113, bf16[1024,1024]{1,0:T(8,128)(2,1)S(1)} %copy-done.20, bf16[4096,1024]{1,0:T(8,128)(2,1)} %all-gather.18.cloned.1.call-done), kind=kOutput, calls=%fused_computation.3 | convolution fusion | flops 8904503296 | bytes 52461568 | tf_op jit(solution)/shard_map/td,id->ti/dot_general | solution.py:111
  466.3 11.0 fusion.67
  477.3 5.6 copy.83
  483.0 5.4 multiply_reduce_fusion.2
  493.0 3.7 convolution_convert_fusion.1
  496.7 6.4 reshape.153
  503.1 5.8 copy.85
  509.0 8.5 convolution_bitcast_fusion
  517.5 5.5 multiply_reduce_fusion
  523.1 3.1 multiply_convert_fusion.1
  526.2 3.0 multiply_bitcast_fusion
  531.5 2.2 copy.90
  535.9 10.4 fusion.62
  547.7 6.0 fusion.28
  553.9 15.6 copy.94
  569.5 9.5 fusion.8
  579.7 16.6 %fusion.58 = f32[1024,4096]{1,0:T(8,128)} fusion(bf16[1024,4096]{1,0:T(8,128)(2,1)} %copy-done.63, f32[1024,1024]{0,1:T(8,128)} %copy-done.6, f32[1024]{0:T(1024)S(1)} %bitcast.121, f32[1024]{0:T(1024)S(1)} %bitcast.118, f32[1024]{0:T(1024)S(1)} %copy-done.45, f32[1024]{0:T(1024)S(1)} %copy-done.39), kind=kOutput, calls=%fused_computation.101 | convolution fusion | flops 8595177472 | bytes 29376512 | tf_op jit(solution)/shard_map/ti,tf->if/dot_general | solution.py:114
  597.1 12.3 multiply_convert_fusion
  609.4 3.3 copy-done.15
  612.7 11.5 fusion.68
  626.7 15.0 all-gather.6
  641.8 58.0 %reduce-scatter.10.cloned.1.call-done = f32[128,1024]{1,0:T(8,128)} async-done(((f32[1024,1024]{1,0:T(8,128)}), f32[128,1024]{1,0:T(8,128)}) %reduce-scatter.10.cloned.1.call-update) | async-done | bytes 524304 | tf_op jit(solution)/shard_map/reduce_scatter | solution.py:162
  699.7 210.7 %reduce-scatter.8.cloned.1.call-done = f32[128,3072]{1,0:T(8,128)} async-done(((f32[1024,3072]{1,0:T(8,128)}), f32[128,3072]{1,0:T(8,128)}) %reduce-scatter.8.cloned.1.call-update) | async-done | bytes 1572880 | tf_op jit(solution)/shard_map/reduce_scatter | solution.py:161
  910.4 285.1 %reduce-scatter.12.cloned.1.call-done = f32[128,4096]{1,0:T(8,128)} async-done(((f32[1024,4096]{1,0:T(8,128)}), f32[128,4096]{1,0:T(8,128)}) %reduce-scatter.12.cloned.1.call-update) | async-done | bytes 2097168 | tf_op jit(solution)/shard_map/reduce_scatter | solution.py:166
  1195.5 285.7 %reduce-scatter.14.cloned.1.call-done = f32[512,1024]{1,0:T(8,128)} async-done(((f32[4096,1024]{1,0:T(8,128)}), f32[512,1024]{1,0:T(8,128)}) %reduce-scatter.14.cloned.1.call-update) | async-done | bytes 2097168 | tf_op jit(solution)/shard_map/reduce_scatter | solution.py:168
  1481.2 14.4 add_convert_fusion.2
  1495.6 2.6 copy.96
  1498.2 5.5 copy.105
  1503.7 3.2 fusion.24
  1507.3 2.1 fusion.22
  1509.8 3.5 convert_reduce_fusion.2
  1513.3 28.5 %all-reduce.7 = (f32[1024]{0:T(1024)S(1)}, f32[1024]{0:T(1024)S(1)}, f32[1024]{0:T(1024)S(1)}, f32[1024]{0:T(1024)S(1)}, f32[1024]{0:T(1024)S(1)}, /*index=5*/f32[4096]{0:T(1024)S(1)}, f32[1024]{0:T(1024)S(1)}) all-reduce(f32[1024]{0:T(1024)S(1)} %get-tuple-element.58, ...), channel_id=3, replica_groups=mesh['fsdp'=8,'dp'=4] {'fsdp'}, use_global_device_ids=true, to_apply=%region_15.0.clone | all-reduce | flops 10240 | bytes 81920
  1542.2 4.0 copy.97
  1546.3 13.6 all-reduce.8
  1559.9 44.1 %all-reduce.12.cloned.1.call-done = (f32[128,128]{1,0:T(8,128)}, f32[128,3072]{1,0:T(8,128)}, f32[128,1024]{1,0:T(8,128)}, f32[128,4096]{1,0:T(8,128)}, f32[512,1024]{1,0:T(8,128)}) async-done(((f32[128,128]{1,0:T(8,128)}, f32[128,3072]{1,0:T(8,128)}, f32[128,1024]{1,0:T(8,128)}, f32[128,4096]{1,0:T(8,128)}, f32[512,1024]{1,0:T(8,128)}), (f32[128,128]{1,0:T(8,128)}, f32[128,3072]{1,0:T(8,128)}, ...) | async-done | bytes 6357008 | tf_op jit(solution)/shard_map/psum | solution.py:185
  1605.6 2.9 copy.138
  (191 shorter events, 29.8 us)
Async XLA Ops:
  7.2 150.9 %all-gather.12.cloned.1.call-start = ((), (), s32[]{:S(2)}) async-start(), calls=%async_computation.5 | async-start | bytes 7077888 | tf_op jit(solution)/shard_map/all_gather | solution.py:44
  7.9 222.5 %all-gather.14.cloned.1.call-start = ((), (), s32[]{:S(2)}) async-start(), calls=%async_computation.6 | async-start | bytes 2359296 | tf_op jit(solution)/shard_map/all_gather | solution.py:45
  8.7 280.8 %all-gather.16.cloned.1.call-start = ((), (), s32[]{:S(2)}) async-start(), calls=%async_computation.7 | async-start | bytes 9437184 | tf_op jit(solution)/shard_map/all_gather | solution.py:51
  9.4 405.2 %all-gather.18.cloned.1.call-start = ((), (), s32[]{:S(2)}) async-start(), calls=%async_computation.8 | async-start | bytes 9437184 | tf_op jit(solution)/shard_map/all_gather | solution.py:53
  10.0 631.8 %reduce-scatter.6.cloned.1.call-start = ((), (), s32[]{:S(2)}) async-start(), calls=%async_computation.9 | async-start | bytes 589824 | tf_op jit(solution)/shard_map/reduce_scatter | solution.py:158
  28.9 119.8 %copy-start.32 = (f32[8,1,128]{2,1,0:T(1,128)}, f32[8,1,128]{2,1,0:T(1,128)S(1)}, u32[]{:S(2)}) copy-start(f32[8,1,128]{2,1,0:T(1,128)S(1)} %convert_element_type.113) | copy-start | bytes 12292
  70.1 219.4 %copy-start.42 = (f32[8,1,128]{2,1,0:T(1,128)}, f32[8,1,128]{2,1,0:T(1,128)S(1)}, u32[]{:S(2)}) copy-start(f32[8,1,128]{2,1,0:T(1,128)S(1)} %convert_element_type.116) | copy-start | bytes 12292
  85.6 203.9 %copy-start.55 = (f32[8,1,128]{2,1,0:T(1,128)}, f32[8,1,128]{2,1,0:T(1,128)S(1)}, u32[]{:S(2)}) copy-start(f32[8,1,128]{2,1,0:T(1,128)S(1)} %convert_element_type.117) | copy-start | bytes 12292
  108.1 306.5 %copy-start.36 = (f32[8,1,512]{2,1,0:T(1,128)}, f32[8,1,512]{2,1,0:T(1,128)S(1)}, u32[]{:S(2)}) copy-start(f32[8,1,512]{2,1,0:T(1,128)S(1)} %convert_element_type.118) | copy-start | bytes 49156
  108.1 7.5 copy-start.50
  108.2 30.3 %copy-start.57 = (s32[8]{0:T(128)S(1)}, s32[8]{0:T(128)}, u32[]{:S(2)}) copy-start(s32[8]{0:T(128)} %param.16) | copy-start | bytes 100
  111.0 119.4 %copy-start = (bf16[1024,1024]{0,1:T(8,128)(2,1)}, bf16[1024,1024]{0,1:T(8,128)(2,1)S(1)}, u32[]{:S(2)}) copy-start(bf16[1024,1024]{0,1:T(8,128)(2,1)S(1)} %copy.73) | copy-start | bytes 6291460
  147.5 5.1 copy-start.28
  148.7 3.9 copy-start.34
  215.6 8.3 copy-start.17
  223.9 3.2 copy-start.9
  223.9 3.4 copy-start.26
  235.4 71.1 %copy-start.38 = (f32[1024]{0:T(1024)}, f32[1024]{0:T(1024)S(1)}, u32[]{:S(2)}) copy-start(f32[1024]{0:T(1024)S(1)} %broadcast_multiply_fusion.1) | copy-start | bytes 12292
  238.4 68.0 %copy-start.44 = (f32[1024]{0:T(1024)}, f32[1024]{0:T(1024)S(1)}, u32[]{:S(2)}) copy-start(f32[1024]{0:T(1024)S(1)} %fusion.54) | copy-start | bytes 12292
  289.5 125.1 %copy-start.20 = (bf16[1024,1024]{1,0:T(8,128)(2,1)S(1)}, bf16[1024,1024]{1,0:T(8,128)(2,1)}, u32[]{:S(2)}) copy-start(bf16[1024,1024]{1,0:T(8,128)(2,1)} %param.29) | copy-start | bytes 6291460
  414.6 51.7 %copy-start.60 = (bf16[1024,4096]{1,0:T(8,128)(2,1)S(1)}, bf16[1024,4096]{1,0:T(8,128)(2,1)}, u32[]{:S(2)}) copy-start(bf16[1024,4096]{1,0:T(8,128)(2,1)} %all-gather.16.cloned.1.call-done) | copy-start | bytes 25165828
  466.3 11.0 copy-start.63
  477.3 5.6 copy-start.39
  477.3 5.6 copy-start.43
  477.3 5.6 copy-start.45
  482.9 5.4 copy-start.49
  483.0 5.4 copy-start.7
  483.0 5.9 copy-start.8
  490.5 2.5 copy-start.61
  503.1 5.8 copy-start.27
  508.9 8.5 copy-start.18
  508.9 8.5 copy-start.19
  508.9 14.1 slice-start
  517.5 5.6 slice-start.1
  523.1 3.1 copy-start.12
  526.2 3.0 copy-start.13
  531.5 4.1 copy-start.3
  531.5 4.5 copy-start.16
  531.5 4.5 copy-start.31
  535.9 10.4 copy-start.58
  547.6 152.1 %reduce-scatter.10.cloned.1.call-start = ((), (), s32[]{:S(2)}) async-start(), calls=%async_computation.11 | async-start | bytes 4718592 | tf_op jit(solution)/shard_map/reduce_scatter | solution.py:162
  553.7 15.8 copy-start.24
  553.7 356.7 %reduce-scatter.8.cloned.1.call-start = ((), (), s32[]{:S(2)}) async-start(), calls=%async_computation.10 | async-start | bytes 14155776 | tf_op jit(solution)/shard_map/reduce_scatter | solution.py:161
  579.1 616.4 %reduce-scatter.12.cloned.1.call-start = ((), (), s32[]{:S(2)}) async-start(), calls=%async_computation.12 | async-start | bytes 18874368 | tf_op jit(solution)/shard_map/reduce_scatter | solution.py:166
  596.4 884.8 %reduce-scatter.14.cloned.1.call-start = ((), (), s32[]{:S(2)}) async-start(), calls=%async_computation.13 | async-start | bytes 18874368 | tf_op jit(solution)/shard_map/reduce_scatter | solution.py:168
  597.1 15.6 copy-start.21
  609.4 3.3 copy-start.15
  624.2 2.5 copy-start.59
  624.2 979.8 %all-reduce.12.cloned.1.call-start = ((), (), s32[]{:S(2)}) async-start(), calls=%async_computation.14 | async-start | bytes 12713984 | tf_op jit(solution)/shard_map/psum | solution.py:185
  1498.1 5.5 copy-start.1
  1498.2 5.5 copy-start.29
  1498.2 5.5 copy-start.33
  1503.7 3.2 copy-start.47
  1503.7 3.6 copy-start.2
  1503.7 3.6 copy-start.35
  1506.9 2.5 copy-start.5
  1506.9 2.9 copy-start.11
  1506.9 2.9 copy-start.41
  1509.8 3.5 copy-start.51
  1509.8 3.5 copy-start.52
  1509.8 3.5 copy-start.53
  1509.8 3.5 copy-start.54
  1604.0 6.4 copy-start.23
  1605.6 6.1 copy-start.22
  (12 other events, 15.2 us)
Sparse Core Ops, SparseCore 0:
  10.2 100.9 all-gather.11
  113.3 48.7 all-gather.13
  164.2 125.2 all-gather.15
  291.5 123.1 all-gather.17
  547.8 59.1 reduce-scatter.5
  610.8 88.8 reduce-scatter.9
  703.3 207.0 reduce-scatter.7
  914.2 281.2 reduce-scatter.11
  1199.7 281.3 reduce-scatter.13
  1483.7 120.2 all-reduce.11
where the time goes:
time: 1630 us; the launch traced here: 1620 us
  waiting for transfers between devices  1050 us (64%)
  matrix products  192 us (12%)
  blocking collectives  177 us (11%)
  local copies, waits for them, and re-layouts  142 us (9%)
  other arithmetic  45.7 us (3%)
  between operations  16.5 us (1%)
    reduce_scatter x1, waiting for transfers between devices, local(): lax.psum_scatter(grad_down, 'fsdp', scatter_dimension=0, tiled=True)  286 us
    reduce_scatter x1, waiting for transfers between devices, local(): lax.psum_scatter(grad_up, 'fsdp', scatter_dimension=0, tiled=True)  285 us
    reduce_scatter x1, waiting for transfers between devices, local(): lax.psum_scatter(grad_qkv, 'fsdp', scatter_dimension=0, tiled=True)  211 us
    all_gather x1, waiting for transfers between devices, local(): lax.all_gather(w_down, 'fsdp', axis=0, tiled=True)  108 us
    unnamed x153, local copies, waits for them, and re-layouts  59.4 us
    reduce_scatter x1, waiting for transfers between devices, local(): lax.psum_scatter(grad_out_w, 'fsdp', scatter_dimension=0, tiled=True)  58 us
    dot_general x1, matrix products, local(): jnp.einsum('td,id->ti', cotangent, down_w, preferred_element_type=jnp.flo...  51.7 us
    all_gather x1, waiting for transfers between devices, local(): lax.all_gather(w_up, 'fsdp', axis=0, tiled=True)  51.1 us
  transfers between devices with their start and end apart: 10, of which 7 were waited for; matrix products, arithmetic and copies ran while one was open for 14% of the time, Pallas kernels for 0%

commit v1 on v0

--- a/solution.py
+++ b/solution.py
@@ -1,9 +1,225 @@
+import functools
+
 import jax
 import jax.numpy as jnp
 from jax import lax
+from jax.experimental import pallas as pl
+from jax.experimental.pallas import tpu as pltpu
 from jax.sharding import PartitionSpec as P
 
 HEADS = 16
+BOTH = ("fsdp", "dp")
+
+
+def flips(which):
+    pairs = []
+    for f in range(8):
+        for d in range(4):
+            z, y, x, c = f // 2, f % 2, d // 2, d % 2
+            if which == "x":
+                x = 1 - x
+            elif which == "y":
+                y = 1 - y
+            elif which == "c":
+                c = 1 - c
+            elif which == "z1":
+                z = z ^ 1
+            elif which == "z2":
+                z = z ^ 2
+            pairs.append((f * 4 + d, (z * 2 + y) * 4 + x * 2 + c))
+    return pairs
+
+
+def swap(values, which):
+    return lax.ppermute(values, BOTH, flips(which))
+
+
+def coords():
+    f, d = lax.axis_index("fsdp"), lax.axis_index("dp")
+    return f // 2, f % 2, d // 2, d % 2
+
+
+def part(values, start, size, axis):
+    return lax.dynamic_slice_in_dim(values, start, size, axis)
+
+
+class Split:
+    def __init__(self, n):
+        self.n = n
+        self.e = n * 3 // 8
+        self.m = n - 2 * self.e
+        self.eh = self.e // 2
+        self.mh = self.m // 2
+
+    def e_start(self, x, c):
+        return x * (self.n - self.e) + c * self.eh
+
+    def m_start(self, c):
+        return self.e + c * self.mh
+
+
+def spread(own, split, axis):
+    z, y, x, c = coords()
+    piece = jnp.concatenate(
+        [
+            part(own, split.e_start(x, c), split.eh, axis),
+            part(own, split.m_start(c), split.mh, axis),
+        ],
+        axis=axis,
+    )
+    near = swap(piece, "z1")
+    two = jnp.stack([piece, near])
+    far = swap(two, "z2")
+    four = jnp.concatenate([two, far])
+    beside = swap(four, "y")
+    seven = jnp.concatenate([near[None], far, beside])
+    across = swap(lax.slice_in_dim(seven, 0, split.eh, axis=axis + 1), "x")
+    return seven, across, swap(seven, "c"), swap(across, "c")
+
+
+def assemble_kernel(split, axis, where_ref, own, seven, across, seven_c, across_c, out, sems, out_sems, hold):
+    z, y, x, c = where_ref[0], where_ref[1], where_ref[2], where_ref[3]
+    rows = own.shape[0]
+    unit = 128 if axis == 1 else 16
+
+    def at(ref, base, start, size):
+        start = pl.multiple_of(start, unit)
+        if axis == 1:
+            return ref.at[pl.ds(base, rows), pl.ds(start, size)]
+        return ref.at[pl.ds(pl.multiple_of(base + start, unit), size), :]
+
+    def cut(ref, j, start, size):
+        if axis == 1:
+            return ref.at[j, :, pl.ds(start, size)]
+        return ref.at[j, pl.ds(start, size), :]
+
+    shards = []
+    for j in range(8):
+        zz = (z, z ^ 1, z ^ 2, z ^ 3)[j % 4]
+        yy = y if j < 4 else 1 - y
+        shards.append(zz * 2 + yy)
+    groups = []
+    for j in range(8):
+        base = pl.multiple_of(shards[j] * rows, rows)
+        if j == 0:
+            copies = [(own, hold.at[pl.ds(base, rows), :])]
+        else:
+            k = j - 1
+            oc = 1 - c
+            copies = [
+                (cut(seven, k, 0, split.eh), at(hold, base, split.e_start(x, c), split.eh)),
+                (cut(seven, k, split.eh, split.mh), at(hold, base, split.m_start(c), split.mh)),
+                (across.at[k], at(hold, base, split.e_start(1 - x, c), split.eh)),
+                (cut(seven_c, k, 0, split.eh), at(hold, base, split.e_start(x, oc), split.eh)),
+                (cut(seven_c, k, split.eh, split.mh), at(hold, base, split.m_start(oc), split.mh)),
+                (across_c.at[k], at(hold, base, split.e_start(1 - x, oc), split.eh)),
+            ]
+        group = [pltpu.make_async_copy(s, d, sems.at[j]) for s, d in copies]
+        for copy in group:
+            copy.start()
+        groups.append(group)
+    outs = []
+    for j in range(8):
+        base = pl.multiple_of(shards[j] * rows, rows)
+        for copy in groups[j]:
+            copy.wait()
+        copy = pltpu.make_async_copy(hold.at[pl.ds(base, rows), :], out.at[pl.ds(base, rows), :], out_sems.at[j])
+        copy.start()
+        outs.append(copy)
+    for copy in outs:
+        copy.wait()
+
+
+def assemble(where, own, parts, split, axis):
+    rows, cols = own.shape
+    anywhere = pl.BlockSpec(memory_space=pl.ANY)
+    return pl.pallas_call(
+        functools.partial(assemble_kernel, split, axis),
+        out_shape=jax.ShapeDtypeStruct((8 * rows, cols), own.dtype),
+        grid_spec=pltpu.PrefetchScalarGridSpec(
+            num_scalar_prefetch=1,
+            grid=(),
+            in_specs=[anywhere] * 5,
+            out_specs=anywhere,
+            scratch_shapes=[
+                pltpu.SemaphoreType.DMA((8,)),
+                pltpu.SemaphoreType.DMA((8,)),
+                pltpu.VMEM((8 * rows, cols), own.dtype),
+            ],
+        ),
+        compiler_params=pltpu.CompilerParams(vmem_limit_bytes=32 * 2**20),
+        cost_estimate=pl.CostEstimate(flops=0, bytes_accessed=32 * rows * cols, transcendentals=0),
+    )(where, own, *parts)
+
+
+def small_kernel(where_ref, parts, out, sems):
+    z, y = where_ref[0], where_ref[1]
+    copies = []
+    for j in range(8):
+        zz = (z, z ^ 1, z ^ 2, z ^ 3)[j % 4]
+        yy = y if j < 4 else 1 - y
+        start = pl.multiple_of((zz * 2 + yy) * 128, 128)
+        copies.append(pltpu.make_async_copy(parts.at[j], out.at[:, pl.ds(start, 128)], sems.at[j]))
+    for copy in copies:
+        copy.start()
+    for copy in copies:
+        copy.wait()
+
+
+def gather_small(where, own):
+    near = jnp.stack([own, swap(own, "z1")])
+    four = jnp.concatenate([near, swap(near, "z2")])
+    eight = jnp.concatenate([four, swap(four, "y")])
+    return pl.pallas_call(
+        small_kernel,
+        out_shape=jax.ShapeDtypeStruct((own.shape[0], 1024), own.dtype),
+        grid_spec=pltpu.PrefetchScalarGridSpec(
+            num_scalar_prefetch=1,
+            grid=(),
+            in_specs=[pl.BlockSpec(memory_space=pltpu.VMEM)],
+            out_specs=pl.BlockSpec(memory_space=pltpu.VMEM),
+            scratch_shapes=[pltpu.SemaphoreType.DMA((8,))],
+        ),
+    )(where, eight)
+
+
+def reduce_grad(grad, first):
+    z, y, x, c = coords()
+    rows, cols = grad.shape
+    r, quarter = rows // 8, cols // 4
+    low = jnp.bfloat16
+    f32 = jnp.float32
+    away = part(grad, (1 - c) * 2 * quarter, 2 * quarter, 1).astype(low)
+    mine = part(grad, c * 2 * quarter, 2 * quarter, 1).astype(f32)
+    half = (mine + swap(away, "c").astype(f32)).reshape(4, 2, r, 2 * quarter)
+
+    def over_x(v):
+        away = part(v, (1 - x) * quarter, quarter, v.ndim - 1).astype(low)
+        return part(v, x * quarter, quarter, v.ndim - 1).astype(f32) + swap(away, "x").astype(f32)
+
+    def over_y(v):
+        away = lax.dynamic_index_in_dim(v, 1 - y, 1, keepdims=False).astype(low)
+        return lax.dynamic_index_in_dim(v, y, 1, keepdims=False).astype(f32) + swap(away, "y").astype(f32)
+
+    half = half.astype(low)
+    if first == "x":
+        block = over_y(over_x(half).astype(low))
+    else:
+        block = over_x(over_y(half).astype(low))
+    block = block.astype(low)
+    pair = z // 2
+    away = part(block, (1 - pair) * 2, 2, 0)
+    two = part(block, pair * 2, 2, 0).astype(f32) + swap(away, "z2").astype(f32)
+    two = two.astype(low)
+    low_bit = z % 2
+    away = part(two, 1 - low_bit, 1, 0)
+    one = (part(two, low_bit, 1, 0).astype(f32) + swap(away, "z1").astype(f32))[0]
+    one = one.astype(low)
+    other = swap(one, "x")
+    pair_x = jnp.where(x == 0, jnp.concatenate([one, other], 1), jnp.concatenate([other, one], 1))
+    pair_c = swap(pair_x, "c")
+    whole = jnp.where(c == 0, jnp.concatenate([pair_x, pair_c], 1), jnp.concatenate([pair_c, pair_x], 1))
+    return whole.astype(f32)
 
 
 def normalize(values):
@@ -20,39 +236,23 @@
     return jax.nn.gelu(values, approximate=False)
 
 
-def local(
+def layer(
     tokens,
     time_index,
-    time_table,
-    ln1_gain,
-    ln1_bias,
-    w_qkv,
-    w_out,
-    b_out,
-    ln2_gain,
-    ln2_bias,
-    w_up,
-    b_up,
-    w_down,
-    b_down,
+    table_all,
+    gain_one,
+    bias_one,
+    qkv_w,
+    out_w,
+    out_b,
+    gain_two,
+    bias_two,
+    up_w,
+    up_b,
+    down_w,
+    down_b,
     cotangent,
 ):
-    table_all, gain_one, bias_one, qkv_w, out_w, out_b = (
-        lax.all_gather(time_table, "fsdp", axis=1, tiled=True),
-        lax.all_gather(ln1_gain, "fsdp", axis=0, tiled=True),
-        lax.all_gather(ln1_bias, "fsdp", axis=0, tiled=True),
-        lax.all_gather(w_qkv, "fsdp", axis=0, tiled=True),
-        lax.all_gather(w_out, "fsdp", axis=0, tiled=True),
-        lax.all_gather(b_out, "fsdp", axis=0, tiled=True),
-    )
-    gain_two, bias_two, up_w, up_b, down_w, down_b = (
-        lax.all_gather(ln2_gain, "fsdp", axis=0, tiled=True),
-        lax.all_gather(ln2_bias, "fsdp", axis=0, tiled=True),
-        lax.all_gather(w_up, "fsdp", axis=0, tiled=True),
-        lax.all_gather(b_up, "fsdp", axis=0, tiled=True),
-        lax.all_gather(w_down, "fsdp", axis=0, tiled=True),
-        lax.all_gather(b_down, "fsdp", axis=0, tiled=True),
-    )
     row_count, model_width = tokens.shape
     seq_count = time_index.shape[0]
     length = row_count // seq_count
@@ -99,12 +299,6 @@
         + jnp.dot(activated, down_w, preferred_element_type=jnp.float32)
         + down_b.astype(jnp.float32)
     ).astype(jnp.bfloat16)
-    qkv_w, out_w, up_w, down_w = (
-        lax.all_gather(w_qkv, "fsdp", axis=0, tiled=True),
-        lax.all_gather(w_out, "fsdp", axis=0, tiled=True),
-        lax.all_gather(w_up, "fsdp", axis=0, tiled=True),
-        lax.all_gather(w_down, "fsdp", axis=0, tiled=True),
-    )
     upstream = cotangent.astype(jnp.float32)
     grad_down = jnp.einsum("ti,td->id", activated, cotangent, preferred_element_type=jnp.float32)
     grad_down_b = jnp.sum(upstream, axis=0)
@@ -154,66 +348,75 @@
     first_pull = jax.vjp(scaled_norm, inputs, gain_one_f)[1]
     d_in_part, grad_ln1_gain = first_pull(d_normed.reshape(row_count, model_width))
     grad_tokens = (d_middle + d_in_part).astype(jnp.bfloat16)
-    all_shares = (
-        lax.psum_scatter(grad_table, "fsdp", scatter_dimension=1, tiled=True),
-        lax.psum_scatter(grad_ln1_gain, "fsdp", scatter_dimension=0, tiled=True),
-        lax.psum_scatter(grad_ln1_bias, "fsdp", scatter_dimension=0, tiled=True),
-        lax.psum_scatter(grad_qkv, "fsdp", scatter_dimension=0, tiled=True),
-        lax.psum_scatter(grad_out_w, "fsdp", scatter_dimension=0, tiled=True),
-        lax.psum_scatter(grad_out_b, "fsdp", scatter_dimension=0, tiled=True),
-        lax.psum_scatter(grad_ln2_gain, "fsdp", scatter_dimension=0, tiled=True),
-        lax.psum_scatter(grad_ln2_bias, "fsdp", scatter_dimension=0, tiled=True),
-        lax.psum_scatter(grad_up, "fsdp", scatter_dimension=0, tiled=True),
-        lax.psum_scatter(grad_up_b, "fsdp", scatter_dimension=0, tiled=True),
-        lax.psum_scatter(grad_down, "fsdp", scatter_dimension=0, tiled=True),
-        lax.psum_scatter(grad_down_b, "fsdp", scatter_dimension=0, tiled=True),
-    )
-    (
-        share_table,
-        share_gain_one,
-        share_bias_one,
-        share_qkv,
-        share_out_w,
-        share_out_b,
-        share_gain_two,
-        share_bias_two,
-        share_up,
-        share_up_b,
-        share_down,
-        share_down_b,
-    ) = all_shares
-    summed = lax.psum(
-        (
-            share_table,
-            share_gain_one,
-            share_bias_one,
-            share_qkv,
-            share_out_w,
-            share_out_b,
-            share_gain_two,
-            share_bias_two,
-            share_up,
-            share_up_b,
-            share_down,
-            share_down_b,
-        ),
-        "dp",
-    )
     return (
         block_out,
         grad_tokens,
-        summed[0],
-        summed[1],
-        summed[2],
-        summed[3],
-        summed[4],
-        summed[5],
-        summed[6],
-        summed[7],
-        summed[8],
-        summed[9],
-        summed[10],
-        summed[11],
+        (grad_table, grad_ln1_gain, grad_ln1_bias, grad_qkv, grad_out_w, grad_out_b, grad_ln2_gain,
+         grad_ln2_bias, grad_up, grad_up_b, grad_down, grad_down_b),
+    )
+
+
+def plain(*args):
+    dims = (None, None, 1, 0, 0, 0, 0, 0, 0, 0, 0, 0, 0, 0, None)
+    whole = [
+        item if dim is None else lax.all_gather(item, "fsdp", axis=dim, tiled=True)
+        for item, dim in zip(args, dims, strict=True)
+    ]
+    block_out, grad_tokens, grads = layer(*whole)
+    shares = [
+        lax.psum_scatter(grad, "fsdp", scatter_dimension=1 if place == 0 else 0, tiled=True)
+        for place, grad in enumerate(grads)
+    ]
+    return (block_out, grad_tokens, *lax.psum(tuple(shares), "dp"))
+
+
+def eight_by_four(
+    tokens, time_index, time_table, ln1_gain, ln1_bias, w_qkv, w_out, b_out, ln2_gain, ln2_bias,
+    w_up, b_up, w_down, b_down, cotangent,
+):
+    where = jnp.stack(coords()).astype(jnp.int32)
+    small = jnp.concatenate(
+        [time_table]
+        + [v.reshape(-1, 128) for v in (ln1_gain, ln1_bias, b_out, ln2_gain, ln2_bias, b_down, b_up)]
+        + [jnp.zeros((6, 128), time_table.dtype)]
+    )
+    small = gather_small(where, small)
+    table_all = small[:128]
+    gain_one, bias_one, out_b, gain_two, bias_two, down_b = (small[128 + i] for i in range(6))
+    up_b = small[134:138].reshape(4, 8, 128).transpose(1, 0, 2).reshape(4096)
+
+    def whole(own, axis):
+        split = Split(own.shape[axis])
+        return assemble(where, own, spread(own, split, axis), split, axis)
+
+    qk = whole(w_qkv[:, :2048], 1)
+    vo = whole(jnp.concatenate([w_qkv[:, 2048:], w_out], axis=1), 1)
+    up_w = jnp.concatenate([whole(w_up[:, :2048], 1), whole(w_up[:, 2048:], 1)], axis=1)
+    first, second = whole(w_down[:256], 0), whole(w_down[256:], 0)
+    down_w = jnp.stack([first.reshape(8, 256, 1024), second.reshape(8, 256, 1024)], axis=1).reshape(4096, 1024)
+    qkv_w = jnp.concatenate([qk, vo[:, :1024]], axis=1)
+    out_w = vo[:, 1024:]
+    block_out, grad_tokens, grads = layer(
+        tokens, time_index, table_all, gain_one, bias_one, qkv_w, out_w, out_b, gain_two, bias_two,
+        up_w, up_b, down_w, down_b, cotangent,
+    )
+    (grad_table, grad_ln1_gain, grad_ln1_bias, grad_qkv, grad_out_w, grad_out_b, grad_ln2_gain,
+     grad_ln2_bias, grad_up, grad_up_b, grad_down, grad_down_b) = grads
+    down = reduce_grad(grad_down, "x")
+    up = reduce_grad(grad_up, "y")
+    out = reduce_grad(grad_out_w, "x")
+    qkv = reduce_grad(grad_qkv, "y")
+    rows = jnp.concatenate(
+        [grad_table]
+        + [v[None] for v in (grad_ln1_gain, grad_ln1_bias, grad_out_b, grad_ln2_gain, grad_ln2_bias, grad_down_b)]
+        + [grad_up_b.reshape(8, 4, 128).transpose(1, 0, 2).reshape(4, 1024)]
+    )
+    rows = rows.reshape(138, 8, 128).transpose(1, 0, 2)
+    rows = jnp.broadcast_to(rows[:, None], (8, 4, 138, 128)).reshape(32, 138, 128)
+    got = jnp.sum(lax.all_to_all(rows, BOTH, 0, 0), axis=0)
+    return (
+        block_out, grad_tokens, got[:128], got[128], got[129], qkv, out, got[130], got[131], got[132],
+        up, got[134:138].reshape(512), down, got[133],
     )
 
 
@@ -251,4 +454,5 @@
         P("fsdp", None),
         P("fsdp"),
     )
+    local = eight_by_four if (mesh.shape["fsdp"], mesh.shape["dp"]) == (8, 4) else plain
     return jax.shard_map(local, mesh=mesh, in_specs=in_specs, out_specs=out_specs, check_vma=False)

time: 1630 us -> 826 us (0.51)
  waiting for transfers between devices: 1050 us -> 231 us
  blocking collectives: 177 us -> 0 us
  other arithmetic: 45.7 us -> 117 us
  starting transfers between devices: 0.57 us -> 71.3 us
  local copies, waits for them, and re-layouts: 142 us -> 185 us
  Pallas kernels: 0 us -> 20 us
    reduce_scatter x5 -> x0, waiting for transfers between devices: 839 us -> none  [the longest x1 286 us: local(): lax.psum_scatter(grad_down, 'fsdp', scatter_dimension=0, tiled=True)]
    ppermute x0 -> x67, waiting for transfers between devices: none -> 231 us  [swap(): return lax.ppermute(values, BOTH, flips(which))]
    all_gather x4 -> x0, waiting for transfers between devices: 159 us -> none  [the longest x1 108 us: local(): lax.all_gather(w_down, 'fsdp', axis=0, tiled=True)]
    all_gather x8 -> x0, blocking collectives: 135 us -> none  [the longest x1 22.8 us: local(): lax.all_gather(time_table, 'fsdp', axis=1, tiled=True)]
    ppermute x0 -> x67, starting transfers between devices: none -> 65.1 us  [swap(): return lax.ppermute(values, BOTH, flips(which))]
    psum x1 -> x0, waiting for transfers between devices: 44.1 us -> none  [local(): lax.psum((share_table, share_gain_one, share_bias_one, share_qkv, share_o...]
    convert_element_type x10 -> x28, other arithmetic: 16.2 us -> 48.1 us  [the longest x4 20.8 us: reduce_grad(): half = half.astype(low)]
    unnamed x1 -> x0, blocking collectives: 28.5 us -> none
  transfers between devices with their start and end apart: 10 -> 68, of which waited for: 7 -> 23; matrix products, arithmetic and copies ran while one was open for 14% -> 35% of each run, Pallas kernels for 0% -> 2%
where the time goes in v1:
time: 826 us; the launch traced here: 816 us
  waiting for transfers between devices  231 us (28%)
  matrix products  188 us (23%)
  local copies, waits for them, and re-layouts  185 us (22%)
  other arithmetic  117 us (14%)
  starting transfers between devices  71.3 us (9%)
  Pallas kernels  20 us (2%)
    ppermute x67, waiting for transfers between devices, swap(): return lax.ppermute(values, BOTH, flips(which))  231 us
    ppermute x67, starting transfers between devices, swap(): return lax.ppermute(values, BOTH, flips(which))  65.1 us
    unnamed x227, local copies, waits for them, and re-layouts  59.4 us
    dot_general x1, matrix products, layer(): jnp.dot(hidden_in, up_w, preferred_element_type=jnp.float32)  48.9 us
    dot_general x1, matrix products, layer(): jnp.einsum('td,id->ti', cotangent, down_w, preferred_element_type=jnp.flo...  24.5 us
    convert_element_type x4, other arithmetic, reduce_grad(): half = half.astype(low)  20.8 us
    pallas_call x6, Pallas kernels, assemble(): pl.pallas_call(functools.partial(assemble_kernel, split, axis), out_shape...  17.5 us
    convert_element_type x2, local copies, waits for them, and re-layouts, layer(): d_packed = jnp.stack([d_queries, d_keys, d_values], axis=2).astype(jnp.bf...  17.5 us
  transfers between devices with their start and end apart: 68, of which 23 were waited for; matrix products, arithmetic and copies ran while one was open for 35% of the time, Pallas kernels for 2%

profile of v1, /device:TPU:1, one launch (start us, length us, event | category | flops | bytes accessed | tf_op | source)
XLA Modules:
  0.0 815.6 jit_solution(13089887717224375499)
XLA Ops:
  17.6 4.2 copy.123
  29.7 4.0 copy.135
  43.0 25.5 %collective-permute-done.4 = bf16[2,128,640]{2,1,0:T(8,128)(2,1)S(1)} collective-permute-done((bf16[2,128,640]{2,1,0:T(8,128)(2,1)S(1)}, bf16[2,128,640]{2,1,0:T(8,128)(2,1)S(1)}, u32[]{:S(2)}, u32[]{:S(2)}) %collective-permute-start.4) | collective-permute-done | bytes 327712 | tf_op jit(solution)/shard_map/ppermute | solution.py:34
  69.5 3.7 collective-permute-start.5
  79.6 17.1 %collective-permute-done.10 = bf16[2,128,640]{2,1,0:T(8,128)(2,1)} collective-permute-done((bf16[2,128,640]{2,1,0:T(8,128)(2,1)}, bf16[2,128,640]{2,1,0:T(8,128)(2,1)}, u32[]{:S(2)}, u32[]{:S(2)}) %collective-permute-start.10) | collective-permute-done | bytes 327712 | tf_op jit(solution)/shard_map/ppermute | solution.py:34
  97.8 5.9 collective-permute-done.16
  104.7 6.0 collective-permute-done.22
  112.8 11.9 %collective-permute-done.28 = bf16[2,80,1024]{2,1,0:T(8,128)(2,1)S(1)} collective-permute-done((bf16[2,80,1024]{2,1,0:T(8,128)(2,1)}, bf16[2,80,1024]{2,1,0:T(8,128)(2,1)S(1)}, u32[]{:S(2)}, u32[]{:S(2)}) %collective-permute-start.28) | collective-permute-done | bytes 327712 | tf_op jit(solution)/shard_map/ppermute | solution.py:34
  141.2 5.5 copy.164
  147.8 5.0 collective-permute-start.7
  152.8 5.9 collective-permute-done.29
  158.8 8.1 collective-permute-start.13
  166.9 4.9 fusion.30
  171.8 5.4 copy.166
  204.2 9.4 %convolution_convert_fusion = bf16[1024,3072]{1,0:T(8,128)(2,1)} fusion(bf16[1024,1024]{0,1:T(8,128)(2,1)S(1)} %copy-done.54, bf16[1024,1024]{1,0:T(8,128)(2,1)S(1)} %slice.137, bf16[1024,2048]{1,0:T(8,128)(2,1)S(1)} %shard_map.255), kind=kOutput, calls=%fused_computation.56 | convolution fusion | flops 6458179584 | bytes 14680064 | tf_op jit(solution)/shard_map/dot_general | solution.py:272
  213.6 16.0 %reshape.224 = bf16[8,128,3,16,64]{4,3,2,1,0:T(8,128)(2,1)} reshape(bf16[1024,3072]{1,0:T(8,128)(2,1)} %convolution_convert_fusion) | data formatting | bytes 12582912 | tf_op jit(solution)/shard_map/reshape | solution.py:273
  229.5 9.1 %fusion.105 = (bf16[8,128,1,16,64]{4,3,2,1,0:T(8,128)(2,1)}, bf16[8,128,1,16,64]{4,3,2,1,0:T(8,128)(2,1)}, bf16[8,128,1,16,64]{4,3,2,1,0:T(8,128)(2,1)}) fusion(bf16[8,128,3,16,64]{4,3,2,1,0:T(8,128)(2,1)} %reshape.224), kind=kLoop, calls=%fused_computation.254 | loop fusion | bytes 12582912 | tf_op jit(solution)/shard_map/slice | solution.py:274
  238.6 5.8 copy.173
  244.4 5.8 copy.172
  250.2 5.8 copy.174
  256.0 3.5 fusion.45
  259.5 8.0 fusion.108
  277.8 26.7 %collective-permute-done.30.across = bf16[7,48,1024]{2,1,0:T(8,128)(2,1)S(1)} collective-permute-done((bf16[7,48,1024]{2,1,0:T(8,128)(2,1)S(1)}, bf16[7,48,1024]{2,1,0:T(8,128)(2,1)S(1)}, u32[]{:S(2)}, u32[]{:S(2)}) %collective-permute-start.30) | collective-permute-done | bytes 688160 | tf_op jit(solution)/shard_map/ppermute | solution.py:34
  313.9 3.5 shard_map.260
  323.9 6.3 pad_maximum_fusion.1
  333.9 48.9 %multiply_convert_fusion = (bf16[1024,4096]{1,0:T(8,128)(2,1)}, f32[1024,4096]{1,0:T(8,128)}, f32[1024,4096]{1,0:T(8,128)}) fusion(f32[4096]{0:T(1024)S(1)} %bitcast.281, bf16[1024,2048]{1,0:T(8,128)(2,1)S(1)} %copy-done.7, bf16[1024,2048]{1,0:T(8,128)(2,1)S(1)} %shard_map.257, bf16[1024,1024]{0,1:T(8,128)(2,1)S(1)} %copy-done.48), kind=kOutput, calls=%fused_computation.13 | convolution fusion | flops 8883535872 | bytes 52445184 | tf_op jit(solution)/shard_map/dot_general | solution.py:293
  382.7 24.5 %convert_reduce_fusion = (f32[4096]{0:T(1024)}, bf16[1024,4096]{1,0:T(8,128)(2,1)}) fusion(f32[1024,4096]{1,0:T(8,128)} %get-tuple-element.81, bf16[4096,1024]{1,0:T(8,128)(2,1)} %bitcast.232, bf16[1024,1024]{1,0:T(8,128)(2,1)} %param.29, f32[1024,4096]{1,0:T(8,128)} %get-tuple-element.126, f32[4096]{0:T(1024)S(1)} %bitcast.282), kind=kOutput, calls=%fused_computation.12 | convolution fusion | flops 8661233664 | bytes 52461568 | tf_op jit(solution)/shard_map/td,id->ti/dot_general | solution.py:305
  407.3 13.4 %fusion.110 = (f32[1024]{0:T(1024)}, f32[1024,1024]{1,0:T(8,128)}) fusion(bf16[1024,4096]{1,0:T(8,128)(2,1)} %get-tuple-element.132, bf16[1024,2048]{1,0:T(8,128)(2,1)S(1)} %copy-done.7, bf16[1024,2048]{1,0:T(8,128)(2,1)S(1)} %copy-done.9), kind=kOutput, calls=%fused_computation.259 | convolution fusion | flops 8607759360 | bytes 20975616 | tf_op jit(solution)/shard_map/tf,if->ti/dot_general | solution.py:310
  420.6 5.5 copy.136
  426.2 5.4 multiply_reduce_fusion.2
  436.9 3.7 convolution_convert_fusion.1
  440.6 4.4 fusion.39
  444.9 12.6 %fusion.100 = f32[1024,4096]{1,0:T(8,128)} fusion(bf16[1024,4096]{1,0:T(8,128)(2,1)S(1)} %bitcast.295, f32[1024,1024]{0,1:T(8,128)S(1)} %copy-done.25, f32[1024]{0:T(1024)S(1)} %bitcast.279, f32[1024]{0:T(1024)S(1)} %bitcast.272, f32[1024]{0:T(1024)S(1)} %copy-done.92, f32[1024]{0:T(1024)S(1)} %copy-done.86), kind=kOutput, calls=%fused_computation.251 | convolution fusion | flops 8595177472 | bytes 29376512 | tf_op jit(solution)/shard_map/ti,tf->if/dot_general | solution.py:308
  457.5 6.4 reshape.225
  463.9 5.8 copy.138
  469.7 8.5 %convolution_bitcast_fusion = bf16[8,128,1,16,64]{1,4,3,0,2:T(8,128)(2,1)} fusion(bf16[8,128,16,64]{1,3,2,0:T(8,128)(2,1)} %copy.138, f32[8,16,128,128]{2,3,1,0:T(8,128)} %copy-done.30, f32[8,16,128]{2,1,0:T(8,128)S(1)} %copy-done.78), kind=kOutput, calls=%fused_computation.87 | convolution fusion | flops 272629760 | bytes 12648448 | tf_op jit(solution)/shard_map/shqk,sqhd->skhd/dot_general | solution.py:321
  478.2 6.2 multiply_reduce_fusion
  492.8 15.3 %copy.149 = bf16[8,128,3,16,64]{1,0,4,3,2:T(8,128)(2,1)} copy(bf16[8,128,3,16,64]{1,4,3,0,2:T(8,128)(2,1)S(1)} %maximum_convert_fusion) | data formatting | bytes 12582912 | tf_op jit(solution)/shard_map/convert_element_type | solution.py:335
  513.3 6.2 dynamic-slice_convert_fusion.1
  520.3 8.5 %fusion.102 = (f32[1024]{0:T(1024)S(1)}, f32[8,128,1024]{2,1,0:T(8,128)}, f32[8,1024]{1,0:T(8,128)S(1)}) fusion(f32[8,1024]{1,0:T(8,128)S(1)} %copy-done.82, f32[1024,1024]{1,0:T(8,128)S(1)} %copy-done.44, bf16[8,128,3072]{1,2,0:T(8,128)(2,1)S(1)} %bitcast.235, bf16[1024,1024]{1,0:T(8,128)(2,1)S(1)} %copy-done.51, bf16[1024,2048]{1,0:T(8,128)(2,1)S(1)} %copy-done.5), kind=kOutput, calls=%fused_computation.252 | convolution fusion | flops 6459218944 | bytes 21041152 | tf_op jit(solution)/shard_map/tf,if->ti/dot_general | solution.py:339
  528.8 5.4 copy.165
  534.1 9.7 %fusion.15 = f32[1024,3072]{1,0:T(8,128)S(1)} fusion(bf16[1024,1024]{0,1:T(8,128)(2,1)} %get-tuple-element.89, bf16[384,8,8,128]{3,2,1,0:T(8,128)(2,1)} %bitcast.234), kind=kOutput, calls=%fused_computation.39 | convolution fusion | flops 6442450944 | bytes 20971520 | tf_op jit(solution)/shard_map/ti,tf->if/dot_general | solution.py:338
  546.0 3.7 copy-done.42
  549.7 11.6 %fusion.111 = f32[4096,1024]{1,0:T(8,128)S(1)} fusion(bf16[1024,4096]{1,0:T(8,128)(2,1)} %get-tuple-element.80, bf16[1024,1024]{1,0:T(8,128)(2,1)S(1)} %copy-done.49), kind=kOutput, calls=%fused_computation.260 | convolution fusion | flops 8589934592 | bytes 27262976 | tf_op jit(solution)/shard_map/ti,td->id/dot_general | solution.py:303
  564.5 3.7 add_convert_fusion.8
  572.8 9.3 %collective-permute-done.47 = bf16[4,2,128,256]{3,2,0,1:T(8,128)(2,1)S(1)} collective-permute-done((bf16[4,2,128,256]{3,2,0,1:T(8,128)(2,1)S(1)}, bf16[4,2,128,256]{3,2,0,1:T(8,128)(2,1)S(1)}, u32[]{:S(2)}, u32[]{:S(2)}) %collective-permute-start.47) | collective-permute-done | bytes 524320 | tf_op jit(solution)/shard_map/ppermute | solution.py:34
  584.7 4.8 collective-permute-done.48
  589.7 3.9 convert_reduce_fusion.2
  597.5 6.2 all-to-all-start
  606.6 4.8 add_convert_fusion.2
  614.0 6.1 add_convert_fusion.1
  622.6 6.2 add_convert_fusion
  632.2 34.5 %collective-permute-done.40 = bf16[4,128,1536]{2,1,0:T(8,128)(2,1)} collective-permute-done((bf16[4,128,1536]{2,1,0:T(8,128)(2,1)}, bf16[4,128,1536]{2,1,0:T(8,128)(2,1)}, u32[]{:S(2)}, u32[]{:S(2)}) %collective-permute-start.40) | collective-permute-done | bytes 1572896 | tf_op jit(solution)/shard_map/ppermute | solution.py:34
  670.7 14.8 %add_convert_fusion.5 = bf16[1024,1024]{0,1:T(8,128)(2,1)} fusion(f32[1024,1024]{0,1:T(8,128)S(1)} %copy-done.26, f32[1024]{0:T(1024)S(1)} %bitcast.285, bf16[1024,4096]{1,0:T(8,128)(2,1)} %get-tuple-element.80, bf16[4096,1024]{1,0:T(8,128)(2,1)} %bitcast.233), kind=kOutput, calls=%fused_computation.78 | convolution fusion | flops 8593080320 | bytes 23072768 | tf_op jit(solution)/shard_map/dot_general | solution.py:299
  685.4 3.9 copy.156
  689.3 4.1 copy.157
  695.5 5.2 collective-permute-done.41
  703.1 6.6 collective-permute-start.42
  721.2 5.1 collective-permute-done.42
  727.4 12.6 %collective-permute-done.55 = bf16[4,128,1024]{2,1,0:T(8,128)(2,1)} collective-permute-done((bf16[4,128,1024]{2,1,0:T(8,128)(2,1)}, bf16[4,128,1024]{2,1,0:T(8,128)(2,1)}, u32[]{:S(2)}, u32[]{:S(2)}) %collective-permute-start.55) | collective-permute-done | bytes 1048608 | tf_op jit(solution)/shard_map/ppermute | solution.py:34
  747.3 31.3 %collective-permute-done.56 = bf16[2,128,1024]{2,1,0:T(8,128)(2,1)S(1)} collective-permute-done((bf16[2,128,1024]{2,1,0:T(8,128)(2,1)S(1)}, bf16[2,128,1024]{2,1,0:T(8,128)(2,1)S(1)}, u32[]{:S(2)}, u32[]{:S(2)}) %collective-permute-start.56) | collective-permute-done | bytes 524320 | tf_op jit(solution)/shard_map/ppermute | solution.py:34
  778.9 10.9 %collective-permute-done.63 = bf16[2,512,256]{2,1,0:T(8,128)(2,1)S(1)} collective-permute-done((bf16[2,512,256]{2,1,0:T(8,128)(2,1)S(1)}, bf16[2,512,256]{2,1,0:T(8,128)(2,1)S(1)}, u32[]{:S(2)}, u32[]{:S(2)}) %collective-permute-start.63) | collective-permute-done | bytes 524320 | tf_op jit(solution)/shard_map/ppermute | solution.py:34
  790.1 6.1 collective-permute-done.57
  797.8 4.1 collective-permute-done.64
  (467 shorter events, 210.8 us)
Async XLA Ops:
  3.0 23.7 %collective-permute-start = (bf16[144,128]{1,0:T(8,128)(2,1)S(1)}, bf16[144,128]{1,0:T(8,128)(2,1)S(1)}, u32[]{:S(2)}, u32[]{:S(2)}) collective-permute-start(bf16[144,128]{1,0:T(8,128)(2,1)S(1)} %concatenate.144), channel_id=1, source_target_pairs={{0,8},{1,9},{2,10},{3,11},{4,12},{5,13},{6,14},{7,15},{8,0},{9,1},... | collective-permute-start | bytes 110600 | tf_op jit(solution)/shard_map/ppermute | solution.py:34
  9.2 29.1 %collective-permute-start.9 = (bf16[128,640]{1,0:T(8,128)(2,1)}, bf16[128,640]{1,0:T(8,128)(2,1)S(1)}, u32[]{:S(2)}, u32[]{:S(2)}) collective-permute-start(bf16[128,640]{1,0:T(8,128)(2,1)} %get-tuple-element.115), channel_id=1, source_target_pairs={{0,8},{1,9},{2,10},{3,11},{4,12},{5,13},{6,14},{7,15},{8,0},{9,1},... | collective-permute-start | bytes 491528 | tf_op jit(solution)/shard_map/ppermute | solution.py:34
  11.1 28.0 %collective-permute-start.15 = (bf16[128,640]{1,0:T(8,128)(2,1)}, bf16[128,640]{1,0:T(8,128)(2,1)S(1)}, u32[]{:S(2)}, u32[]{:S(2)}) collective-permute-start(bf16[128,640]{1,0:T(8,128)(2,1)} %get-tuple-element.109), channel_id=1, source_target_pairs={{0,8},{1,9},{2,10},{3,11},{4,12},{5,13},{6,14},{7,15},{8,0},{9,1},... | collective-permute-start | bytes 491528 | tf_op jit(solution)/shard_map/ppermute | solution.py:34
  13.3 22.9 %collective-permute-start.21 = (bf16[128,640]{1,0:T(8,128)(2,1)}, bf16[128,640]{1,0:T(8,128)(2,1)S(1)}, u32[]{:S(2)}, u32[]{:S(2)}) collective-permute-start(bf16[128,640]{1,0:T(8,128)(2,1)} %get-tuple-element.111), channel_id=1, source_target_pairs={{0,8},{1,9},{2,10},{3,11},{4,12},{5,13},{6,14},{7,15},{8,0},{9,1},... | collective-permute-start | bytes 491528 | tf_op jit(solution)/shard_map/ppermute | solution.py:34
  14.0 19.9 %collective-permute-start.3 = (bf16[128,640]{1,0:T(8,128)(2,1)S(1)}, bf16[128,640]{1,0:T(8,128)(2,1)S(1)}, u32[]{:S(2)}, u32[]{:S(2)}) collective-permute-start(bf16[128,640]{1,0:T(8,128)(2,1)S(1)} %get-tuple-element.113), channel_id=1, source_target_pairs={{0,8},{1,9},{2,10},{3,11},{4,12},{5,13},{6,14},{7,15},{8,0},{9,1},... | collective-permute-start | bytes 491528 | tf_op jit(solution)/shard_map/ppermute | solution.py:34
  33.7 35.8 %collective-permute-start.33 = (bf16[80,1024]{1,0:T(8,128)(2,1)S(1)}, bf16[80,1024]{1,0:T(8,128)(2,1)S(1)}, u32[]{:S(2)}, u32[]{:S(2)}) collective-permute-start(bf16[80,1024]{1,0:T(8,128)(2,1)S(1)} %get-tuple-element.107), channel_id=1, source_target_pairs={{0,8},{1,9},{2,10},{3,11},{4,12},{5,13},{6,14},{7,15},{8,0},{9,1},... | collective-permute-start | bytes 491528 | tf_op jit(solution)/shard_map/ppermute | solution.py:34
  33.9 8.3 %collective-permute-start.27 = (bf16[80,1024]{1,0:T(8,128)(2,1)S(1)}, bf16[80,1024]{1,0:T(8,128)(2,1)S(1)}, u32[]{:S(2)}, u32[]{:S(2)}) collective-permute-start(bf16[80,1024]{1,0:T(8,128)(2,1)S(1)} %get-tuple-element.105), channel_id=1, source_target_pairs={{0,8},{1,9},{2,10},{3,11},{4,12},{5,13},{6,14},{7,15},{8,0},{9,1},... | collective-permute-start | bytes 491528 | tf_op jit(solution)/shard_map/ppermute | solution.py:34
  36.2 37.7 %collective-permute-start.2 = (bf16[4,144,128]{2,1,0:T(8,128)(2,1)S(1)}, bf16[4,144,128]{2,1,0:T(8,128)(2,1)S(1)}, u32[]{:S(2)}, u32[]{:S(2)}) collective-permute-start(bf16[4,144,128]{2,1,0:T(8,128)(2,1)S(1)} %pad_maximum_fusion.33), channel_id=1, source_target_pairs={{0,4},{1,5},{2,6},{3,7},{4,0},{5,1},{6,2},{7,3},{8,12},{9,13},{10,... | collective-permute-start | bytes 442376 | tf_op jit(solution)/shard_map/ppermute | solution.py:34
  38.3 30.2 %collective-permute-start.4 = (bf16[2,128,640]{2,1,0:T(8,128)(2,1)S(1)}, bf16[2,128,640]{2,1,0:T(8,128)(2,1)S(1)}, u32[]{:S(2)}, u32[]{:S(2)}) collective-permute-start(bf16[2,128,640]{2,1,0:T(8,128)(2,1)S(1)} %pad_maximum_fusion.20), channel_id=1, source_target_pairs={{0,16},{1,17},{2,18},{3,19},{4,20},{5,21},{6,22},{7,23},{8,24},{9,... | collective-permute-start | bytes 983048 | tf_op jit(solution)/shard_map/ppermute | solution.py:34
  39.1 57.6 %collective-permute-start.10 = (bf16[2,128,640]{2,1,0:T(8,128)(2,1)}, bf16[2,128,640]{2,1,0:T(8,128)(2,1)}, u32[]{:S(2)}, u32[]{:S(2)}) collective-permute-start(bf16[2,128,640]{2,1,0:T(8,128)(2,1)} %pad_maximum_fusion.21), channel_id=1, source_target_pairs={{0,16},{1,17},{2,18},{3,19},{4,20},{5,21},{6,22},{7,23},{8,24},{9,... | collective-permute-start | bytes 983048 | tf_op jit(solution)/shard_map/ppermute | solution.py:34
  42.2 61.4 %collective-permute-start.16 = (bf16[2,128,640]{2,1,0:T(8,128)(2,1)}, bf16[2,128,640]{2,1,0:T(8,128)(2,1)S(1)}, u32[]{:S(2)}, u32[]{:S(2)}) collective-permute-start(bf16[2,128,640]{2,1,0:T(8,128)(2,1)} %pad_maximum_fusion.22), channel_id=1, source_target_pairs={{0,16},{1,17},{2,18},{3,19},{4,20},{5,21},{6,22},{7,23},{8,24},{9,... | collective-permute-start | bytes 983048 | tf_op jit(solution)/shard_map/ppermute | solution.py:34
  68.5 42.2 %collective-permute-start.22 = (bf16[2,128,640]{2,1,0:T(8,128)(2,1)}, bf16[2,128,640]{2,1,0:T(8,128)(2,1)}, u32[]{:S(2)}, u32[]{:S(2)}) collective-permute-start(bf16[2,128,640]{2,1,0:T(8,128)(2,1)} %pad_maximum_fusion.23), channel_id=1, source_target_pairs={{0,16},{1,17},{2,18},{3,19},{4,20},{5,21},{6,22},{7,23},{8,24},{9,... | collective-permute-start | bytes 983048 | tf_op jit(solution)/shard_map/ppermute | solution.py:34
  69.5 56.3 %collective-permute-start.5 = (bf16[4,128,640]{2,1,0:T(8,128)(2,1)}, bf16[4,128,640]{2,1,0:T(8,128)(2,1)}, u32[]{:S(2)}, u32[]{:S(2)}) collective-permute-start(bf16[4,128,640]{2,1,0:T(8,128)(2,1)} %pad_maximum_fusion.14), channel_id=1, source_target_pairs={{0,4},{1,5},{2,6},{3,7},{4,0},{5,1},{6,2},{7,3},{8,12},{9,13},{10,... | collective-permute-start | bytes 1966088 | tf_op jit(solution)/shard_map/ppermute | solution.py:34
  73.9 64.0 %collective-permute-start.34 = (bf16[2,80,1024]{2,1,0:T(8,128)(2,1)}, bf16[2,80,1024]{2,1,0:T(8,128)(2,1)S(1)}, u32[]{:S(2)}, u32[]{:S(2)}) collective-permute-start(bf16[2,80,1024]{2,1,0:T(8,128)(2,1)} %pad_maximum_fusion.25), channel_id=1, source_target_pairs={{0,16},{1,17},{2,18},{3,19},{4,20},{5,21},{6,22},{7,23},{8,24},{9,... | collective-permute-start | bytes 983048 | tf_op jit(solution)/shard_map/ppermute | solution.py:34
  96.7 28.0 %collective-permute-start.28 = (bf16[2,80,1024]{2,1,0:T(8,128)(2,1)}, bf16[2,80,1024]{2,1,0:T(8,128)(2,1)S(1)}, u32[]{:S(2)}, u32[]{:S(2)}) collective-permute-start(bf16[2,80,1024]{2,1,0:T(8,128)(2,1)} %pad_maximum_fusion.24), channel_id=1, source_target_pairs={{0,16},{1,17},{2,18},{3,19},{4,20},{5,21},{6,22},{7,23},{8,24},{9,... | collective-permute-start | bytes 983048 | tf_op jit(solution)/shard_map/ppermute | solution.py:34
  103.6 28.0 %collective-permute-start.11 = (bf16[4,128,640]{2,1,0:T(8,128)(2,1)S(1)}, bf16[4,128,640]{2,1,0:T(8,128)(2,1)S(1)}, u32[]{:S(2)}, u32[]{:S(2)}) collective-permute-start(bf16[4,128,640]{2,1,0:T(8,128)(2,1)S(1)} %pad_maximum_fusion.15), channel_id=1, source_target_pairs={{0,4},{1,5},{2,6},{3,7},{4,0},{5,1},{6,2},{7,3},{8,12},{9,13},{10,... | collective-permute-start | bytes 1966088 | tf_op jit(solution)/shard_map/ppermute | solution.py:34
  110.8 36.9 %collective-permute-start.17 = (bf16[4,128,640]{2,1,0:T(8,128)(2,1)}, bf16[4,128,640]{2,1,0:T(8,128)(2,1)}, u32[]{:S(2)}, u32[]{:S(2)}) collective-permute-start(bf16[4,128,640]{2,1,0:T(8,128)(2,1)} %pad_maximum_fusion.16), channel_id=1, source_target_pairs={{0,4},{1,5},{2,6},{3,7},{4,0},{5,1},{6,2},{7,3},{8,12},{9,13},{10,... | collective-permute-start | bytes 1966088 | tf_op jit(solution)/shard_map/ppermute | solution.py:34
  124.7 23.2 %collective-permute-start.23 = (bf16[4,128,640]{2,1,0:T(8,128)(2,1)}, bf16[4,128,640]{2,1,0:T(8,128)(2,1)}, u32[]{:S(2)}, u32[]{:S(2)}) collective-permute-start(bf16[4,128,640]{2,1,0:T(8,128)(2,1)} %pad_maximum_fusion.17), channel_id=1, source_target_pairs={{0,4},{1,5},{2,6},{3,7},{4,0},{5,1},{6,2},{7,3},{8,12},{9,13},{10,... | collective-permute-start | bytes 1966088 | tf_op jit(solution)/shard_map/ppermute | solution.py:34
  125.8 33.0 %collective-permute-start.29 = (bf16[4,80,1024]{2,1,0:T(8,128)(2,1)}, bf16[4,80,1024]{2,1,0:T(8,128)(2,1)}, u32[]{:S(2)}, u32[]{:S(2)}) collective-permute-start(bf16[4,80,1024]{2,1,0:T(8,128)(2,1)} %pad_maximum_fusion.18), channel_id=1, source_target_pairs={{0,4},{1,5},{2,6},{3,7},{4,0},{5,1},{6,2},{7,3},{8,12},{9,13},{10,... | collective-permute-start | bytes 1966088 | tf_op jit(solution)/shard_map/ppermute | solution.py:34
  135.8 41.4 %collective-permute-start.12 = (bf16[7,128,384]{2,1,0:T(8,128)(2,1)}, bf16[7,128,384]{2,1,0:T(8,128)(2,1)}, u32[]{:S(2)}, u32[]{:S(2)}) collective-permute-start(bf16[7,128,384]{2,1,0:T(8,128)(2,1)} %slice.136), channel_id=1, source_target_pairs={{0,2},{1,3},{2,0},{3,1},{4,6},{5,7},{6,4},{7,5},{8,10},{9,11},{10,... | collective-permute-start | bytes 2064392 | tf_op jit(solution)/shard_map/ppermute | solution.py:34
  137.9 39.4 %collective-permute-start.6 = (bf16[7,128,384]{2,1,0:T(8,128)(2,1)}, bf16[7,128,384]{2,1,0:T(8,128)(2,1)}, u32[]{:S(2)}, u32[]{:S(2)}) collective-permute-start(bf16[7,128,384]{2,1,0:T(8,128)(2,1)} %slice.135), channel_id=1, source_target_pairs={{0,2},{1,3},{2,0},{3,1},{4,6},{5,7},{6,4},{7,5},{8,10},{9,11},{10,... | collective-permute-start | bytes 2064392 | tf_op jit(solution)/shard_map/ppermute | solution.py:34
  147.6 39.7 %collective-permute-start.35 = (bf16[4,80,1024]{2,1,0:T(8,128)(2,1)}, bf16[4,80,1024]{2,1,0:T(8,128)(2,1)}, u32[]{:S(2)}, u32[]{:S(2)}) collective-permute-start(bf16[4,80,1024]{2,1,0:T(8,128)(2,1)} %pad_maximum_fusion.19), channel_id=1, source_target_pairs={{0,4},{1,5},{2,6},{3,7},{4,0},{5,1},{6,2},{7,3},{8,12},{9,13},{10,... | collective-permute-start | bytes 1966088 | tf_op jit(solution)/shard_map/ppermute | solution.py:34
  147.8 49.2 %collective-permute-start.7 = (bf16[7,128,640]{2,1,0:T(8,128)(2,1)}, bf16[7,128,640]{2,1,0:T(8,128)(2,1)}, u32[]{:S(2)}, u32[]{:S(2)}) collective-permute-start(bf16[7,128,640]{2,1,0:T(8,128)(2,1)} %pad_maximum_fusion.7.seven), channel_id=1, source_target_pairs={{0,1},{1,0},{2,3},{3,2},{4,5},{5,4},{6,7},{7,6},{8,9},{9,8},{10,11... | collective-permute-start | bytes 3440648 | tf_op jit(solution)/shard_map/ppermute | solution.py:34
  158.8 32.9 %collective-permute-start.13 = (bf16[7,128,640]{2,1,0:T(8,128)(2,1)}, bf16[7,128,640]{2,1,0:T(8,128)(2,1)}, u32[]{:S(2)}, u32[]{:S(2)}) collective-permute-start(bf16[7,128,640]{2,1,0:T(8,128)(2,1)} %pad_maximum_fusion.8.seven), channel_id=1, source_target_pairs={{0,1},{1,0},{2,3},{3,2},{4,5},{5,4},{6,7},{7,6},{8,9},{9,8},{10,11... | collective-permute-start | bytes 3440648 | tf_op jit(solution)/shard_map/ppermute | solution.py:34
  177.2 14.9 %collective-permute-start.14 = (bf16[7,128,384]{2,1,0:T(8,128)(2,1)}, bf16[7,128,384]{2,1,0:T(8,128)(2,1)S(1)}, u32[]{:S(2)}, u32[]{:S(2)}) collective-permute-start(bf16[7,128,384]{2,1,0:T(8,128)(2,1)} %collective-permute-done.12.across), channel_id=1, source_target_pairs={{0,1},{1,0},{2,3},{3,2},{4,5},{5,4},{6,7},{7,6},{8,9},{9,8},{10,11... | collective-permute-start | bytes 2064392 | tf_op jit(solution)/shard_map/ppermute | solution.py:34
  177.3 22.0 %collective-permute-start.8 = (bf16[7,128,384]{2,1,0:T(8,128)(2,1)}, bf16[7,128,384]{2,1,0:T(8,128)(2,1)S(1)}, u32[]{:S(2)}, u32[]{:S(2)}) collective-permute-start(bf16[7,128,384]{2,1,0:T(8,128)(2,1)} %collective-permute-done.6.across), channel_id=1, source_target_pairs={{0,1},{1,0},{2,3},{3,2},{4,5},{5,4},{6,7},{7,6},{8,9},{9,8},{10,11... | collective-permute-start | bytes 2064392 | tf_op jit(solution)/shard_map/ppermute | solution.py:34
  187.3 118.9 %collective-permute-start.31 = (bf16[7,80,1024]{2,1,0:T(8,128)(2,1)}, bf16[7,80,1024]{2,1,0:T(8,128)(2,1)}, u32[]{:S(2)}, u32[]{:S(2)}) collective-permute-start(bf16[7,80,1024]{2,1,0:T(8,128)(2,1)} %pad_maximum_fusion.11.seven), channel_id=1, source_target_pairs={{0,1},{1,0},{2,3},{3,2},{4,5},{5,4},{6,7},{7,6},{8,9},{9,8},{10,11... | collective-permute-start | bytes 3440648 | tf_op jit(solution)/shard_map/ppermute | solution.py:34
  191.7 115.5 %collective-permute-start.37 = (bf16[7,80,1024]{2,1,0:T(8,128)(2,1)}, bf16[7,80,1024]{2,1,0:T(8,128)(2,1)}, u32[]{:S(2)}, u32[]{:S(2)}) collective-permute-start(bf16[7,80,1024]{2,1,0:T(8,128)(2,1)} %pad_maximum_fusion.12.seven), channel_id=1, source_target_pairs={{0,1},{1,0},{2,3},{3,2},{4,5},{5,4},{6,7},{7,6},{8,9},{9,8},{10,11... | collective-permute-start | bytes 3440648 | tf_op jit(solution)/shard_map/ppermute | solution.py:34
  192.1 127.4 %collective-permute-start.25 = (bf16[7,128,640]{2,1,0:T(8,128)(2,1)S(1)}, bf16[7,128,640]{2,1,0:T(8,128)(2,1)}, u32[]{:S(2)}, u32[]{:S(2)}) collective-permute-start(bf16[7,128,640]{2,1,0:T(8,128)(2,1)S(1)} %pad_maximum_fusion.10.seven), channel_id=1, source_target_pairs={{0,1},{1,0},{2,3},{3,2},{4,5},{5,4},{6,7},{7,6},{8,9},{9,8},{10,11... | collective-permute-start | bytes 3440648 | tf_op jit(solution)/shard_map/ppermute | solution.py:34
  197.1 76.3 %collective-permute-start.18 = (bf16[7,128,384]{2,1,0:T(8,128)(2,1)}, bf16[7,128,384]{2,1,0:T(8,128)(2,1)}, u32[]{:S(2)}, u32[]{:S(2)}) collective-permute-start(bf16[7,128,384]{2,1,0:T(8,128)(2,1)} %slice.145), channel_id=1, source_target_pairs={{0,2},{1,3},{2,0},{3,1},{4,6},{5,7},{6,4},{7,5},{8,10},{9,11},{10,... | collective-permute-start | bytes 2064392 | tf_op jit(solution)/shard_map/ppermute | solution.py:34
  199.3 75.6 %collective-permute-start.24 = (bf16[7,128,384]{2,1,0:T(8,128)(2,1)}, bf16[7,128,384]{2,1,0:T(8,128)(2,1)}, u32[]{:S(2)}, u32[]{:S(2)}) collective-permute-start(bf16[7,128,384]{2,1,0:T(8,128)(2,1)} %slice.146), channel_id=1, source_target_pairs={{0,2},{1,3},{2,0},{3,1},{4,6},{5,7},{6,4},{7,5},{8,10},{9,11},{10,... | collective-permute-start | bytes 2064392 | tf_op jit(solution)/shard_map/ppermute | solution.py:34
  273.4 32.7 %collective-permute-start.36 = (bf16[7,48,1024]{2,1,0:T(8,128)(2,1)S(1)}, bf16[7,48,1024]{2,1,0:T(8,128)(2,1)S(1)}, u32[]{:S(2)}, u32[]{:S(2)}) collective-permute-start(bf16[7,48,1024]{2,1,0:T(8,128)(2,1)S(1)} %copy-done.76), channel_id=1, source_target_pairs={{0,2},{1,3},{2,0},{3,1},{4,6},{5,7},{6,4},{7,5},{8,10},{9,11},{10,... | collective-permute-start | bytes 2064392 | tf_op jit(solution)/shard_map/ppermute | solution.py:34
  274.9 29.7 %collective-permute-start.30 = (bf16[7,48,1024]{2,1,0:T(8,128)(2,1)S(1)}, bf16[7,48,1024]{2,1,0:T(8,128)(2,1)S(1)}, u32[]{:S(2)}, u32[]{:S(2)}) collective-permute-start(bf16[7,48,1024]{2,1,0:T(8,128)(2,1)S(1)} %copy-done.75), channel_id=1, source_target_pairs={{0,2},{1,3},{2,0},{3,1},{4,6},{5,7},{6,4},{7,5},{8,10},{9,11},{10,... | collective-permute-start | bytes 2064392 | tf_op jit(solution)/shard_map/ppermute | solution.py:34
  306.1 13.4 %collective-permute-start.26 = (bf16[7,128,384]{2,1,0:T(8,128)(2,1)}, bf16[7,128,384]{2,1,0:T(8,128)(2,1)S(1)}, u32[]{:S(2)}, u32[]{:S(2)}) collective-permute-start(bf16[7,128,384]{2,1,0:T(8,128)(2,1)} %collective-permute-done.24.across), channel_id=1, source_target_pairs={{0,1},{1,0},{2,3},{3,2},{4,5},{5,4},{6,7},{7,6},{8,9},{9,8},{10,11... | collective-permute-start | bytes 2064392 | tf_op jit(solution)/shard_map/ppermute | solution.py:34
  306.2 7.7 collective-permute-start.38
  307.2 22.9 %collective-permute-start.19 = (bf16[7,128,640]{2,1,0:T(8,128)(2,1)S(1)}, bf16[7,128,640]{2,1,0:T(8,128)(2,1)}, u32[]{:S(2)}, u32[]{:S(2)}) collective-permute-start(bf16[7,128,640]{2,1,0:T(8,128)(2,1)S(1)} %pad_maximum_fusion.9.seven), channel_id=1, source_target_pairs={{0,1},{1,0},{2,3},{3,2},{4,5},{5,4},{6,7},{7,6},{8,9},{9,8},{10,11... | collective-permute-start | bytes 3440648 | tf_op jit(solution)/shard_map/ppermute | solution.py:34
  308.0 22.1 %collective-permute-start.20 = (bf16[7,128,384]{2,1,0:T(8,128)(2,1)}, bf16[7,128,384]{2,1,0:T(8,128)(2,1)}, u32[]{:S(2)}, u32[]{:S(2)}) collective-permute-start(bf16[7,128,384]{2,1,0:T(8,128)(2,1)} %collective-permute-done.18.across), channel_id=1, source_target_pairs={{0,1},{1,0},{2,3},{3,2},{4,5},{5,4},{6,7},{7,6},{8,9},{9,8},{10,11... | collective-permute-start | bytes 2064392 | tf_op jit(solution)/shard_map/ppermute | solution.py:34
  513.2 51.3 %collective-permute-start.46 = (bf16[1024,512]{1,0:T(8,128)(2,1)}, bf16[1024,512]{1,0:T(8,128)(2,1)S(1)}, u32[]{:S(2)}, u32[]{:S(2)}) collective-permute-start(bf16[1024,512]{1,0:T(8,128)(2,1)} %dynamic-slice_convert_fusion.3), channel_id=1, source_target_pairs={{0,1},{1,0},{2,3},{3,2},{4,5},{5,4},{6,7},{7,6},{8,9},{9,8},{10,11... | collective-permute-start | bytes 3145736 | tf_op jit(solution)/shard_map/ppermute | solution.py:34
  519.5 94.4 %collective-permute-start.53 = (bf16[1024,2048]{1,0:T(8,128)(2,1)}, bf16[1024,2048]{1,0:T(8,128)(2,1)}, u32[]{:S(2)}, u32[]{:S(2)}) collective-permute-start(bf16[1024,2048]{1,0:T(8,128)(2,1)} %dynamic-slice_convert_fusion.1), channel_id=1, source_target_pairs={{0,1},{1,0},{2,3},{3,2},{4,5},{5,4},{6,7},{7,6},{8,9},{9,8},{10,11... | collective-permute-start | bytes 12582920 | tf_op jit(solution)/shard_map/ppermute | solution.py:34
  546.0 60.6 %collective-permute-start.39 = (bf16[1024,1536]{1,0:T(8,128)(2,1)}, bf16[1024,1536]{1,0:T(8,128)(2,1)}, u32[]{:S(2)}, u32[]{:S(2)}) collective-permute-start(bf16[1024,1536]{1,0:T(8,128)(2,1)} %dynamic-slice_convert_fusion.2), channel_id=1, source_target_pairs={{0,1},{1,0},{2,3},{3,2},{4,5},{5,4},{6,7},{7,6},{8,9},{9,8},{10,11... | collective-permute-start | bytes 9437192 | tf_op jit(solution)/shard_map/ppermute | solution.py:34
  568.3 13.7 %collective-permute-start.47 = (bf16[4,2,128,256]{3,2,0,1:T(8,128)(2,1)S(1)}, bf16[4,2,128,256]{3,2,0,1:T(8,128)(2,1)S(1)}, u32[]{:S(2)}, u32[]{:S(2)}) collective-permute-start(bf16[4,2,128,256]{3,2,0,1:T(8,128)(2,1)S(1)} %copy.180), channel_id=1, source_target_pairs={{0,2},{1,3},{2,0},{3,1},{4,6},{5,7},{6,4},{7,5},{8,10},{9,11},{10,... | collective-permute-start | bytes 1572872 | tf_op jit(solution)/shard_map/ppermute | solution.py:34
  572.7 49.9 %collective-permute-start.60 = (bf16[4096,512]{1,0:T(8,128)(2,1)}, bf16[4096,512]{1,0:T(8,128)(2,1)}, u32[]{:S(2)}, u32[]{:S(2)}) collective-permute-start(bf16[4096,512]{1,0:T(8,128)(2,1)} %dynamic-slice_convert_fusion), channel_id=1, source_target_pairs={{0,1},{1,0},{2,3},{3,2},{4,5},{5,4},{6,7},{7,6},{8,9},{9,8},{10,11... | collective-permute-start | bytes 12582920 | tf_op jit(solution)/shard_map/ppermute | solution.py:34
  582.2 7.2 collective-permute-start.48
  595.1 8.6 %collective-permute-start.50 = (bf16[1,128,256]{2,1,0:T(8,128)(2,1)}, bf16[1,128,256]{2,1,0:T(8,128)(2,1)}, u32[]{:S(2)}, u32[]{:S(2)}) collective-permute-start(bf16[1,128,256]{2,1,0:T(8,128)(2,1)} %constant_dynamic-slice_fusion.7), channel_id=1, source_target_pairs={{0,8},{1,9},{2,10},{3,11},{4,12},{5,13},{6,14},{7,15},{8,0},{9,1},... | collective-permute-start | bytes 196616 | tf_op jit(solution)/shard_map/ppermute | solution.py:34
  597.5 123.0 %all-to-all-start = ((f32[32,138,128]{2,1,0:T(8,128)}), f32[32,138,128]{2,1,0:T(8,128)S(1)}, u32[]{:S(2)}, u32[]{:S(2)}) async-start(f32[32,138,128]{2,1,0:T(8,128)} %bitcast.231), calls=%async_computation | async-start | bytes 4718592 | tf_op jit(solution)/shard_map/all_to_all | solution.py:416
  605.2 88.2 %collective-permute-start.51 = (bf16[128,256]{1,0:T(8,128)(2,1)}, bf16[128,256]{1,0:T(8,128)(2,1)S(1)}, u32[]{:S(2)}, u32[]{:S(2)}) collective-permute-start(bf16[128,256]{1,0:T(8,128)(2,1)} %fusion.79), channel_id=1, source_target_pairs={{0,2},{1,3},{2,0},{3,1},{4,6},{5,7},{6,4},{7,5},{8,10},{9,11},{10,... | collective-permute-start | bytes 196616 | tf_op jit(solution)/shard_map/ppermute | solution.py:34
  612.8 53.9 %collective-permute-start.40 = (bf16[4,128,1536]{2,1,0:T(8,128)(2,1)}, bf16[4,128,1536]{2,1,0:T(8,128)(2,1)}, u32[]{:S(2)}, u32[]{:S(2)}) collective-permute-start(bf16[4,128,1536]{2,1,0:T(8,128)(2,1)} %dynamic-slice_bitcast_fusion.1), channel_id=1, source_target_pairs={{0,4},{1,5},{2,6},{3,7},{4,0},{5,1},{6,2},{7,3},{8,12},{9,13},{10,... | collective-permute-start | bytes 4718600 | tf_op jit(solution)/shard_map/ppermute | solution.py:34
  621.7 89.8 %collective-permute-start.54 = (bf16[4,128,2048]{2,1,0:T(8,128)(2,1)}, bf16[4,128,2048]{2,1,0:T(8,128)(2,1)}, u32[]{:S(2)}, u32[]{:S(2)}) collective-permute-start(bf16[4,128,2048]{2,1,0:T(8,128)(2,1)} %dynamic-slice_bitcast_fusion), channel_id=1, source_target_pairs={{0,4},{1,5},{2,6},{3,7},{4,0},{5,1},{6,2},{7,3},{8,12},{9,13},{10,... | collective-permute-start | bytes 6291464 | tf_op jit(solution)/shard_map/ppermute | solution.py:34
  631.9 84.0 %collective-permute-start.61 = (bf16[4,2,512,256]{3,2,0,1:T(8,128)(2,1)}, bf16[4,2,512,256]{3,2,0,1:T(8,128)(2,1)}, u32[]{:S(2)}, u32[]{:S(2)}) collective-permute-start(bf16[4,2,512,256]{3,2,0,1:T(8,128)(2,1)} %copy.187), channel_id=1, source_target_pairs={{0,2},{1,3},{2,0},{3,1},{4,6},{5,7},{6,4},{7,5},{8,10},{9,11},{10,... | collective-permute-start | bytes 6291464 | tf_op jit(solution)/shard_map/ppermute | solution.py:34
  670.6 30.1 %collective-permute-start.41 = (bf16[4,128,768]{2,1,0:T(8,128)(2,1)}, bf16[4,128,768]{2,1,0:T(8,128)(2,1)}, u32[]{:S(2)}, u32[]{:S(2)}) collective-permute-start(bf16[4,128,768]{2,1,0:T(8,128)(2,1)} %constant_dynamic-slice_fusion.13), channel_id=1, source_target_pairs={{0,2},{1,3},{2,0},{3,1},{4,6},{5,7},{6,4},{7,5},{8,10},{9,11},{10,... | collective-permute-start | bytes 2359304 | tf_op jit(solution)/shard_map/ppermute | solution.py:34
  694.4 24.8 %collective-permute-start.52 = (bf16[128,512]{1,0:T(8,128)(2,1)S(1)}, bf16[128,512]{1,0:T(8,128)(2,1)S(1)}, u32[]{:S(2)}, u32[]{:S(2)}) collective-permute-start(bf16[128,512]{1,0:T(8,128)(2,1)S(1)} %maximum_select_fusion.7), channel_id=1, source_target_pairs={{0,1},{1,0},{2,3},{3,2},{4,5},{5,4},{6,7},{7,6},{8,9},{9,8},{10,11... | collective-permute-start | bytes 393224 | tf_op jit(solution)/shard_map/ppermute | solution.py:34
  703.1 23.1 %collective-permute-start.42 = (bf16[2,128,768]{2,1,0:T(8,128)(2,1)}, bf16[2,128,768]{2,1,0:T(8,128)(2,1)}, u32[]{:S(2)}, u32[]{:S(2)}) collective-permute-start(bf16[2,128,768]{2,1,0:T(8,128)(2,1)} %constant_dynamic-slice_fusion.12), channel_id=1, source_target_pairs={{0,16},{1,17},{2,18},{3,19},{4,20},{5,21},{6,22},{7,23},{8,24},{9,... | collective-permute-start | bytes 1179656 | tf_op jit(solution)/shard_map/ppermute | solution.py:34
  715.8 24.3 %collective-permute-start.55 = (bf16[4,128,1024]{2,1,0:T(8,128)(2,1)}, bf16[4,128,1024]{2,1,0:T(8,128)(2,1)}, u32[]{:S(2)}, u32[]{:S(2)}) collective-permute-start(bf16[4,128,1024]{2,1,0:T(8,128)(2,1)} %constant_dynamic-slice_fusion.6), channel_id=1, source_target_pairs={{0,2},{1,3},{2,0},{3,1},{4,6},{5,7},{6,4},{7,5},{8,10},{9,11},{10,... | collective-permute-start | bytes 3145736 | tf_op jit(solution)/shard_map/ppermute | solution.py:34
  719.1 24.3 %collective-permute-start.62 = (bf16[4,512,256]{2,1,0:T(8,128)(2,1)}, bf16[4,512,256]{2,1,0:T(8,128)(2,1)}, u32[]{:S(2)}, u32[]{:S(2)}) collective-permute-start(bf16[4,512,256]{2,1,0:T(8,128)(2,1)} %dynamic-slice_bitcast_fusion.2), channel_id=1, source_target_pairs={{0,4},{1,5},{2,6},{3,7},{4,0},{5,1},{6,2},{7,3},{8,12},{9,13},{10,... | collective-permute-start | bytes 3145736 | tf_op jit(solution)/shard_map/ppermute | solution.py:34
  727.4 19.8 %collective-permute-start.43 = (bf16[1,128,768]{2,1,0:T(8,128)(2,1)S(1)}, bf16[1,128,768]{2,1,0:T(8,128)(2,1)S(1)}, u32[]{:S(2)}, u32[]{:S(2)}) collective-permute-start(bf16[1,128,768]{2,1,0:T(8,128)(2,1)S(1)} %constant_dynamic-slice_fusion.11), channel_id=1, source_target_pairs={{0,8},{1,9},{2,10},{3,11},{4,12},{5,13},{6,14},{7,15},{8,0},{9,1},... | collective-permute-start | bytes 589832 | tf_op jit(solution)/shard_map/ppermute | solution.py:34
  742.1 36.5 %collective-permute-start.56 = (bf16[2,128,1024]{2,1,0:T(8,128)(2,1)S(1)}, bf16[2,128,1024]{2,1,0:T(8,128)(2,1)S(1)}, u32[]{:S(2)}, u32[]{:S(2)}) collective-permute-start(bf16[2,128,1024]{2,1,0:T(8,128)(2,1)S(1)} %constant_dynamic-slice_fusion.5), channel_id=1, source_target_pairs={{0,16},{1,17},{2,18},{3,19},{4,20},{5,21},{6,22},{7,23},{8,24},{9,... | collective-permute-start | bytes 1572872 | tf_op jit(solution)/shard_map/ppermute | solution.py:34
  745.0 44.9 %collective-permute-start.63 = (bf16[2,512,256]{2,1,0:T(8,128)(2,1)S(1)}, bf16[2,512,256]{2,1,0:T(8,128)(2,1)S(1)}, u32[]{:S(2)}, u32[]{:S(2)}) collective-permute-start(bf16[2,512,256]{2,1,0:T(8,128)(2,1)S(1)} %constant_dynamic-slice_fusion.1), channel_id=1, source_target_pairs={{0,16},{1,17},{2,18},{3,19},{4,20},{5,21},{6,22},{7,23},{8,24},{9,... | collective-permute-start | bytes 1572872 | tf_op jit(solution)/shard_map/ppermute | solution.py:34
  747.2 49.5 %collective-permute-start.44 = (bf16[128,768]{1,0:T(8,128)(2,1)S(1)}, bf16[128,768]{1,0:T(8,128)(2,1)S(1)}, u32[]{:S(2)}, u32[]{:S(2)}) collective-permute-start(bf16[128,768]{1,0:T(8,128)(2,1)S(1)} %fusion.76), channel_id=1, source_target_pairs={{0,2},{1,3},{2,0},{3,1},{4,6},{5,7},{6,4},{7,5},{8,10},{9,11},{10,... | collective-permute-start | bytes 589832 | tf_op jit(solution)/shard_map/ppermute | solution.py:34
  778.9 17.3 %collective-permute-start.57 = (bf16[1,128,1024]{2,1,0:T(8,128)(2,1)S(1)}, bf16[1,128,1024]{2,1,0:T(8,128)(2,1)S(1)}, u32[]{:S(2)}, u32[]{:S(2)}) collective-permute-start(bf16[1,128,1024]{2,1,0:T(8,128)(2,1)S(1)} %constant_dynamic-slice_fusion.4), channel_id=1, source_target_pairs={{0,8},{1,9},{2,10},{3,11},{4,12},{5,13},{6,14},{7,15},{8,0},{9,1},... | collective-permute-start | bytes 786440 | tf_op jit(solution)/shard_map/ppermute | solution.py:34
  790.1 11.8 %collective-permute-start.64 = (bf16[1,512,256]{2,1,0:T(8,128)(2,1)S(1)}, bf16[1,512,256]{2,1,0:T(8,128)(2,1)S(1)}, u32[]{:S(2)}, u32[]{:S(2)}) collective-permute-start(bf16[1,512,256]{2,1,0:T(8,128)(2,1)S(1)} %constant_dynamic-slice_fusion), channel_id=1, source_target_pairs={{0,8},{1,9},{2,10},{3,11},{4,12},{5,13},{6,14},{7,15},{8,0},{9,1},... | collective-permute-start | bytes 786440 | tf_op jit(solution)/shard_map/ppermute | solution.py:34
  796.3 7.3 collective-permute-start.58
  796.8 14.1 %collective-permute-start.45 = (bf16[128,1536]{1,0:T(8,128)(2,1)S(1)}, bf16[128,1536]{1,0:T(8,128)(2,1)S(1)}, u32[]{:S(2)}, u32[]{:S(2)}) collective-permute-start(bf16[128,1536]{1,0:T(8,128)(2,1)S(1)} %maximum_select_fusion.5), channel_id=1, source_target_pairs={{0,1},{1,0},{2,3},{3,2},{4,5},{5,4},{6,7},{7,6},{8,9},{9,8},{10,11... | collective-permute-start | bytes 1179656 | tf_op jit(solution)/shard_map/ppermute | solution.py:34
  801.9 7.5 collective-permute-start.65
  803.7 8.5 %collective-permute-start.59 = (bf16[128,2048]{1,0:T(8,128)(2,1)S(1)}, bf16[128,2048]{1,0:T(8,128)(2,1)S(1)}, u32[]{:S(2)}, u32[]{:S(2)}) collective-permute-start(bf16[128,2048]{1,0:T(8,128)(2,1)S(1)} %maximum_select_fusion.3), channel_id=1, source_target_pairs={{0,1},{1,0},{2,3},{3,2},{4,5},{5,4},{6,7},{7,6},{8,9},{9,8},{10,11... | collective-permute-start | bytes 1572872 | tf_op jit(solution)/shard_map/ppermute | solution.py:34
  (113 other events, 2017.0 us)

commit v2 on v1

v2 whole, which is shorter than its diff:
```python
import functools

import jax
import jax.numpy as jnp
from jax import lax
from jax.experimental import pallas as pl
from jax.experimental.pallas import tpu as pltpu
from jax.sharding import PartitionSpec as P

HEADS = 16
BOTH = ("fsdp", "dp")
LOW = jnp.bfloat16
F32 = jnp.float32
NT = (((1,), (1,)), ((), ()))
TN = (((0,), (0,)), ((), ()))


def flips(which):
    pairs = []
    for f in range(8):
        for d in range(4):
            z, y, x, c = f // 2, f % 2, d // 2, d % 2
            if which == "x":
                x = 1 - x
            elif which == "y":
                y = 1 - y
            elif which == "c":
                c = 1 - c
            elif which == "z1":
                z = z ^ 1
            elif which == "z2":
                z = z ^ 2
            pairs.append((f * 4 + d, (z * 2 + y) * 4 + x * 2 + c))
    return pairs


def swap(values, which):
    return lax.ppermute(values, BOTH, flips(which))


def coords():
    f, d = lax.axis_index("fsdp"), lax.axis_index("dp")
    return f // 2, f % 2, d // 2, d % 2


def call(kernel, grid, ins, outs, flops=0, nbytes=0, scratch=(), prefetch=0, aliases=None, limit=18, after=()):
    after = tuple(after)

    def spec(block, index):
        if block is None:
            return pl.BlockSpec(memory_space=pl.ANY)
        if index in constant and grid:
            return pl.BlockSpec(block, index, pipeline_mode=pl.Buffered(1))
        return pl.BlockSpec(block, index)

    def body(*refs):
        n = prefetch + len(ins)
        kernel(*refs[:n], *refs[n + len(after) :])

    run = pl.pallas_call(
        body,
        out_shape=[jax.ShapeDtypeStruct(shape, kind) for shape, kind, _, _ in outs],
        grid_spec=pltpu.PrefetchScalarGridSpec(
            num_scalar_prefetch=prefetch,
            grid=grid,
            in_specs=[spec(block, index) for block, index in ins] + [spec(None, None)] * len(after),
            out_specs=[spec(block, index) for _, _, block, index in outs],
            scratch_shapes=scratch,
        ),
        input_output_aliases=aliases or {},
        compiler_params=pltpu.CompilerParams(
            vmem_limit_bytes=limit * 2**20, dimension_semantics=("arbitrary",) * len(grid)
        ),
        cost_estimate=pl.CostEstimate(flops=0, bytes_accessed=1024, transcendentals=0),
    )
    return lambda *args: run(*args, *after)


def simple(kernel, args, outs, where=None, after=(), limit=12):
    def whole(shape):
        return shape, lambda *_: (0,) * len(shape)

    prefetch = 0 if where is None else 1
    run = call(
        kernel,
        (),
        [whole(a.shape) for a in args],
        [(shape, kind, *whole(shape)) for shape, kind in outs],
        prefetch=prefetch,
        after=after,
        limit=limit,
    )
    return run(*(() if where is None else (where,)), *args)


constant = []


def fixed(*index):
    constant.append(lambda *grid: index)
    return constant[-1]


def ends(n):
    e = n * 3 // 8
    return e // 2, (n - 2 * e) // 2


def end_start(n, x, c):
    eh, mh = ends(n)
    return x * (n - 2 * eh) + c * eh


def middle_start(n, c):
    eh, mh = ends(n)
    return 2 * eh + c * mh


COLS, ROWS = 2048, 256
CE, CM = ends(COLS)
RE, RM = ends(ROWS)
CW, RW = CE + CM, RE + RM


def lanes(start, size=128):
    return pl.ds(start if isinstance(start, int) else pl.multiple_of(start, 128), size)


def own_columns(where, dest, read):
    x, c = where[2], where[3]
    for i in range(CW // 128):
        start = end_start(COLS, x, c) + i * 128 if i < CE // 128 else middle_start(COLS, c) + i * 128 - CE
        dest[:, i * 128 : (i + 1) * 128] = read(start)


def own_first_kernel(where, qkv, out_w, parts):
    own_columns(where, parts.at[0], lambda start: qkv[:, lanes(start)])
    own_columns(
        where,
        parts.at[1],
        lambda start: jnp.where(
            start < 1024, qkv[:, lanes(2048 + jnp.minimum(start, 896))], out_w[:, lanes(jnp.maximum(start - 1024, 0))]
        ),
    )


def own_other_kernel(where, up_w, down_w, parts, tall):
    x, c = where[2], where[3]
    for half in range(2):
        own_columns(
            where, parts.at[half], lambda start: up_w[:, lanes((start // 256) * 512 + half * 256 + start % 256)]
        )
        for size, first, at in ((RE, end_start(ROWS, x, c), 0), (RM, middle_start(ROWS, c), RE)):
            tall[half, at : at + size, :] = down_w[pl.ds(pl.multiple_of(half * 256 + first, 16), size), :]


def move(jobs, after=()):
    args = []
    for _, copies in jobs:
        for array, _, _ in copies:
            if not any(array is a for a in args):
                args.append(array)

    def kernel(*refs):
        outs = refs[len(args) :]
        for out, (_, copies) in zip(outs, jobs, strict=True):
            for array, read, write in copies:
                ref = refs[[i for i, a in enumerate(args) if a is array][0]]
                out[write] = ref[read if read != () else ...]

    return simple(kernel, args, [(shape, LOW) for shape, _ in jobs], after=after)


class Piece:
    def __init__(self, part, index, shape, axis):
        self.part, self.index, self.shape, self.axis = part, index, shape, axis
        self.e = CE if axis == 1 else RE
        self.inner = (slice(0, 128), slice(0, CW)) if axis == 1 else (slice(None), slice(None))
        self.end = (slice(0, 128), slice(0, CE)) if axis == 1 else (slice(0, RE), slice(None))

    def two(self):
        return (2, *self.shape), [(self.part, self.index, 0), (self.near, self.near_index, 1)]

    def four(self):
        return (4, *self.shape), [
            (self.part, self.index, 0),
            (self.near, self.near_index, 1),
            (self.far, slice(None), slice(2, 4)),
        ]

    def blocks(self):
        found = [(self.near, self.near_index)] + [(self.far, (i,)) for i in range(2)]
        return found + [(self.beside, (i,)) for i in range(4)]

    def across_send(self):
        shape = (128, CE) if self.axis == 1 else (RE, 1024)
        return (7, *shape), [(a, (*i, *self.end), j) for j, (a, i) in enumerate(self.blocks())]

    def core_send(self):
        if self.axis == 1:
            shape, first, last = (128, CW + CE), (slice(None), slice(0, CW)), (slice(None), slice(CW, CW + CE))
        else:
            shape, first, last = (RW + RE, 1024), (slice(0, RW), slice(None)), (slice(RW, RW + RE), slice(None))
        copies = [(a, (*i, *self.inner), (j, *first)) for j, (a, i) in enumerate(self.blocks())]
        return (7, *shape), copies + [(self.across, j, (j, *last)) for j in range(7)]

    def move_z1(self, near, near_index):
        self.near, self.near_index = near, near_index

    def move_z2(self, two):
        self.far = swap(two, "z2")

    def move_y(self, four):
        self.beside = swap(four, "y")

    def move_x(self, send):
        self.across = swap(send, "x")

    def move_c(self, send):
        self.other = swap(send, "c")


def assemble_kernel(axis, own_copies, near_index, where, *refs):
    n_own = len(own_copies)
    owns = refs[:n_own]
    near, far, beside, across, other, out, sems, out_sems, hold = refs[n_own:]
    z, y, x, c = where[0], where[1], where[2], where[3]
    rows = 128 if axis == 1 else ROWS
    size = COLS if axis == 1 else ROWS
    eh, mh = ends(size)

    def at(base, start, count):
        if axis == 1:
            return hold.at[pl.ds(base, rows), lanes(start, count)]
        return hold.at[pl.ds(pl.multiple_of(base + start, 16), count), :]

    def cut(block, start, count):
        if axis == 1:
            return block.at[pl.ds(0, 128), pl.ds(start, count)]
        return block.at[pl.ds(start, count), :]

    groups, bases = [], []
    for j in range(8):
        zz = (z, z ^ 1, z ^ 2, z ^ 3)[j % 4]
        yy = y if j < 4 else 1 - y
        base = pl.multiple_of((zz * 2 + yy) * rows, rows)
        if j == 0:
            copies = []
            for ref, (read, start, count) in zip(owns, own_copies, strict=True):
                for k in range(len(read)):
                    copies.append((ref.at[read[k]], at(base, start[k], count)))
        else:
            close = near.at[near_index[0]] if near_index else near
            mine = (close, far.at[0], far.at[1], beside.at[0], beside.at[1], beside.at[2], beside.at[3])[j - 1]
            oc = 1 - c
            copies = [
                (cut(mine, 0, eh), at(base, end_start(size, x, c), eh)),
                (cut(mine, eh, mh), at(base, middle_start(size, c), mh)),
                (cut(across.at[j - 1], 0, eh), at(base, end_start(size, 1 - x, c), eh)),
                (cut(other.at[j - 1], 0, eh), at(base, end_start(size, x, oc), eh)),
                (cut(other.at[j - 1], eh, mh), at(base, middle_start(size, oc), mh)),
                (cut(other.at[j - 1], eh + mh, eh), at(base, end_start(size, 1 - x, oc), eh)),
            ]
        group = [pltpu.make_async_copy(s, d, sems.at[j]) for s, d in copies]
        for copy in group:
            copy.start()
        groups.append(group)
        bases.append(base)
    outs = []
    for j in range(8):
        for copy in groups[j]:
            copy.wait()
        rows_of = pl.ds(bases[j], rows)
        copy = pltpu.make_async_copy(hold.at[rows_of, :], out.at[rows_of, :], out_sems.at[j])
        copy.start()
        outs.append(copy)
    for copy in outs:
        copy.wait()


def assemble(where, piece, owns, after=()):
    shape = (1024, COLS) if piece.axis == 1 else (8 * ROWS, 1024)
    args = [o[0] for o in owns] + [piece.near, piece.far, piece.beside, piece.across, piece.other]
    return call(
        functools.partial(assemble_kernel, piece.axis, [o[1:] for o in owns], piece.near_index),
        (),
        [(None, None)] * len(args),
        [(shape, LOW, None, None)],
        prefetch=1,
        scratch=[pltpu.SemaphoreType.DMA((8,)), pltpu.SemaphoreType.DMA((8,)), pltpu.VMEM(shape, LOW)],
        after=after,
        limit=8,
    )(where, *args)[0]


def small_kernel(where, four, beside, time_index, table, vec, up_b, scale):
    z, y = where[0], where[1]
    for j in range(8):
        block = four.at[j] if j < 4 else beside.at[j - 4]
        shard = (z ^ (j % 4)) * 2 + (y if j < 4 else 1 - y)
        table[:, lanes(shard * 128)] = block[:128, :]
        vec[:, lanes(shard * 128)] = block[128:, :].astype(F32)
        for row in range(4):
            unit = lanes(shard * 256 + (row % 2) * 128)
            up_b[row // 2 : row // 2 + 1, unit] = block[134 + row : 135 + row, :].astype(F32)
    numbers = lax.broadcasted_iota(jnp.int32, (time_index.shape[0], 128), 1)
    one_hot = (numbers == time_index[...]).astype(F32).astype(LOW)
    scale[...] = 1.0 + jnp.dot(one_hot, table[...], preferred_element_type=F32)


def small_params(where, four, beside, time_index, after=()):
    return simple(
        small_kernel,
        (four, beside, time_index),
        [((128, 1024), LOW), ((16, 1024), F32), ((2, 2048), F32), ((time_index.shape[0], 1024), F32)],
        where=where,
        after=after,
    )


def rows_kernel(d_emb, sums_one, sums_two, up_a, up_b, times, out):
    for s in range(8):
        here = slice(s * 128, (s + 1) * 128)
        rows = [d_emb[i, :, here] for i in range(8)]
        rows += [sums_one[0:2, here], sums_two[2:3, here], sums_two[0:2, here], sums_two[3:4, here]]
        for sums in (up_a, up_b):
            rows += [sums[:, s * 256 + j * 128 : s * 256 + (j + 1) * 128] for j in range(2)]
        rows += [times[...], jnp.zeros((5, 128), F32)]
        block = jnp.concatenate(rows, axis=0)
        for copy in range(4):
            out[s * 4 + copy] = block


def mm(a, b):
    return jnp.dot(a, b, preferred_element_type=F32)


def mm_nt(a, b):
    return lax.dot_general(a, b, NT, preferred_element_type=F32)


def mm_tn(a, b):
    return lax.dot_general(a, b, TN, preferred_element_type=F32)


def centre(values):
    mean = jnp.mean(values, axis=-1, keepdims=True)
    centred = values - mean
    scale = lax.rsqrt(jnp.mean(centred * centred, axis=-1, keepdims=True) + 1e-05)
    return centred * scale, scale


def first_norm_kernel(tokens, gain, bias, scale, scaled):
    hat, _ = centre(tokens[...].astype(F32))
    scaled[...] = ((hat * gain[...] + bias[...]) * scale[0]).astype(LOW)


def first_norm(tokens, gain, bias, scale, after=()):
    rows, width = tokens.shape
    seqs = scale.shape[0]
    length = rows // seqs
    return call(
        first_norm_kernel,
        (seqs,),
        [
            ((length, width), lambda i: (i, 0)),
            ((1, width), fixed(0, 0)),
            ((1, width), fixed(0, 0)),
            ((1, 1, width), lambda i: (i, 0, 0)),
        ],
        [((rows, width), LOW, (length, width), lambda i: (i, 0))],
        after=after,
    )(tokens, gain, bias, scale)[0]


def halves(values):
    lane = lax.broadcasted_iota(jnp.int32, values.shape, 1)
    zero = jnp.zeros_like(values)
    return jnp.concatenate([jnp.where(lane < 64, values, zero), jnp.where(lane < 64, zero, values)], axis=0)


def side(values):
    n = values.shape[0] // 2
    return jnp.concatenate([values[:n], values[n:]], axis=1)


def project_kernel(x, w, out):
    out[...] = mm(x[...], w[...]).astype(LOW)


def project(x, w, tile=512, after=()):
    rows, width = x.shape
    n = w.shape[1]
    return call(
        project_kernel,
        (n // tile,),
        [((rows, width), fixed(0, 0)), ((width, tile), lambda i: (0, i))],
        [((rows, n), LOW, (rows, tile), lambda i: (0, i))],
        after=after,
    )(x, w)[0]


def units_of(rows, length, at_once=8):
    units = []
    for seq in range(rows // length):
        for pair in range(2):
            units.append((seq, pair, (slice(seq * length, (seq + 1) * length), slice(pair * 128, (pair + 1) * 128))))
    return [units[i : i + at_once] for i in range(0, len(units), at_once)]


def attend_kernel(length, scaled, wv, q_in, k_in, *refs):
    v_out, probs_out, mix_out = refs[-3:]
    factor = 64 ** (-0.5) * 1.4426950408889634
    v_out[...] = mm(scaled[...], wv[...]).astype(LOW)
    for units in units_of(scaled.shape[0], length):
        scores = [mm_nt(halves(q_in[here]), k_in[here]) for _, _, here in units]
        found = []
        for s in scores:
            e = jnp.exp2((s - jnp.max(s, axis=-1, keepdims=True)) * factor)
            found.append((e * (1.0 / jnp.sum(e, axis=-1, keepdims=True))).astype(LOW))
        for (seq, pair, here), probs in zip(units, found, strict=True):
            probs_out[0, seq, pair] = probs
            mix_out[here] = mm(side(probs), halves(v_out[here])).astype(LOW)


def attend(scaled, qk, vo, length, first=0, count=None, earlier=(), after=()):
    rows, width = scaled.shape
    groups = width // 256
    seqs = rows // length
    count = groups if count is None else count
    column = lambda i: (0, first + i)
    wide = ((rows, width), LOW, (rows, 256), column)
    probs = (groups, seqs, 2, 2 * length, length)
    return call(
        functools.partial(attend_kernel, length),
        (count,),
        [
            ((rows, width), fixed(0, 0)),
            ((width, 256), column),
            ((rows, 256), column),
            ((rows, 256), lambda i: (0, groups + first + i)),
        ]
        + [(None, None)] * len(earlier),
        [wide, (probs, LOW, (1, *probs[1:]), lambda i: (first + i, 0, 0, 0, 0)), wide],
        aliases={4 + i: i for i in range(len(earlier))},
        after=after,
    )(scaled, vo, qk, qk, *earlier)


def middle_kernel(mix, tokens, w, out_b, gain, bias, middle_out, hidden_out):
    middle = tokens[...].astype(F32) + mm(mix[...], w[...]) + out_b[...]
    middle_out[...] = middle
    hat, _ = centre(middle)
    hidden_out[...] = (hat * gain[...] + bias[...]).astype(LOW)


def second_norm(mix, tokens, vo, out_b, gain, bias, after=()):
    rows, width = tokens.shape
    row = lambda i: (i, 0)
    vec = ((1, width), fixed(0, 0))
    return call(
        middle_kernel,
        (rows // 256,),
        [((256, width), row), ((256, width), row), ((width, width), fixed(0, 1)), vec, vec, vec],
        [((rows, width), F32, (256, width), row), ((rows, width), LOW, (256, width), row)],
        after=after,
    )(mix, tokens, vo, out_b, gain, bias)


def gelu_parts(v):
    cdf = 0.5 + 0.5 * lax.erf(v * 0.5**0.5)
    bell = jnp.exp(-0.5 * v * v)
    return v * cdf, cdf + (v * 0.3989422804014327) * bell


def up_kernel(hidden, w, bias, act, slope):
    value, pull = gelu_parts(mm(hidden[...], w[...]) + bias[...])
    act[...] = value.astype(LOW)
    slope[...] = pull.astype(LOW)


def up(hidden, w, bias, tile=512, after=()):
    rows, width = hidden.shape
    n = w.shape[1]
    column = lambda i: (0, i)
    return call(
        up_kernel,
        (n // tile,),
        [((rows, width), fixed(0, 0)), ((width, tile), column), ((1, tile), column)],
        [((rows, n), LOW, (rows, tile), column)] * 2,
        limit=22,
        after=after,
    )(hidden, w, bias)


def down_kernel(act_a, act_b, first, second, middle, bias, out):
    total = middle[...] + bias[...]
    total += mm(act_a[...], first[...])
    total += mm(act_b[...], second[...])
    out[...] = total.astype(LOW)


def down(acts, ws, middle, bias, tile=256, after=()):
    rows, width = middle.shape
    k = ws[0].shape[0]
    row = lambda i: (i, 0)
    return call(
        down_kernel,
        (rows // tile,),
        [((tile, k), row)] * 2
        + [((k, width), fixed(0, 0))] * 2
        + [((tile, width), row), ((1, width), fixed(0, 0))],
        [((rows, width), LOW, (tile, width), row)],
        limit=24,
        after=after,
    )(*acts, *ws, middle, bias)[0]


def pull_kernel(cot, w, slope, *refs):
    d_pre, sums = refs[-2:]
    value = (mm_nt(cot[...], w[...]) * slope[...].astype(F32)).astype(LOW)
    d_pre[0] = value
    sums[...] = jnp.sum(value.astype(F32), axis=0, keepdims=True)


def pull(cot, w, slope, half, earlier=None, tile=512, after=()):
    rows, width = cot.shape
    n = w.shape[0]
    column = lambda i: (0, i)
    ins = [((rows, width), fixed(0, 0)), ((tile, width), lambda i: (i, 0)), ((rows, tile), column)]
    return call(
        pull_kernel,
        (n // tile,),
        ins + ([] if earlier is None else [(None, None)]),
        [((2, rows, n), LOW, (1, rows, tile), lambda i: (half, 0, i)), ((1, n), F32, (1, tile), column)],
        aliases={} if earlier is None else {3: 0},
        after=after,
    )(cot, w, slope, *(() if earlier is None else (earlier,)))


def norm_back(d_out, hat, scale, gain):
    e = d_out * gain
    mean = jnp.mean(e, axis=-1, keepdims=True)
    slant = jnp.mean(e * hat, axis=-1, keepdims=True)
    return (e - mean - hat * slant) * scale


def fold(*rows_of):
    sums = [jnp.sum(v, axis=0, keepdims=True) for v in rows_of]
    return jnp.concatenate(sums + [jnp.zeros_like(sums[0])] * (8 - len(sums)), axis=0)


def middle_back_kernel(d_pre, wa, wb, middle, cot, gain, w_out, d_middle_out, d_low_out, d_mix_out, sums):
    d_hidden = mm_nt(d_pre[0], wa[...]) + mm_nt(d_pre[1], wb[...])
    hat, scale = centre(middle[...])
    d_middle = cot[...].astype(F32) + norm_back(d_hidden, hat, scale, gain[...])
    d_middle_out[...] = d_middle
    d_low = d_middle.astype(LOW)
    d_low_out[...] = d_low
    d_mix_out[...] = mm_nt(d_low, w_out[...]).astype(LOW)

    @pl.when(pl.program_id(0) == 0)
    def _():
        sums[...] = jnp.zeros_like(sums)

    sums[...] += fold(d_hidden * hat, d_hidden, d_low.astype(F32), cot[...].astype(F32))


def middle_back(d_pre, ws, middle, cot, gain, vo, tile=256, after=()):
    rows, width = middle.shape
    row = lambda i: (i, 0)
    return call(
        middle_back_kernel,
        (rows // tile,),
        [
            ((2, tile, d_pre.shape[2]), lambda i: (0, i, 0)),
            (ws[0].shape, fixed(0, 0)),
            (ws[1].shape, fixed(0, 0)),
            ((tile, width), row),
            ((tile, width), row),
            ((1, width), fixed(0, 0)),
            ((width, width), fixed(0, 1)),
        ],
        [
            ((rows, width), F32, (tile, width), row),
            ((rows, width), LOW, (tile, width), row),
            ((rows, width), LOW, (tile, width), row),
            ((8, width), F32, (8, width), fixed(0, 0)),
        ],
        limit=32,
        after=after,
    )(d_pre, *ws, middle, cot, gain, vo)


def attend_back_kernel(length, d_mix, probs, q_in, k_in, v_in, *refs):
    out = refs[-1]
    factor = 64 ** (-0.5)
    for units in units_of(d_mix.shape[0], length, 4):
        dms = [halves(d_mix[here]) for _, _, here in units]
        d_probs = [mm_nt(dm, v_in[here]) for dm, (_, _, here) in zip(dms, units, strict=True)]
        found = []
        for d, (seq, pair, _) in zip(d_probs, units, strict=True):
            high = probs[0, seq, pair].astype(F32)
            found.append((high * (d - jnp.sum(d * high, axis=-1, keepdims=True))).astype(LOW))
        for dm, d_scores, (seq, pair, here) in zip(dms, found, units, strict=True):
            out[(2, *here)] = mm_tn(probs[0, seq, pair], dm).astype(LOW)
            out[(0, *here)] = (mm(side(d_scores), halves(k_in[here])) * factor).astype(LOW)
            out[(1, *here)] = (mm_tn(d_scores, halves(q_in[here])) * factor).astype(LOW)


def attend_back(d_mix, probs, qk, v, length, first=0, count=None, earlier=(), after=()):
    rows, width = d_mix.shape
    count = width // 256 if count is None else count
    wide = ((rows, 256), lambda i: (0, first + i))
    return call(
        functools.partial(attend_back_kernel, length),
        (count,),
        [
            wide,
            ((1,) + probs.shape[1:], lambda i: (first + i, 0, 0, 0, 0)),
            wide,
            ((rows, 256), lambda i: (0, width // 256 + first + i)),
            wide,
        ]
        + [(None, None)] * len(earlier),
        [((3, rows, width), LOW, (3, rows, 256), lambda i: (0, 0, first + i))],
        aliases={5 + i: i for i in range(len(earlier))},
        after=after,
    )(d_mix, probs, qk, qk, v, *earlier)[0]


def input_back_kernel(length, d, wq, wk, wv, tokens, d_middle, gain, bias, scale, out, sums, d_emb):
    d_scaled = mm_nt(d[0], wq[...]) + mm_nt(d[1], wk[...]) + mm_nt(d[2], wv[...])
    hat, spread = centre(tokens[...].astype(F32))
    normed = hat * gain[...] + bias[...]
    count = tokens.shape[0] // length
    parts = []
    for i in range(count):
        here = slice(i * length, (i + 1) * length)
        d_emb[i] = jnp.sum(d_scaled[here] * normed[here], axis=0, keepdims=True)
        parts.append(d_scaled[here] * scale[i])
    d_normed = jnp.concatenate(parts, axis=0)
    out[...] = (d_middle[...] + norm_back(d_normed, hat, spread, gain[...])).astype(LOW)

    @pl.when(pl.program_id(0) == 0)
    def _():
        sums[...] = jnp.zeros_like(sums)

    sums[...] += fold(d_normed * hat, d_normed)


def input_back(d_packed, qk, vo, tokens, d_middle, gain, bias, scale, tile=256, after=()):
    rows, width = tokens.shape
    seqs = scale.shape[0]
    length = rows // seqs
    row = lambda i: (i, 0)
    wide = ((tile, width), row)
    vec = ((1, width), fixed(0, 0))
    some = ((tile // length, 1, width), lambda i: (i, 0, 0))
    return call(
        functools.partial(input_back_kernel, length),
        (rows // tile,),
        [
            ((3, tile, width), lambda i: (0, i, 0)),
            ((width, width), fixed(0, 0)),
            ((width, width), fixed(0, 1)),
            ((width, width), fixed(0, 0)),
            wide, wide, vec, vec, some,
        ],
        [
            ((rows, width), LOW, (tile, width), row),
            ((8, width), F32, (8, width), fixed(0, 0)),
            ((seqs, 1, width), F32) + some,
        ],
        limit=26,
        after=after,
    )(d_packed, qk, qk, vo, tokens, d_middle, gain, bias, scale)


def tall_away_kernel(where, a, b, cot, away):
    left = jnp.concatenate([a[...], b[...]], axis=1)
    value = mm_tn(left, cot[...]).astype(LOW)
    x = where[2]
    for xr in range(2):
        for half in range(2):
            low, high = value[half * 256 : half * 256 + 128], value[half * 256 + 128 : half * 256 + 256]
            away[xr, 0, 0, half] = jnp.where((x ^ xr) == 0, low, high)


def tall_shard(zr, yr, where):
    return ((zr ^ where[0]) * 2) + (yr ^ where[1])


def tall_ins(acts, cot, core):
    rows, width = cot.shape
    act = ((rows, 256), lambda zr, yr, where: (0, tall_shard(zr, yr, where)))
    return [act, act, ((rows, width // 2), lambda zr, yr, where: (0, where[3] ^ core))]


def tall_away(where, acts, cot, after=()):
    n = cot.shape[1] // 2
    return call(
        tall_away_kernel,
        (4, 2),
        tall_ins(acts, cot, 1),
        [((2, 2, 4, 2, 128, n), LOW, (2, 1, 1, 2, 128, n), lambda zr, yr, where: (0, yr, zr, 0, 0, 0))],
        prefetch=1,
        after=after,
    )(where, *acts, cot)[0]


def tall_mine_kernel(where, a, b, cot, core, xa, yb, ka, kb):
    left = jnp.concatenate([a[...], b[...]], axis=1)
    value = mm_tn(left, cot[...])
    x = where[2]
    zr, yr = pl.program_id(0), pl.program_id(1)
    sums = []
    for xr in range(2):
        halves_of = []
        for half in range(2):
            low, high = value[half * 256 : half * 256 + 128], value[half * 256 + 128 : half * 256 + 256]
            total = jnp.where((x ^ xr) == 0, low, high) + core[xr, 0, 0, half].astype(F32)
            halves_of.append(total.astype(LOW))
        sums.append(halves_of)

    @pl.when(zr < 2)
    def _():
        for half in range(2):
            ka[0, 0, half] = sums[0][half]
            xa[0, 0, half] = sums[1][half]

    @pl.when((zr >= 2) & (yr == 0))
    def _():
        for xr in range(2):
            for half in range(2):
                kb[xr, 0, half] = sums[xr][half]

    @pl.when((zr >= 2) & (yr == 1))
    def _():
        for xr in range(2):
            for half in range(2):
                yb[xr, 0, half] = sums[xr][half]


def tall_mine(where, acts, cot, core, after=()):
    n = cot.shape[1] // 2
    shape = (2, 2, 2, 128, n)
    by_y = (
        shape,
        LOW,
        (1, 1, 2, 128, n),
        lambda zr, yr, where: (jnp.where(zr < 2, yr, 1), jnp.minimum(zr, 1), 0, 0, 0),
    )
    by_x = (shape, LOW, (2, 1, 2, 128, n), lambda zr, yr, where: (0, jnp.maximum(zr - 2, 0), 0, 0, 0))
    return call(
        tall_mine_kernel,
        (4, 2),
        tall_ins(acts, cot, 0) + [((2, 1, 1, 2, 128, n), lambda zr, yr, where: (0, yr, zr, 0, 0, 0))],
        [by_y, by_x, by_y, by_x],
        prefetch=1,
        after=after,
    )(where, *acts, cot, core)


def row_value(step, lefts, rights, counts, hold):
    first = 0
    for left, right, count in zip(lefts, rights, counts, strict=True):

        def put(left=left, right=right):
            b = right[0] if len(right.shape) == 3 else right[...]
            hold[...] = mm_tn(left[...], b)

        if len(lefts) == 1:
            put()
        else:
            pl.when((step >= first) & (step < first + count))(put)
        first += count


def row_from(where, xr, yr, zr):
    start = ((where[0] ^ zr) * 2 + (where[1] ^ yr)) * 128 + (where[2] ^ xr) * 64
    return pl.ds(pl.multiple_of(start, 64), 64)


def row_away_kernel(counts, where, *refs):
    n = len(counts)
    lefts, rights, away, hold = refs[:n], refs[n : 2 * n], refs[2 * n], refs[2 * n + 1]
    row_value(pl.program_id(0), lefts, rights, counts, hold)
    for xr in range(2):
        for yr in range(2):
            for zr in range(4):
                away[xr, yr, zr] = hold[row_from(where, xr, yr, zr), :].astype(LOW)


def row_mine_kernel(counts, where, *refs):
    n = len(counts)
    lefts, rights = refs[:n], refs[n : 2 * n]
    core, xa, yb, ka, kb, hold = refs[2 * n :]
    row_value(pl.program_id(0), lefts, rights, counts, hold)
    for xr in range(2):
        for yr in range(2):
            for zr in range(4):
                total = hold[row_from(where, xr, yr, zr), :] + core[xr, yr, zr].astype(F32)
                total = total.astype(LOW)
                if zr < 2:
                    (ka if xr == 0 else xa)[yr, zr] = total
                else:
                    (kb if yr == 0 else yb)[xr, zr - 2] = total


def row_specs(pairs, core, tile):
    ins, counts = [], []
    for a, _, _ in pairs:
        ins.append((a.shape, lambda j, where: (0, 0)))
    first = 0
    for _, b, kind in pairs:
        tokens = b.shape[-2]
        if kind == "layers":
            count = b.shape[0] * (b.shape[2] // 2 // tile)
            each = b.shape[2] // 2 // tile
            spec = (
                (1, tokens, tile),
                lambda j, where, f=first, m=count, e=each: (
                    jnp.clip(j - f, 0, m - 1) // e,
                    0,
                    (where[3] ^ core) * e + jnp.clip(j - f, 0, m - 1) % e,
                ),
            )
        elif kind == "layer":
            count = b.shape[2] // tile
            spec = (
                (1, tokens, tile),
                lambda j, where, f=first, m=count: (where[3] ^ core, 0, jnp.clip(j - f, 0, m - 1)),
            )
        else:
            count = b.shape[1] // 2 // tile
            spec = (
                (tokens, tile),
                lambda j, where, f=first, m=count: (0, (where[3] ^ core) * m + jnp.clip(j - f, 0, m - 1)),
            )
        ins.append(spec)
        counts.append(count)
        first += count
    return ins, counts


def row_away(where, pairs, tile=512, after=()):
    ins, counts = row_specs(pairs, 1, tile)
    steps = sum(counts)
    return call(
        functools.partial(row_away_kernel, counts),
        (steps,),
        ins,
        [((2, 2, 4, 64, steps * tile), LOW, (2, 2, 4, 64, tile), lambda j, where: (0, 0, 0, 0, j))],
        prefetch=1,
        scratch=[pltpu.VMEM((1024, tile), F32)],
        after=after,
    )(where, *[a for a, _, _ in pairs], *[b for _, b, _ in pairs])[0]


def row_mine(where, pairs, core, tile=512, after=()):
    ins, counts = row_specs(pairs, 0, tile)
    steps = sum(counts)
    out = ((2, 2, 64, steps * tile), LOW, (2, 2, 64, tile), lambda j, where: (0, 0, 0, j))
    return call(
        functools.partial(row_mine_kernel, counts),
        (steps,),
        ins + [((2, 2, 4, 64, tile), lambda j, where: (0, 0, 0, 0, j))],
        [out] * 4,
        prefetch=1,
        scratch=[pltpu.VMEM((1024, tile), F32)],
        after=after,
    )(where, *[a for a, _, _ in pairs], *[b for _, b, _ in pairs], core)


def add_up(jobs, after=()):
    args = []
    for _, terms in jobs:
        for array, _ in terms:
            if not any(array is a for a in args):
                args.append(array)

    def kernel(*refs):
        for out, (_, terms) in zip(refs[len(args) :], jobs, strict=True):
            total = None
            for array, index in terms:
                value = refs[[i for i, a in enumerate(args) if a is array][0]][index].astype(F32)
                total = value if total is None else total + value
            out[...] = total.astype(LOW)

    return simple(kernel, args, [(shape, LOW) for shape, _ in jobs], after=after)


class Reduction:
    def __init__(self, xa, yb, ka, kb):
        self.ka, self.kb = ka, kb
        self.tail = ka.shape[2:]
        self.xa, self.yb = swap(xa, "x"), swap(yb, "y")

    def second(self):
        shape = (2, *self.tail)
        return [(shape, [(self.ka, 1), (self.xa, 1)]), (shape, [(self.kb, 1), (self.yb, 1)])]

    def go_second(self, ya, xb):
        self.ya, self.xb = swap(ya, "y"), swap(xb, "x")

    def third(self):
        return [((2, *self.tail), [(self.kb, 0), (self.yb, 0), (self.xb, slice(None))])]

    def go_third(self, far):
        self.far = swap(far, "z2")

    def fourth(self):
        return [(self.tail, [(self.ka, (0, 1)), (self.xa, (0, 1)), (self.ya, 1), (self.far, 1)])]

    def go_fourth(self, near):
        self.near = swap(near, "z1")

    def last(self):
        terms = [(self.ka, (0, 0)), (self.xa, (0, 0)), (self.ya, 0), (self.far, 0), (self.near, slice(None))]
        return [(self.tail, terms)]

    def go_last(self, one):
        self.one = one
        self.by_x, self.by_c = swap(one, "x"), swap(one, "c")

    def go_corner(self):
        self.corner = swap(self.by_x, "c")


def tall_shard_kernel(where, one, by_x, by_c, corner, out):
    x, c = where[2], where[3]
    n = one.shape[-1]
    for block, xx, cc in ((one, x, c), (by_x, 1 - x, c), (by_c, x, 1 - c), (corner, 1 - x, 1 - c)):
        for half in range(2):
            rows = pl.ds(pl.multiple_of(half * 256 + xx * 128, 128), 128)
            out[rows, lanes(cc * n, n)] = block[half].astype(F32)


def up_shard_kernel(where, one, by_x, by_c, corner, up_out, out_out):
    x, c = where[2], where[3]
    for block, xx, cc in ((one, x, c), (by_x, 1 - x, c), (by_c, x, 1 - c), (corner, 1 - x, 1 - c)):
        rows = pl.ds(pl.multiple_of(xx * 64, 64), 64)
        for s in range(8):
            up_out[rows, lanes(s * 512 + cc * 256, 256)] = block[:, s * 256 : (s + 1) * 256].astype(F32)
        out_out[rows, lanes(cc * 512, 512)] = block[:, 2048:].astype(F32)


def qkv_shard_kernel(where, one, by_x, by_c, corner, out):
    x, c = where[2], where[3]
    for block, xx, cc in ((one, x, c), (by_x, 1 - x, c), (by_c, x, 1 - c), (corner, 1 - x, 1 - c)):
        rows = pl.ds(pl.multiple_of(xx * 64, 64), 64)
        for layer in range(3):
            out[rows, lanes(layer * 1024 + cc * 512, 512)] = block[:, layer * 512 : (layer + 1) * 512].astype(F32)


def shard_of(kernel, where, r, shapes, after=()):
    return simple(kernel, (r.one, r.by_x, r.by_c, r.corner), [(s, F32) for s in shapes], where=where, after=after)


def table_kernel(got, table, vec):
    n = got.shape[0]
    times = lax.broadcasted_iota(jnp.int32, (128, 8), 0).astype(F32)
    total = jnp.zeros(table.shape, F32)
    sums = jnp.zeros(vec.shape, F32)
    for i in range(n):
        hot = (times == got[i, 18:19, 0:8]).astype(F32)
        total += lax.dot_general(hot, got[i, 0:8, :], (((1,), (0,)), ((), ())), precision=lax.Precision.HIGHEST)
        sums += got[i, 8:24, :]
    table[...] = total
    vec[...] = sums


def normalize(values):
    centred = values - jnp.mean(values, axis=-1, keepdims=True)
    spread = jnp.mean(centred * centred, axis=-1, keepdims=True)
    return centred * lax.rsqrt(spread + 1e-05)


def scaled_norm(values, gain):
    return normalize(values) * gain


def exact_gelu(values):
    return jax.nn.gelu(values, approximate=False)


def layer(
    tokens,
    time_index,
    table_all,
    gain_one,
    bias_one,
    qkv_w,
    out_w,
    out_b,
    gain_two,
    bias_two,
    up_w,
    up_b,
    down_w,
    down_b,
    cotangent,
):
    row_count, model_width = tokens.shape
    seq_count = time_index.shape[0]
    length = row_count // seq_count
    head_dim = model_width // HEADS
    factor = head_dim ** (-0.5)
    levels = table_all.shape[0]
    gain_one_f = gain_one.astype(jnp.float32)
    gain_two_f = gain_two.astype(jnp.float32)
    one_hot = time_index[:, None] == jnp.arange(levels, dtype=jnp.int32)[None, :]
    embedding = jnp.dot(one_hot.astype(jnp.bfloat16), table_all, preferred_element_type=jnp.float32)
    scale_seq = (1.0 + embedding)[:, None, :]
    inputs = tokens.astype(jnp.float32)
    normed = (normalize(inputs) * gain_one_f + bias_one.astype(jnp.float32)).reshape(
        seq_count, length, model_width
    )
    scaled = (normed * scale_seq).astype(jnp.bfloat16).reshape(row_count, model_width)
    packed = jnp.dot(scaled, qkv_w, preferred_element_type=jnp.float32).astype(jnp.bfloat16)
    packed = packed.reshape(seq_count, length, 3, HEADS, head_dim)
    queries = packed[:, :, 0]
    key_heads = packed[:, :, 1]
    value_heads = packed[:, :, 2]
    scores = (
        jnp.einsum("sqhd,skhd->shqk", queries, key_heads, preferred_element_type=jnp.float32)
        * factor
    )
    attn_probs = jax.nn.softmax(scores, axis=-1)
    probs_low = attn_probs.astype(jnp.bfloat16)
    attn_mix = jnp.einsum(
        "shqk,skhd->sqhd", probs_low, value_heads, preferred_element_type=jnp.float32
    )
    attn_mix = attn_mix.astype(jnp.bfloat16).reshape(row_count, model_width)
    middle = (
        inputs
        + jnp.dot(attn_mix, out_w, preferred_element_type=jnp.float32)
        + out_b.astype(jnp.float32)
    )
    hidden_in = (normalize(middle) * gain_two_f + bias_two.astype(jnp.float32)).astype(jnp.bfloat16)
    pre_act = jnp.dot(hidden_in, up_w, preferred_element_type=jnp.float32) + up_b.astype(
        jnp.float32
    )
    activated = exact_gelu(pre_act).astype(jnp.bfloat16)
    block_out = (
        middle
        + jnp.dot(activated, down_w, preferred_element_type=jnp.float32)
        + down_b.astype(jnp.float32)
    ).astype(jnp.bfloat16)
    upstream = cotangent.astype(jnp.float32)
    grad_down = jnp.einsum("ti,td->id", activated, cotangent, preferred_element_type=jnp.float32)
    grad_down_b = jnp.sum(upstream, axis=0)
    d_act = jnp.einsum("td,id->ti", cotangent, down_w, preferred_element_type=jnp.float32)
    gelu_pull = jax.vjp(exact_gelu, pre_act)[1]
    d_pre = gelu_pull(d_act)[0].astype(jnp.bfloat16)
    grad_up = jnp.einsum("ti,tf->if", hidden_in, d_pre, preferred_element_type=jnp.float32)
    grad_up_b = jnp.sum(d_pre.astype(jnp.float32), axis=0)
    d_hidden = jnp.einsum("tf,if->ti", d_pre, up_w, preferred_element_type=jnp.float32)
    grad_ln2_bias = jnp.sum(d_hidden, axis=0)
    second_pull = jax.vjp(scaled_norm, middle, gain_two_f)[1]
    d_mid_part, grad_ln2_gain = second_pull(d_hidden)
    d_middle = upstream + d_mid_part
    d_mid_low = d_middle.astype(jnp.bfloat16)
    grad_out_w = jnp.einsum("ti,td->id", attn_mix, d_mid_low, preferred_element_type=jnp.float32)
    grad_out_b = jnp.sum(d_mid_low.astype(jnp.float32), axis=0)
    d_mix = jnp.einsum("td,id->ti", d_mid_low, out_w, preferred_element_type=jnp.float32)
    d_mix = d_mix.astype(jnp.bfloat16).reshape(seq_count, length, HEADS, head_dim)
    d_probs = jnp.einsum("sqhd,skhd->shqk", d_mix, value_heads, preferred_element_type=jnp.float32)
    d_values = jnp.einsum("shqk,sqhd->skhd", probs_low, d_mix, preferred_element_type=jnp.float32)
    d_scores = (
        attn_probs * (d_probs - jnp.sum(d_probs * attn_probs, axis=-1, keepdims=True))
    ).astype(jnp.bfloat16)
    d_queries = (
        jnp.einsum("shqk,skhd->sqhd", d_scores, key_heads, preferred_element_type=jnp.float32)
        * factor
    )
    d_keys = (
        jnp.einsum("shqk,sqhd->skhd", d_scores, queries, preferred_element_type=jnp.float32)
        * factor
    )
    d_packed = (
        jnp.stack([d_queries, d_keys, d_values], axis=2)
        .astype(jnp.bfloat16)
        .reshape(row_count, 3 * model_width)
    )
    grad_qkv = jnp.einsum("ti,tf->if", scaled, d_packed, preferred_element_type=jnp.float32)
    d_scaled = jnp.einsum("tf,if->ti", d_packed, qkv_w, preferred_element_type=jnp.float32).reshape(
        seq_count, length, model_width
    )
    d_normed = d_scaled * scale_seq
    grad_ln1_bias = jnp.sum(d_normed, axis=(0, 1))
    d_embedding = jnp.sum(d_scaled * normed, axis=1)
    grad_table = jnp.einsum(
        "sn,sd->nd", one_hot.astype(jnp.float32), d_embedding, precision=lax.Precision.HIGHEST
    )
    first_pull = jax.vjp(scaled_norm, inputs, gain_one_f)[1]
    d_in_part, grad_ln1_gain = first_pull(d_normed.reshape(row_count, model_width))
    grad_tokens = (d_middle + d_in_part).astype(jnp.bfloat16)
    return (
        block_out,
        grad_tokens,
        (grad_table, grad_ln1_gain, grad_ln1_bias, grad_qkv, grad_out_w, grad_out_b, grad_ln2_gain,
         grad_ln2_bias, grad_up, grad_up_b, grad_down, grad_down_b),
    )


def plain(*args):
    dims = (None, None, 1, 0, 0, 0, 0, 0, 0, 0, 0, 0, 0, 0, None)
    whole = [
        item if dim is None else lax.all_gather(item, "fsdp", axis=dim, tiled=True)
        for item, dim in zip(args, dims, strict=True)
    ]
    block_out, grad_tokens, grads = layer(*whole)
    shares = [
        lax.psum_scatter(grad, "fsdp", scatter_dimension=1 if place == 0 else 0, tiled=True)
        for place, grad in enumerate(grads)
    ]
    return (block_out, grad_tokens, *lax.psum(tuple(shares), "dp"))


def eight_by_four(
    tokens, time_index, time_table, ln1_gain, ln1_bias, w_qkv, w_out, b_out, ln2_gain, ln2_bias,
    w_up, b_up, w_down, b_down, cotangent,
):
    where = jnp.stack(coords()).astype(jnp.int32)
    seqs = time_index.shape[0]
    length = tokens.shape[0] // seqs
    vec = jnp.concatenate(
        [v.reshape(-1, 128) for v in (ln1_gain, ln1_bias, b_out, ln2_gain, ln2_bias, b_down, b_up)]
        + [jnp.zeros((6, 128), LOW)]
    )
    times = time_index.reshape(seqs, 1)
    token = [where]

    def then(values):
        token[0] = values[0] if isinstance(values, (list, tuple)) else values
        return values

    def after(*more):
        return (token[0], *more)

    (parts_first,) = then(
        simple(own_first_kernel, (w_qkv, w_out), [((2, 128, CW), LOW)], where=where)
    )
    small = jnp.concatenate([time_table, vec])
    small_near = swap(small, "z1")
    pieces = [Piece(parts_first, (i,), (128, CW), 1) for i in range(2)]
    near = swap(parts_first, "z1")
    for piece in pieces:
        piece.move_z1(near, piece.index)

    def tick(*jobs, extra=()):
        stages = {
            "z": ("two", "move_z2"), "y": ("four", "move_y"), "x": ("across_send", "move_x"), "c": ("core_send", "move_c"),
        }
        jobs = [(pieces[n], *stages[stage]) for stage, n in jobs]
        made = then(move([getattr(p, make)() for p, make, _ in jobs] + list(extra), after=after()))
        for (p, _, go), value in zip(jobs, made):
            getattr(p, go)(value)
        return made[len(jobs) :]

    tick(("z", 0), ("z", 1))
    parts_up, parts_down = then(
        simple(
            own_other_kernel, (w_up, w_down), [((2, 128, CW), LOW), ((2, RW, 1024), LOW)], where=where, after=after()
        )
    )
    pieces += [Piece(parts_up, (i,), (128, CW), 1) for i in range(2)]
    pieces += [Piece(parts_down, (i,), (RW, 1024), 0) for i in range(2)]
    near_up, near_down = swap(parts_up, "z1"), swap(parts_down, "z1")
    for i in range(2):
        pieces[2 + i].move_z1(near_up, (i,))
        pieces[4 + i].move_z1(near_down, (i,))
    everything = slice(None)
    owns = [
        [(w_qkv, [(everything, pl.ds(0, 2048))], [0], 2048)],
        [(w_qkv, [(everything, pl.ds(2048, 1024))], [0], 1024), (w_out, [(everything, everything)], [1024], 1024)],
    ]
    for half in range(2):
        reads = [(everything, pl.ds(s * 512 + half * 256, 256)) for s in range(8)]
        owns.append([(w_up, reads, [s * 256 for s in range(8)], 256)])
    for half in range(2):
        owns.append([(w_down, [(pl.ds(half * 256, 256), everything)], [0], 256)])

    def whole(n):
        return then(assemble(where, pieces[n], owns[n], after=after()))

    extra = [((2, 144, 128), [(small, (), 0), (small_near, (), 1)])]
    (small_two,) = tick(("y", 0), extra=extra)
    small_far = swap(small_two, "z2")
    extra = [((4, 144, 128), [(small_two, (), slice(0, 2)), (small_far, (), slice(2, 4))])]
    (small_four,) = tick(("x", 0), ("y", 1), ("z", 2), extra=extra)
    small_beside = swap(small_four, "y")
    table, vec, up_b, scale = then(small_params(where, small_four, small_beside, times, after=after()))
    gain_one, bias_one, out_b, gain_two, bias_two, down_b = (vec[i : i + 1] for i in range(6))
    scale = scale.reshape(seqs, 1, -1)
    scaled = then(first_norm(tokens, gain_one, bias_one, scale, after=after()))
    tick(("c", 0), ("x", 1), ("y", 2), ("z", 3))
    w_qk = whole(0)
    tick(("c", 1), ("x", 2), ("y", 3), ("z", 4))
    qk = then(project(scaled, w_qk, after=after()))
    vo = whole(1)
    tick(("c", 2), ("x", 3), ("y", 4), ("z", 5))
    begun = then(attend(scaled, qk, vo, length, 0, 2, after=after()))
    up_a = whole(2)
    tick(("c", 3), ("x", 4), ("y", 5))
    v, probs, mix = then(attend(scaled, qk, vo, length, 2, 2, begun, after=after()))
    tick(("c", 4), ("x", 5))
    middle, hidden = then(second_norm(mix, tokens, vo, out_b, gain_two, bias_two, after=after()))
    act_a, slope_a = then(up(hidden, up_a, up_b[0:1], after=after()))
    up_b_w = whole(3)
    tick(("c", 5))
    act_b, slope_b = then(up(hidden, up_b_w, up_b[1:2], after=after()))
    acts = (act_a, act_b)
    core_one = swap(then(tall_away(where, acts, cotangent, after=after())), "c")
    downs = [whole(4)]
    d_pre, up_sum_a = then(pull(cotangent, downs[0], slope_a, 0, after=after()))
    one = Reduction(*then(tall_mine(where, acts, cotangent, core_one, after=after())))
    downs.append(whole(5))
    d_pre, up_sum_b = then(pull(cotangent, downs[1], slope_b, 1, d_pre, after=after()))
    d_middle, d_low, d_mix, sums_two = then(
        middle_back(d_pre, (up_a, up_b_w), middle, cotangent, gain_two, vo, after=after())
    )

    def step(*jobs):
        names = {
            "second": Reduction.go_second, "third": Reduction.go_third, "fourth": Reduction.go_fourth,
            "last": Reduction.go_last,
        }
        lists = [getattr(r, stage)() for r, stage in jobs]
        made = then(add_up([item for items in lists for item in items], after=after()))
        for (r, stage), items in zip(jobs, lists, strict=True):
            values, made = made[: len(items)], made[len(items) :]
            names[stage](r, *values)

    step((one, "second"))
    pairs = [(hidden, d_pre, "layer"), (mix, d_low, "columns")]
    core_two = swap(then(row_away(where, pairs, after=after())), "c")
    begun = then(attend_back(d_mix, probs, qk, v, length, 0, 2, after=after()))
    step((one, "third"))
    two = Reduction(*then(row_mine(where, pairs, core_two, after=after())))
    d_packed = then(attend_back(d_mix, probs, qk, v, length, 2, 2, (begun,), after=after()))
    pairs = [(scaled, d_packed, "layers")]
    core_three = swap(then(row_away(where, pairs, after=after())), "c")
    grad_tokens, sums_one, d_emb = then(
        input_back(d_packed, w_qk, vo, tokens, d_middle, gain_one, bias_one, scale, after=after())
    )
    step((one, "fourth"), (two, "second"))
    three = Reduction(*then(row_mine(where, pairs, core_three, after=after())))
    (rows,) = then(
        simple(
            rows_kernel,
            (d_emb, sums_one, sums_two, up_sum_a, up_sum_b, jnp.pad(time_index.astype(F32), (0, 120))[None]),
            [((32, 24, 128), F32)],
            after=after(),
        )
    )
    got = lax.all_to_all(rows, BOTH, 0, 0)
    block_out = then(down(acts, downs, middle, down_b, after=after()))
    step((one, "last"), (two, "third"), (three, "second"))
    one.go_corner()
    (down_shard,) = then(shard_of(tall_shard_kernel, where, one, [(512, 1024)], after=after()))
    step((three, "third"))
    step((two, "fourth"))
    grad_table, sums = then(
        simple(table_kernel, (got,), [((128, 128), F32), ((16, 128), F32)], after=after())
    )
    step((two, "last"), (three, "fourth"))
    two.go_corner()
    step((three, "last"))
    three.go_corner()
    up_shard, out_shard = then(shard_of(up_shard_kernel, where, two, [(128, 4096), (128, 1024)], after=after()))
    (qkv_shard,) = then(shard_of(qkv_shard_kernel, where, three, [(128, 3072)], after=after()))
    return (
        block_out, grad_tokens, grad_table, sums[0], sums[1], qkv_shard, out_shard, sums[2], sums[3], sums[4],
        up_shard, sums[6:10].reshape(512), down_shard, sums[5],
    )


def solution(mesh):
    in_specs = (
        P(("fsdp", "dp"), None),
        P(("fsdp", "dp")),
        P(None, "fsdp"),
        P("fsdp"),
        P("fsdp"),
        P("fsdp", None),
        P("fsdp", None),
        P("fsdp"),
        P("fsdp"),
        P("fsdp"),
        P("fsdp", None),
        P("fsdp"),
        P("fsdp", None),
        P("fsdp"),
        P(("fsdp", "dp"), None),
    )
    out_specs = (
        P(("fsdp", "dp"), None),
        P(("fsdp", "dp"), None),
        P(None, "fsdp"),
        P("fsdp"),
        P("fsdp"),
        P("fsdp", None),
        P("fsdp", None),
        P("fsdp"),
        P("fsdp"),
        P("fsdp"),
        P("fsdp", None),
        P("fsdp"),
        P("fsdp", None),
        P("fsdp"),
    )
    local = eight_by_four if (mesh.shape["fsdp"], mesh.shape["dp"]) == (8, 4) else plain
    return jax.shard_map(local, mesh=mesh, in_specs=in_specs, out_specs=out_specs, check_vma=False)
```

time: 826 us -> 530 us (0.64)
  Pallas kernels: 20 us -> 214 us
  matrix products: 188 us -> 0 us
  local copies, waits for them, and re-layouts: 185 us -> 52.9 us
  other arithmetic: 117 us -> 0.08 us
  waiting for transfers between devices: 231 us -> 190 us
  starting transfers between devices: 71.3 us -> 61.3 us
    pallas_call x7 -> x51, Pallas kernels: 20 us -> 214 us  [call(): return lambda *args: run(*args, *after)]
    dot_general x20 -> x0, matrix products: 188 us -> none  [the longest x1 48.9 us: layer(): jnp.dot(hidden_in, up_w, preferred_element_type=jnp.float32)]
    convert_element_type x28 -> x1, other arithmetic: 48.1 us -> 0.01 us  [eight_by_four(): time_index.astype(F32)]
    ppermute x67 -> x60, waiting for transfers between devices: 231 us -> 188 us  [swap(): return lax.ppermute(values, BOTH, flips(which))]
    reshape x6 -> x3, local copies, waits for them, and re-layouts: 39.5 us -> 0.69 us  [the longest x1 0.58 us: eight_by_four(): sums[6:10].reshape(512)]
    convert_element_type x7 -> x0, local copies, waits for them, and re-layouts: 33.6 us -> none  [the longest x2 17.5 us: layer(): d_packed = jnp.stack([d_queries, d_keys, d_values], axis=2).astype(jnp.bf...]
    slice x13 -> x2, local copies, waits for them, and re-layouts: 24.5 us -> 0.03 us  [the longest x1 0.02 us: eight_by_four(): vec[i:i + 1]]
    concatenate x17 -> x0, other arithmetic: 20.6 us -> none  [the longest x6 11.4 us: spread(): seven = jnp.concatenate([near[None], far, beside])]
  transfers between devices with their start and end apart: 68 -> 61, of which waited for: 23 -> 27; matrix products, arithmetic and copies ran while one was open for 35% -> 0% of each run, Pallas kernels for 2% -> 28%
where the time goes in v2:
time: 530 us; the launch traced here: 521 us
  Pallas kernels  214 us (40%)
  waiting for transfers between devices  190 us (36%)
  starting transfers between devices  61.3 us (12%)
  local copies, waits for them, and re-layouts  52.9 us (10%)
    pallas_call x51, Pallas kernels, call(): return lambda *args: run(*args, *after)  214 us
    ppermute x60, waiting for transfers between devices, swap(): return lax.ppermute(values, BOTH, flips(which))  188 us
    ppermute x60, starting transfers between devices, swap(): return lax.ppermute(values, BOTH, flips(which))  55.2 us
    unnamed x240, local copies, waits for them, and re-layouts  51.5 us
  transfers between devices with their start and end apart: 61, of which 27 were waited for; matrix products, arithmetic and copies ran while one was open for 0% of the time, Pallas kernels for 28%

profile of v2, /device:TPU:1, one launch (start us, length us, event | category | flops | bytes accessed | tf_op | source)
XLA Modules:
  0.0 520.8 jit_solution(6305083741344690049)
XLA Ops:
  3.7 2.2 collective-permute-start
  5.9 7.4 %collective-permute-done.refs_1_.refs_0_.refs_2_.refs_3_ = bf16[2,128,640]{2,1,0:T(8,128)(2,1)S(1)} collective-permute-done((bf16[2,128,640]{2,1,0:T(8,128)(2,1)S(1)}, bf16[2,128,640]{2,1,0:T(8,128)(2,1)S(1)}, u32[]{:S(2)}, u32[]{:S(2)}) %collective-permute-start) | collective-permute-done | bytes 327712 | tf_op jit(solution)/shard_map/ppermute | solution.py:38
  19.3 4.3 collective-permute-done.2.refs_4_
  23.6 8.1 %collective-permute-done.1.refs_2_.refs_1_.refs_3_ = bf16[2,128,640]{2,1,0:T(8,128)(2,1)S(1)} collective-permute-done((bf16[2,128,640]{2,1,0:T(8,128)(2,1)}, bf16[2,128,640]{2,1,0:T(8,128)(2,1)S(1)}, u32[]{:S(2)}, u32[]{:S(2)}) %collective-permute-start.1) | collective-permute-done | bytes 327712 | tf_op jit(solution)/shard_map/ppermute | solution.py:38
  34.4 3.0 collective-permute-start.4
  37.4 9.7 %collective-permute-done.5.refs_6_.refs_7_.refs_4_.refs_0_.refs_2_ = bf16[2,128,640]{2,1,0:T(8,128)(2,1)S(1)} collective-permute-done((bf16[2,128,640]{2,1,0:T(8,128)(2,1)S(1)}, bf16[2,128,640]{2,1,0:T(8,128)(2,1)S(1)}, u32[]{:S(2)}, u32[]{:S(2)}) %collective-permute-start.5) | collective-permute-done | bytes 327712 | tf_op jit(solution)/shard_map/ppermute | solution.py:38
  47.7 6.9 %collective-permute-done.6.refs_8_ = bf16[2,144,128]{2,1,0:T(8,128)(2,1)S(1)} collective-permute-done((bf16[2,144,128]{2,1,0:T(8,128)(2,1)S(1)}, bf16[2,144,128]{2,1,0:T(8,128)(2,1)S(1)}, u32[]{:S(2)}, u32[]{:S(2)}) %collective-permute-start.6) | collective-permute-done | bytes 73760 | tf_op jit(solution)/shard_map/ppermute | solution.py:38
  58.8 16.2 %collective-permute-done.7.refs_2_ = bf16[4,144,128]{2,1,0:T(8,128)(2,1)} collective-permute-done((bf16[4,144,128]{2,1,0:T(8,128)(2,1)}, bf16[4,144,128]{2,1,0:T(8,128)(2,1)}, u32[]{:S(2)}, u32[]{:S(2)}) %collective-permute-start.7) | collective-permute-done | bytes 147488 | tf_op jit(solution)/shard_map/ppermute | solution.py:38
  76.9 2.3 shard_map.260.refs_9_.refs_0_.refs_1_
  79.3 2.3 shard_map.261
  81.6 2.9 collective-permute-start.15
  85.0 2.4 collective-permute-start.13
  90.1 10.4 %collective-permute-done.14.refs_10_.refs_7_.refs_4_.refs_0_.refs_2_ = bf16[2,80,1024]{2,1,0:T(8,128)(2,1)S(1)} collective-permute-done((bf16[2,80,1024]{2,1,0:T(8,128)(2,1)S(1)}, bf16[2,80,1024]{2,1,0:T(8,128)(2,1)S(1)}, u32[]{:S(2)}, u32[]{:S(2)}) %collective-permute-start.14) | collective-permute-done | bytes 327712 | tf_op jit(solution)/shard_map/ppermute | solution.py:38
  107.0 5.6 %shard_map.264.refs_8_.refs_2_.refs_3_ = bf16[1024,2048]{1,0:T(8,128)(2,1)S(1)} custom-call(bf16[1024,1024]{1,0:T(8,128)(2,1)S(1)} %shard_map.260.refs_9_.refs_0_.refs_1_, bf16[1024,2048]{1,0:T(8,128)(2,1)S(1)} %shard_map.262.refs_11_.refs_1_.refs_2_, bf16[7,128,1024]{2,1,0:T(8,128)(2,1)S(1)} %get-tuple-element.112.refs_2_), custom_call_target="tpu_custom_call" | custom-call | bytes 1024 | tf_op jit(solution)/shard_map/pallas_call | solution.py:76
  114.3 10.0 %collective-permute-done.19.refs_8_.refs_5_.refs_1_.refs_3_ = bf16[2,80,1024]{2,1,0:T(8,128)(2,1)S(1)} collective-permute-done((bf16[2,80,1024]{2,1,0:T(8,128)(2,1)S(1)}, bf16[2,80,1024]{2,1,0:T(8,128)(2,1)S(1)}, u32[]{:S(2)}, u32[]{:S(2)}) %collective-permute-start.19) | collective-permute-done | bytes 327712 | tf_op jit(solution)/shard_map/ppermute | solution.py:38
  126.7 5.1 shard_map.267
  133.9 9.5 %collective-permute-done.22.refs_8_.refs_4_.refs_1_.refs_3_ = bf16[2,80,1024]{2,1,0:T(8,128)(2,1)S(1)} collective-permute-done((bf16[2,80,1024]{2,1,0:T(8,128)(2,1)S(1)}, bf16[2,80,1024]{2,1,0:T(8,128)(2,1)S(1)}, u32[]{:S(2)}, u32[]{:S(2)}) %collective-permute-start.22) | collective-permute-done | bytes 327712 | tf_op jit(solution)/shard_map/ppermute | solution.py:38
  147.5 5.5 %shard_map.270 = (bf16[1024,1024]{1,0:T(8,128)(2,1)S(1)}, bf16[4,8,2,256,128]{4,3,2,1,0:T(8,128)(2,1)S(1)}, bf16[1024,1024]{1,0:T(8,128)(2,1)S(1)}) custom-call(bf16[1024,1024]{1,0:T(8,128)(2,1)S(1)} %shard_map.260.refs_9_.refs_0_.refs_1_, ...), custom_call_target="tpu_custom_call", output_to_operand_aliasing={{0}: (4, {}), {1}: (5, {}), {2}: (6, {})} | custom-call | bytes 1024 | tf_op jit(solution)/shard_map/pallas_call | solution.py:76
  155.1 7.3 %collective-permute-done.25.refs_5_.refs_2_.refs_4_ = bf16[4,80,1024]{2,1,0:T(8,128)(2,1)S(1)} collective-permute-done((bf16[4,80,1024]{2,1,0:T(8,128)(2,1)S(1)}, bf16[4,80,1024]{2,1,0:T(8,128)(2,1)S(1)}, u32[]{:S(2)}, u32[]{:S(2)}) %collective-permute-start.25) | collective-permute-done | bytes 655392 | tf_op jit(solution)/shard_map/ppermute | solution.py:38
  164.2 4.2 shard_map.272
  168.4 8.8 %shard_map.273 = (bf16[1024,2048]{1,0:T(8,128)(2,1)S(1)}, bf16[1024,2048]{1,0:T(8,128)(2,1)S(1)}) custom-call(bf16[1024,1024]{1,0:T(8,128)(2,1)S(1)} %get-tuple-element.129.refs_0_.refs_1_, bf16[1024,2048]{1,0:T(8,128)(2,1)S(1)} %shard_map.268.refs_9_.refs_1_, f32[1,2048]{1,0:T(1,128)S(1)} %get-tuple-element.183.refs_2_, ...), custom_call_target="tpu_custom_call" | custom-call | bytes 1024 | tf_op jit(solution)/shard_map/pallas_call | solution.py:76
  177.2 4.0 shard_map.274.refs_4_.refs_1_.refs_2_
  183.4 8.8 %shard_map.276 = (bf16[1024,2048]{1,0:T(8,128)(2,1)S(1)}, bf16[1024,2048]{1,0:T(8,128)(2,1)S(1)}) custom-call(bf16[1024,1024]{1,0:T(8,128)(2,1)S(1)} %get-tuple-element.129.refs_0_.refs_1_, bf16[1024,2048]{1,0:T(8,128)(2,1)S(1)} %shard_map.274.refs_4_.refs_1_.refs_2_, f32[1,2048]{1,0:T(1,128)S(1)} %get-tuple-element.182.refs_2_, ...), custom_call_target="tpu_custom_call" | custom-call | bytes 1024 | tf_op jit(solution)/shard_map/pallas_call | solution.py:76
  192.2 8.3 %shard_map.277.refs_7_ = bf16[2,2,4,2,128,512]{5,4,3,2,1,0:T(8,128)(2,1)S(1)} custom-call(s32[4]{0:T(128)S(1)} %pad_add_fusion.refs_0_, bf16[1024,2048]{1,0:T(8,128)(2,1)S(1)} %get-tuple-element.132.refs_7_.refs_1_.refs_0_, bf16[1024,2048]{1,0:T(8,128)(2,1)S(1)} %get-tuple-element.134.refs_2_.refs_4_.refs_1_, bf16[1024,1024]{1,0:T(8,128)(2,1)S(1)} %copy-done.22, ...), custom_call_target="tpu_custom_call" | custom-call | bytes 1024 | tf_op jit(solution)/shard_map/pallas_call | solution.py:76
  202.2 8.8 %collective-permute-done.28.refs_6_ = bf16[7,128,1024]{2,1,0:T(8,128)(2,1)S(1)} collective-permute-done((bf16[7,128,1024]{2,1,0:T(8,128)(2,1)S(1)}, bf16[7,128,1024]{2,1,0:T(8,128)(2,1)S(1)}, u32[]{:S(2)}, u32[]{:S(2)}) %collective-permute-start.28) | collective-permute-done | bytes 1835040 | tf_op jit(solution)/shard_map/ppermute | solution.py:38
  211.0 5.9 %shard_map.278.refs_1_.refs_3_.refs_2_ = bf16[2048,1024]{1,0:T(8,128)(2,1)S(1)} custom-call(s32[4]{0:T(128)S(1)} %pad_add_fusion.refs_0_, bf16[512,1024]{1,0:T(8,128)(2,1)S(1)} %copy-done.41, bf16[2,80,1024]{2,1,0:T(8,128)(2,1)S(1)} %collective-permute-done.14.refs_10_.refs_7_.refs_4_.refs_0_.refs_2_, bf16[2,80,1024]{2,1,0:T(8,128)(2,1)S(1)} %copy-done.65, ...), custom_call_target="tpu_custom_call" | custom-call | bytes 1024 | tf_op jit(solution)/shard_map/pallas_call | solution.py:76
  216.9 6.2 %shard_map.279 = (bf16[2,1024,2048]{2,1,0:T(8,128)(2,1)S(1)}, f32[1,2048]{1,0:T(1,128)S(1)}) custom-call(bf16[1024,1024]{1,0:T(8,128)(2,1)S(1)} %copy-done.22, bf16[2048,1024]{1,0:T(8,128)(2,1)S(1)} %shard_map.278.refs_1_.refs_3_.refs_2_, bf16[1024,2048]{1,0:T(8,128)(2,1)S(1)} %copy-done.80, bf16[2048,1024]{1,0:T(8,128)(2,1)S(1)} %shard_map.278.refs_1_.refs_3_.refs_2_), custom_call_target="tpu_custom_call" | custom-call | bytes 1024 | tf_op jit(solution)/shard_map/pallas_call | solution.py:76
  223.2 11.0 %shard_map.280 = (bf16[2,2,2,128,512]{4,3,2,1,0:T(8,128)(2,1)}, bf16[2,2,2,128,512]{4,3,2,1,0:T(8,128)(2,1)}, bf16[2,2,2,128,512]{4,3,2,1,0:T(8,128)(2,1)S(1)}, bf16[2,2,2,128,512]{4,3,2,1,0:T(8,128)(2,1)S(1)}) custom-call(s32[4]{0:T(128)S(1)} %pad_add_fusion.refs_0_, bf16[1024,2048]{1,0:T(8,128)(2,1)S(1)} %get-tuple-element.132.refs_7_.refs_1_.refs_0_, ...), custom_call_target="tpu_custom_call" | custom-call | bytes 1024 | tf_op jit(solution)/shard_map/pallas_call | solution.py:76
  235.8 6.0 %shard_map.281.refs_1_.refs_4_.refs_3_ = bf16[2048,1024]{1,0:T(8,128)(2,1)S(1)} custom-call(s32[4]{0:T(128)S(1)} %pad_add_fusion.refs_0_, bf16[512,1024]{1,0:T(8,128)(2,1)S(1)} %copy-done.41, bf16[2,80,1024]{2,1,0:T(8,128)(2,1)S(1)} %collective-permute-done.14.refs_10_.refs_7_.refs_4_.refs_0_.refs_2_, ...), custom_call_target="tpu_custom_call" | custom-call | bytes 1024 | tf_op jit(solution)/shard_map/pallas_call | solution.py:76
  241.9 6.2 %shard_map.282 = (bf16[2,1024,2048]{2,1,0:T(8,128)(2,1)S(1)}, f32[1,2048]{1,0:T(1,128)S(1)}) custom-call(bf16[1024,1024]{1,0:T(8,128)(2,1)S(1)} %copy-done.22, bf16[2048,1024]{1,0:T(8,128)(2,1)S(1)} %shard_map.281.refs_1_.refs_4_.refs_3_, bf16[1024,2048]{1,0:T(8,128)(2,1)S(1)} %copy-done.82, ...), custom_call_target="tpu_custom_call", output_to_operand_aliasing={{0}: (3, {})} | custom-call | bytes 1024 | tf_op jit(solution)/shard_map/pallas_call | solution.py:76
  248.2 3.3 copy-done
  251.5 2.2 copy-done.12
  255.9 17.4 %shard_map.283 = (f32[1024,1024]{1,0:T(8,128)S(1)}, bf16[1024,1024]{1,0:T(8,128)(2,1)S(1)}, bf16[1024,1024]{1,0:T(8,128)(2,1)S(1)}, f32[8,1024]{1,0:T(8,128)S(1)}) custom-call(bf16[2,1024,2048]{2,1,0:T(8,128)(2,1)} %copy-done, bf16[1024,2048]{1,0:T(8,128)(2,1)S(1)} %copy-done.16, bf16[1024,2048]{1,0:T(8,128)(2,1)S(1)} %copy-done.12, ...), custom_call_target="tpu_custom_call" | custom-call | bytes 1024 | tf_op jit(solution)/shard_map/pallas_call | solution.py:76
  273.9 2.4 shard_map.284
  278.5 2.5 copy-done.1
  281.1 8.5 %shard_map.285.refs_5_ = bf16[2,2,4,64,2560]{4,3,2,1,0:T(8,128)(2,1)S(1)} custom-call(s32[4]{0:T(128)S(1)} %pad_add_fusion.refs_0_, bf16[1024,1024]{1,0:T(8,128)(2,1)S(1)} %copy-done.31, bf16[1024,1024]{1,0:T(8,128)(2,1)S(1)} %copy-done.33, bf16[2,1024,2048]{2,1,0:T(8,128)(2,1)S(1)} %copy-done.1, bf16[1024,1024]{1,0:T(8,128)(2,1)S(1)} %get-tuple-element.142.refs_4_, ...), custom_call_target="tpu_custom_call" | custom-call | bytes 1024 | tf_op jit(solution)/shard_map/pallas_call | solution.py:76
  291.4 5.8 %shard_map.286.refs_3_.refs_5_ = bf16[3,1024,1024]{2,1,0:T(8,128)(2,1)S(1)} custom-call(bf16[1024,1024]{1,0:T(8,128)(2,1)S(1)} %copy-done.52, bf16[4,8,2,256,128]{4,3,2,1,0:T(8,128)(2,1)S(1)} %copy-done.29, bf16[1024,2048]{1,0:T(8,128)(2,1)S(1)} %shard_map.264.refs_8_.refs_2_.refs_3_, bf16[1024,2048]{1,0:T(8,128)(2,1)S(1)} %shard_map.264.refs_8_.refs_2_.refs_3_, ...), custom_call_target="tpu_custom_call" | custom-call | bytes 1024 | tf_op jit(solution)/shard_map/pallas_call | solution.py:76
  297.3 6.6 %collective-permute-done.34.refs_2_ = bf16[2,2,128,512]{3,2,1,0:T(8,128)(2,1)S(1)} collective-permute-done((bf16[2,2,128,512]{3,2,1,0:T(8,128)(2,1)S(1)}, bf16[2,2,128,512]{3,2,1,0:T(8,128)(2,1)S(1)}, u32[]{:S(2)}, u32[]{:S(2)}) %collective-permute-start.34) | collective-permute-done | bytes 524320 | tf_op jit(solution)/shard_map/ppermute | solution.py:38
  304.1 2.3 copy-done.77
  306.4 3.4 copy-done.2
  311.4 2.5 copy-done.78
  313.8 9.4 %shard_map.288 = (bf16[2,2,64,2560]{3,2,1,0:T(8,128)(2,1)S(1)}, bf16[2,2,64,2560]{3,2,1,0:T(8,128)(2,1)S(1)}, bf16[2,2,64,2560]{3,2,1,0:T(8,128)(2,1)S(1)}, bf16[2,2,64,2560]{3,2,1,0:T(8,128)(2,1)S(1)}) custom-call(s32[4]{0:T(128)S(1)} %pad_add_fusion.refs_0_, bf16[1024,1024]{1,0:T(8,128)(2,1)S(1)} %copy-done.31, bf16[1024,1024]{1,0:T(8,128)(2,1)S(1)} %copy-done.34, ...), custom_call_target="tpu_custom_call" | custom-call | bytes 1024 | tf_op jit(solution)/shard_map/pallas_call | solution.py:76
  326.4 5.8 %shard_map.289.refs_2_.refs_3_.refs_0_ = bf16[3,1024,1024]{2,1,0:T(8,128)(2,1)S(1)} custom-call(bf16[1024,1024]{1,0:T(8,128)(2,1)S(1)} %copy-done.53, bf16[4,8,2,256,128]{4,3,2,1,0:T(8,128)(2,1)S(1)} %copy-done.29, bf16[1024,2048]{1,0:T(8,128)(2,1)S(1)} %shard_map.264.refs_8_.refs_2_.refs_3_, ...), custom_call_target="tpu_custom_call", output_to_operand_aliasing={{}: (5, {})} | custom-call | bytes 1024 | tf_op jit(solution)/shard_map/pallas_call | solution.py:76
  332.3 5.2 %shard_map.290.refs_9_ = bf16[2,2,4,64,1536]{4,3,2,1,0:T(8,128)(2,1)S(1)} custom-call(s32[4]{0:T(128)S(1)} %pad_add_fusion.refs_0_, bf16[1024,1024]{1,0:T(8,128)(2,1)S(1)} %copy-done.8, bf16[3,1024,1024]{2,1,0:T(8,128)(2,1)S(1)} %shard_map.289.refs_2_.refs_3_.refs_0_, bf16[3,1024,1024]{2,1,0:T(8,128)(2,1)S(1)} %shard_map.289.refs_2_.refs_3_.refs_0_), custom_call_target="tpu_custom_call" | custom-call | bytes 1024 | tf_op jit(solution)/shard_map/pallas_call | solution.py:76
  341.0 11.7 %shard_map.291 = (bf16[1024,1024]{1,0:T(8,128)(2,1)}, f32[8,1024]{1,0:T(8,128)S(1)}, f32[8,1,1024]{2,1,0:T(1,128)S(1)}) custom-call(bf16[3,1024,1024]{2,1,0:T(8,128)(2,1)S(1)} %shard_map.289.refs_2_.refs_3_.refs_0_, bf16[1024,2048]{1,0:T(8,128)(2,1)S(1)} %copy-done.6, bf16[1024,2048]{1,0:T(8,128)(2,1)S(1)} %copy-done.6, bf16[1024,2048]{1,0:T(8,128)(2,1)S(1)} %copy-done.4, ...), custom_call_target="tpu_custom_call" | custom-call | bytes 1024 | tf_op jit(solution)/shard_map/pallas_call | solution.py:76
  352.8 28.0 %collective-permute-done.36.refs_2_ = bf16[2,2,128,512]{3,2,1,0:T(8,128)(2,1)S(1)} collective-permute-done((bf16[2,2,128,512]{3,2,1,0:T(8,128)(2,1)S(1)}, bf16[2,2,128,512]{3,2,1,0:T(8,128)(2,1)S(1)}, u32[]{:S(2)}, u32[]{:S(2)}) %collective-permute-start.36) | collective-permute-done | bytes 524320 | tf_op jit(solution)/shard_map/ppermute | solution.py:38
  382.9 2.6 shard_map.292
  385.5 7.8 %shard_map.293 = (bf16[2,2,64,1536]{3,2,1,0:T(8,128)(2,1)S(1)}, bf16[2,2,64,1536]{3,2,1,0:T(8,128)(2,1)}, bf16[2,2,64,1536]{3,2,1,0:T(8,128)(2,1)S(1)}, bf16[2,2,64,1536]{3,2,1,0:T(8,128)(2,1)S(1)}) custom-call(s32[4]{0:T(128)S(1)} %pad_add_fusion.refs_0_, bf16[1024,1024]{1,0:T(8,128)(2,1)S(1)} %copy-done.8, ...), custom_call_target="tpu_custom_call" | custom-call | bytes 1024 | tf_op jit(solution)/shard_map/pallas_call | solution.py:76
  399.3 2.2 copy-done.27
  401.5 10.5 %shard_map.295.refs_12_ = bf16[1024,1024]{1,0:T(8,128)(2,1)} custom-call(bf16[1024,2048]{1,0:T(8,128)(2,1)S(1)} %copy-done.14, bf16[1024,2048]{1,0:T(8,128)(2,1)S(1)} %copy-done.19, bf16[2048,1024]{1,0:T(8,128)(2,1)S(1)} %copy-done.10, bf16[2048,1024]{1,0:T(8,128)(2,1)S(1)} %copy-done.21, f32[1024,1024]{1,0:T(8,128)S(1)} %copy-done.27, ...), custom_call_target="tpu_custom_call" | custom-call | bytes 1024 | tf_op jit(solution)/shard_map/pallas_call | solution.py:76
  412.0 13.2 %collective-permute-done.42.refs_7_ = bf16[2,64,2560]{2,1,0:T(8,128)(2,1)S(1)} collective-permute-done((bf16[2,64,2560]{2,1,0:T(8,128)(2,1)}, bf16[2,64,2560]{2,1,0:T(8,128)(2,1)S(1)}, u32[]{:S(2)}, u32[]{:S(2)}) %collective-permute-start.42) | collective-permute-done | bytes 655392 | tf_op jit(solution)/shard_map/ppermute | solution.py:38
  427.4 2.5 shard_map.296
  432.1 6.1 %all-to-all-start = ((f32[32,24,128]{2,1,0:T(8,128)}), f32[32,24,128]{2,1,0:T(8,128)}, u32[]{:S(2)}, u32[]{:S(2)}) async-start(f32[32,24,128]{2,1,0:T(8,128)} %shard_map.294.refs_6_), calls=%async_computation | async-start | bytes 786432 | tf_op jit(solution)/shard_map/all_to_all | solution.py:1259
  438.7 3.7 collective-permute-start.49
  443.7 3.0 shard_map.297.refs_3_
  452.5 2.6 collective-permute-start.51
  455.1 19.8 %collective-permute-done.45.refs_3_ = bf16[2,64,2560]{2,1,0:T(8,128)(2,1)} collective-permute-done((bf16[2,64,2560]{2,1,0:T(8,128)(2,1)}, bf16[2,64,2560]{2,1,0:T(8,128)(2,1)}, u32[]{:S(2)}, u32[]{:S(2)}) %collective-permute-start.45) | collective-permute-done | bytes 655392 | tf_op jit(solution)/shard_map/ppermute | solution.py:38
  476.9 2.2 all-to-all-done.refs_0_
  479.1 3.4 shard_map.300
  482.5 5.1 collective-permute-done.51.refs_8_.refs_3_
  487.6 7.0 %collective-permute-done.52.refs_4_ = bf16[64,2560]{1,0:T(8,128)(2,1)} collective-permute-done((bf16[64,2560]{1,0:T(8,128)(2,1)}, bf16[64,2560]{1,0:T(8,128)(2,1)}, u32[]{:S(2)}, u32[]{:S(2)}) %collective-permute-start.52) | collective-permute-done | bytes 327712 | tf_op jit(solution)/shard_map/ppermute | solution.py:38
  500.6 4.9 collective-permute-done.53.refs_4_
  511.3 2.8 collective-permute-start.56
  514.7 2.2 shard_map.303
  (360 shorter events, 100.2 us)
Async XLA Ops:
  3.7 9.6 %collective-permute-start = (bf16[2,128,640]{2,1,0:T(8,128)(2,1)S(1)}, bf16[2,128,640]{2,1,0:T(8,128)(2,1)S(1)}, u32[]{:S(2)}, u32[]{:S(2)}) collective-permute-start(bf16[2,128,640]{2,1,0:T(8,128)(2,1)S(1)} %shard_map.254.refs_0_.refs_2_.refs_3_), channel_id=1, source_target_pairs={{0,8},{1,9},{2,10},{3,11},{4,12},{5,13},{6,14},{7,15},{8,0},{9,1},... | collective-permute-start | bytes 983048 | tf_op jit(solution)/shard_map/ppermute | solution.py:38
  14.9 16.8 %collective-permute-start.1 = (bf16[2,128,640]{2,1,0:T(8,128)(2,1)}, bf16[2,128,640]{2,1,0:T(8,128)(2,1)S(1)}, u32[]{:S(2)}, u32[]{:S(2)}) collective-permute-start(bf16[2,128,640]{2,1,0:T(8,128)(2,1)} %get-tuple-element.95.refs_3_), channel_id=1, source_target_pairs={{0,16},{1,17},{2,18},{3,19},{4,20},{5,21},{6,22},{7,23},{8,24},{9,... | collective-permute-start | bytes 983048 | tf_op jit(solution)/shard_map/ppermute | solution.py:38
  17.2 6.3 %collective-permute-start.2 = (bf16[144,128]{1,0:T(8,128)(2,1)S(1)}, bf16[144,128]{1,0:T(8,128)(2,1)S(1)}, u32[]{:S(2)}, u32[]{:S(2)}) collective-permute-start(bf16[144,128]{1,0:T(8,128)(2,1)S(1)} %concatenate.3.refs_3_), channel_id=1, source_target_pairs={{0,8},{1,9},{2,10},{3,11},{4,12},{5,13},{6,14},{7,15},{8,0},{9,1},... | collective-permute-start | bytes 110600 | tf_op jit(solution)/shard_map/ppermute | solution.py:38
  31.8 22.8 %collective-permute-start.3 = (bf16[4,128,640]{2,1,0:T(8,128)(2,1)S(1)}, bf16[4,128,640]{2,1,0:T(8,128)(2,1)S(1)}, u32[]{:S(2)}, u32[]{:S(2)}) collective-permute-start(bf16[4,128,640]{2,1,0:T(8,128)(2,1)S(1)} %get-tuple-element.97.refs_9_), channel_id=1, source_target_pairs={{0,4},{1,5},{2,6},{3,7},{4,0},{5,1},{6,2},{7,3},{8,12},{9,13},{10,... | collective-permute-start | bytes 1966088 | tf_op jit(solution)/shard_map/ppermute | solution.py:38
  32.8 14.4 %collective-permute-start.5 = (bf16[2,128,640]{2,1,0:T(8,128)(2,1)S(1)}, bf16[2,128,640]{2,1,0:T(8,128)(2,1)S(1)}, u32[]{:S(2)}, u32[]{:S(2)}) collective-permute-start(bf16[2,128,640]{2,1,0:T(8,128)(2,1)S(1)} %get-tuple-element.96.refs_5_.refs_6_.refs_7_), channel_id=1, source_target_pairs={{0,8},{1,9},{2,10},{3,11},{4,12},{5,13},{6,14},{7,15},{8,0},{9,1},... | collective-permute-start | bytes 983048 | tf_op jit(solution)/shard_map/ppermute | solution.py:38
  34.4 13.3 %collective-permute-start.4 = (bf16[2,128,640]{2,1,0:T(8,128)(2,1)S(1)}, bf16[2,128,640]{2,1,0:T(8,128)(2,1)S(1)}, u32[]{:S(2)}, u32[]{:S(2)}) collective-permute-start(bf16[2,128,640]{2,1,0:T(8,128)(2,1)S(1)} %copy-done.110), channel_id=1, source_target_pairs={{0,16},{1,17},{2,18},{3,19},{4,20},{5,21},{6,22},{7,23},{8,24},{9,... | collective-permute-start | bytes 983048 | tf_op jit(solution)/shard_map/ppermute | solution.py:38
  37.3 17.3 %collective-permute-start.6 = (bf16[2,144,128]{2,1,0:T(8,128)(2,1)S(1)}, bf16[2,144,128]{2,1,0:T(8,128)(2,1)S(1)}, u32[]{:S(2)}, u32[]{:S(2)}) collective-permute-start(bf16[2,144,128]{2,1,0:T(8,128)(2,1)S(1)} %get-tuple-element.99.refs_7_), channel_id=1, source_target_pairs={{0,16},{1,17},{2,18},{3,19},{4,20},{5,21},{6,22},{7,23},{8,24},{9,... | collective-permute-start | bytes 221192 | tf_op jit(solution)/shard_map/ppermute | solution.py:38
  56.0 23.2 %collective-permute-start.9 = (bf16[7,128,384]{2,1,0:T(8,128)(2,1)}, bf16[7,128,384]{2,1,0:T(8,128)(2,1)}, u32[]{:S(2)}, u32[]{:S(2)}) collective-permute-start(bf16[7,128,384]{2,1,0:T(8,128)(2,1)} %get-tuple-element.101.refs_4_), channel_id=1, source_target_pairs={{0,2},{1,3},{2,0},{3,1},{4,6},{5,7},{6,4},{7,5},{8,10},{9,11},{10,... | collective-permute-start | bytes 2064392 | tf_op jit(solution)/shard_map/ppermute | solution.py:38
  57.3 22.0 %collective-permute-start.8 = (bf16[4,128,640]{2,1,0:T(8,128)(2,1)}, bf16[4,128,640]{2,1,0:T(8,128)(2,1)S(1)}, u32[]{:S(2)}, u32[]{:S(2)}) collective-permute-start(bf16[4,128,640]{2,1,0:T(8,128)(2,1)} %get-tuple-element.105), channel_id=1, source_target_pairs={{0,4},{1,5},{2,6},{3,7},{4,0},{5,1},{6,2},{7,3},{8,12},{9,13},{10,... | collective-permute-start | bytes 1966088 | tf_op jit(solution)/shard_map/ppermute | solution.py:38
  57.5 17.6 %collective-permute-start.7 = (bf16[4,144,128]{2,1,0:T(8,128)(2,1)}, bf16[4,144,128]{2,1,0:T(8,128)(2,1)}, u32[]{:S(2)}, u32[]{:S(2)}) collective-permute-start(bf16[4,144,128]{2,1,0:T(8,128)(2,1)} %get-tuple-element.100.refs_1_), channel_id=1, source_target_pairs={{0,4},{1,5},{2,6},{3,7},{4,0},{5,1},{6,2},{7,3},{8,12},{9,13},{10,... | collective-permute-start | bytes 442376 | tf_op jit(solution)/shard_map/ppermute | solution.py:38
  58.7 20.5 %collective-permute-start.10 = (bf16[2,128,640]{2,1,0:T(8,128)(2,1)}, bf16[2,128,640]{2,1,0:T(8,128)(2,1)}, u32[]{:S(2)}, u32[]{:S(2)}) collective-permute-start(bf16[2,128,640]{2,1,0:T(8,128)(2,1)} %get-tuple-element.106), channel_id=1, source_target_pairs={{0,16},{1,17},{2,18},{3,19},{4,20},{5,21},{6,22},{7,23},{8,24},{9,... | collective-permute-start | bytes 983048 | tf_op jit(solution)/shard_map/ppermute | solution.py:38
  79.2 68.3 %copy-start.7 = (bf16[1024,1024]{1,0:T(8,128)(2,1)}, bf16[1024,1024]{1,0:T(8,128)(2,1)S(1)}, u32[]{:S(2)}) copy-start(bf16[1024,1024]{1,0:T(8,128)(2,1)S(1)} %shard_map.260.refs_9_.refs_0_.refs_1_) | copy-start | bytes 6291460
  81.6 6.3 %collective-permute-start.15 = (bf16[7,128,1024]{2,1,0:T(8,128)(2,1)S(1)}, bf16[7,128,1024]{2,1,0:T(8,128)(2,1)S(1)}, u32[]{:S(2)}, u32[]{:S(2)}) collective-permute-start(bf16[7,128,1024]{2,1,0:T(8,128)(2,1)S(1)} %get-tuple-element.111.refs_7_), channel_id=1, source_target_pairs={{0,1},{1,0},{2,3},{3,2},{4,5},{5,4},{6,7},{7,6},{8,9},{9,8},{10,11... | collective-permute-start | bytes 5505032 | tf_op jit(solution)/shard_map/ppermute | solution.py:38
  84.5 17.0 %collective-permute-start.11 = (bf16[7,128,384]{2,1,0:T(8,128)(2,1)S(1)}, bf16[7,128,384]{2,1,0:T(8,128)(2,1)S(1)}, u32[]{:S(2)}, u32[]{:S(2)}) collective-permute-start(bf16[7,128,384]{2,1,0:T(8,128)(2,1)S(1)} %get-tuple-element.107), channel_id=1, source_target_pairs={{0,2},{1,3},{2,0},{3,1},{4,6},{5,7},{6,4},{7,5},{8,10},{9,11},{10,... | collective-permute-start | bytes 2064392 | tf_op jit(solution)/shard_map/ppermute | solution.py:38
  84.8 16.0 %collective-permute-start.12 = (bf16[4,128,640]{2,1,0:T(8,128)(2,1)S(1)}, bf16[4,128,640]{2,1,0:T(8,128)(2,1)S(1)}, u32[]{:S(2)}, u32[]{:S(2)}) collective-permute-start(bf16[4,128,640]{2,1,0:T(8,128)(2,1)S(1)} %get-tuple-element.108), channel_id=1, source_target_pairs={{0,4},{1,5},{2,6},{3,7},{4,0},{5,1},{6,2},{7,3},{8,12},{9,13},{10,... | collective-permute-start | bytes 1966088 | tf_op jit(solution)/shard_map/ppermute | solution.py:38
  85.0 15.5 %collective-permute-start.14 = (bf16[2,80,1024]{2,1,0:T(8,128)(2,1)S(1)}, bf16[2,80,1024]{2,1,0:T(8,128)(2,1)S(1)}, u32[]{:S(2)}, u32[]{:S(2)}) collective-permute-start(bf16[2,80,1024]{2,1,0:T(8,128)(2,1)S(1)} %copy-done.92), channel_id=1, source_target_pairs={{0,8},{1,9},{2,10},{3,11},{4,12},{5,13},{6,14},{7,15},{8,0},{9,1},... | collective-permute-start | bytes 983048 | tf_op jit(solution)/shard_map/ppermute | solution.py:38
  85.0 15.5 %collective-permute-start.13 = (bf16[2,128,640]{2,1,0:T(8,128)(2,1)S(1)}, bf16[2,128,640]{2,1,0:T(8,128)(2,1)S(1)}, u32[]{:S(2)}, u32[]{:S(2)}) collective-permute-start(bf16[2,128,640]{2,1,0:T(8,128)(2,1)S(1)} %get-tuple-element.109), channel_id=1, source_target_pairs={{0,16},{1,17},{2,18},{3,19},{4,20},{5,21},{6,22},{7,23},{8,24},{9,... | collective-permute-start | bytes 983048 | tf_op jit(solution)/shard_map/ppermute | solution.py:38
  102.8 9.8 %collective-permute-start.16 = (bf16[7,128,1024]{2,1,0:T(8,128)(2,1)S(1)}, bf16[7,128,1024]{2,1,0:T(8,128)(2,1)S(1)}, u32[]{:S(2)}, u32[]{:S(2)}) collective-permute-start(bf16[7,128,1024]{2,1,0:T(8,128)(2,1)S(1)} %get-tuple-element.112.refs_2_), channel_id=1, source_target_pairs={{0,1},{1,0},{2,3},{3,2},{4,5},{5,4},{6,7},{7,6},{8,9},{9,8},{10,11... | collective-permute-start | bytes 5505032 | tf_op jit(solution)/shard_map/ppermute | solution.py:38
  104.4 19.8 %collective-permute-start.17 = (bf16[7,128,384]{2,1,0:T(8,128)(2,1)S(1)}, bf16[7,128,384]{2,1,0:T(8,128)(2,1)S(1)}, u32[]{:S(2)}, u32[]{:S(2)}) collective-permute-start(bf16[7,128,384]{2,1,0:T(8,128)(2,1)S(1)} %get-tuple-element.113), channel_id=1, source_target_pairs={{0,2},{1,3},{2,0},{3,1},{4,6},{5,7},{6,4},{7,5},{8,10},{9,11},{10,... | collective-permute-start | bytes 2064392 | tf_op jit(solution)/shard_map/ppermute | solution.py:38
  105.7 18.6 %collective-permute-start.18 = (bf16[4,128,640]{2,1,0:T(8,128)(2,1)S(1)}, bf16[4,128,640]{2,1,0:T(8,128)(2,1)S(1)}, u32[]{:S(2)}, u32[]{:S(2)}) collective-permute-start(bf16[4,128,640]{2,1,0:T(8,128)(2,1)S(1)} %get-tuple-element.114), channel_id=1, source_target_pairs={{0,4},{1,5},{2,6},{3,7},{4,0},{5,1},{6,2},{7,3},{8,12},{9,13},{10,... | collective-permute-start | bytes 1966088 | tf_op jit(solution)/shard_map/ppermute | solution.py:38
  106.9 17.3 %collective-permute-start.19 = (bf16[2,80,1024]{2,1,0:T(8,128)(2,1)S(1)}, bf16[2,80,1024]{2,1,0:T(8,128)(2,1)S(1)}, u32[]{:S(2)}, u32[]{:S(2)}) collective-permute-start(bf16[2,80,1024]{2,1,0:T(8,128)(2,1)S(1)} %get-tuple-element.115), channel_id=1, source_target_pairs={{0,16},{1,17},{2,18},{3,19},{4,20},{5,21},{6,22},{7,23},{8,24},{9,... | collective-permute-start | bytes 983048 | tf_op jit(solution)/shard_map/ppermute | solution.py:38
  114.3 49.4 %copy-start.3 = (bf16[1024,2048]{1,0:T(8,128)(2,1)}, bf16[1024,2048]{1,0:T(8,128)(2,1)S(1)}, u32[]{:S(2)}) copy-start(bf16[1024,2048]{1,0:T(8,128)(2,1)S(1)} %shard_map.265.refs_9_.refs_1_.refs_2_.refs_6_.refs_3_) | copy-start | bytes 12582916
  125.6 6.2 %collective-permute-start.23 = (bf16[7,128,1024]{2,1,0:T(8,128)(2,1)S(1)}, bf16[7,128,1024]{2,1,0:T(8,128)(2,1)S(1)}, u32[]{:S(2)}, u32[]{:S(2)}) collective-permute-start(bf16[7,128,1024]{2,1,0:T(8,128)(2,1)S(1)} %get-tuple-element.116.refs_4_), channel_id=1, source_target_pairs={{0,1},{1,0},{2,3},{3,2},{4,5},{5,4},{6,7},{7,6},{8,9},{9,8},{10,11... | collective-permute-start | bytes 5505032 | tf_op jit(solution)/shard_map/ppermute | solution.py:38
  126.2 17.2 %collective-permute-start.20 = (bf16[7,128,384]{2,1,0:T(8,128)(2,1)S(1)}, bf16[7,128,384]{2,1,0:T(8,128)(2,1)S(1)}, u32[]{:S(2)}, u32[]{:S(2)}) collective-permute-start(bf16[7,128,384]{2,1,0:T(8,128)(2,1)S(1)} %get-tuple-element.120), channel_id=1, source_target_pairs={{0,2},{1,3},{2,0},{3,1},{4,6},{5,7},{6,4},{7,5},{8,10},{9,11},{10,... | collective-permute-start | bytes 2064392 | tf_op jit(solution)/shard_map/ppermute | solution.py:38
  126.4 17.0 %collective-permute-start.21 = (bf16[4,80,1024]{2,1,0:T(8,128)(2,1)S(1)}, bf16[4,80,1024]{2,1,0:T(8,128)(2,1)S(1)}, u32[]{:S(2)}, u32[]{:S(2)}) collective-permute-start(bf16[4,80,1024]{2,1,0:T(8,128)(2,1)S(1)} %get-tuple-element.121), channel_id=1, source_target_pairs={{0,4},{1,5},{2,6},{3,7},{4,0},{5,1},{6,2},{7,3},{8,12},{9,13},{10,... | collective-permute-start | bytes 1966088 | tf_op jit(solution)/shard_map/ppermute | solution.py:38
  126.7 16.7 %collective-permute-start.22 = (bf16[2,80,1024]{2,1,0:T(8,128)(2,1)S(1)}, bf16[2,80,1024]{2,1,0:T(8,128)(2,1)S(1)}, u32[]{:S(2)}, u32[]{:S(2)}) collective-permute-start(bf16[2,80,1024]{2,1,0:T(8,128)(2,1)S(1)} %get-tuple-element.122), channel_id=1, source_target_pairs={{0,16},{1,17},{2,18},{3,19},{4,20},{5,21},{6,22},{7,23},{8,24},{9,... | collective-permute-start | bytes 983048 | tf_op jit(solution)/shard_map/ppermute | solution.py:38
  144.9 32.3 %collective-permute-start.26 = (bf16[7,128,1024]{2,1,0:T(8,128)(2,1)}, bf16[7,128,1024]{2,1,0:T(8,128)(2,1)}, u32[]{:S(2)}, u32[]{:S(2)}) collective-permute-start(bf16[7,128,1024]{2,1,0:T(8,128)(2,1)} %get-tuple-element.123.refs_7_), channel_id=1, source_target_pairs={{0,1},{1,0},{2,3},{3,2},{4,5},{5,4},{6,7},{7,6},{8,9},{9,8},{10,11... | collective-permute-start | bytes 5505032 | tf_op jit(solution)/shard_map/ppermute | solution.py:38
  145.5 17.1 %collective-permute-start.24 = (bf16[7,48,1024]{2,1,0:T(8,128)(2,1)S(1)}, bf16[7,48,1024]{2,1,0:T(8,128)(2,1)S(1)}, u32[]{:S(2)}, u32[]{:S(2)}) collective-permute-start(bf16[7,48,1024]{2,1,0:T(8,128)(2,1)S(1)} %get-tuple-element.125), channel_id=1, source_target_pairs={{0,2},{1,3},{2,0},{3,1},{4,6},{5,7},{6,4},{7,5},{8,10},{9,11},{10,... | collective-permute-start | bytes 2064392 | tf_op jit(solution)/shard_map/ppermute | solution.py:38
  146.3 16.0 %collective-permute-start.25 = (bf16[4,80,1024]{2,1,0:T(8,128)(2,1)S(1)}, bf16[4,80,1024]{2,1,0:T(8,128)(2,1)S(1)}, u32[]{:S(2)}, u32[]{:S(2)}) collective-permute-start(bf16[4,80,1024]{2,1,0:T(8,128)(2,1)S(1)} %get-tuple-element.126), channel_id=1, source_target_pairs={{0,4},{1,5},{2,6},{3,7},{4,0},{5,1},{6,2},{7,3},{8,12},{9,13},{10,... | collective-permute-start | bytes 1966088 | tf_op jit(solution)/shard_map/ppermute | solution.py:38
  162.8 18.5 %collective-permute-start.27 = (bf16[7,48,1024]{2,1,0:T(8,128)(2,1)S(1)}, bf16[7,48,1024]{2,1,0:T(8,128)(2,1)S(1)}, u32[]{:S(2)}, u32[]{:S(2)}) collective-permute-start(bf16[7,48,1024]{2,1,0:T(8,128)(2,1)S(1)} %get-tuple-element.133), channel_id=1, source_target_pairs={{0,2},{1,3},{2,0},{3,1},{4,6},{5,7},{6,4},{7,5},{8,10},{9,11},{10,... | collective-permute-start | bytes 2064392 | tf_op jit(solution)/shard_map/ppermute | solution.py:38
  177.2 46.0 %copy-start.13 = (bf16[1024,2048]{1,0:T(8,128)(2,1)}, bf16[1024,2048]{1,0:T(8,128)(2,1)S(1)}, u32[]{:S(2)}) copy-start(bf16[1024,2048]{1,0:T(8,128)(2,1)S(1)} %get-tuple-element.132.refs_7_.refs_1_.refs_0_) | copy-start | bytes 12582916
  200.6 22.6 %collective-permute-start.30 = (bf16[2,2,4,2,128,512]{5,4,3,2,1,0:T(8,128)(2,1)S(1)}, bf16[2,2,4,2,128,512]{5,4,3,2,1,0:T(8,128)(2,1)}, u32[]{:S(2)}, u32[]{:S(2)}) collective-permute-start(bf16[2,2,4,2,128,512]{5,4,3,2,1,0:T(8,128)(2,1)S(1)} %shard_map.277.refs_7_), channel_id=1, source_target_pairs={{0,1},{1,0},{2,3},{3,2},{4,5},{5,4},{6,7},{7,6},{8,9},{9,8},{10,11... | collective-permute-start | bytes 12582920 | tf_op jit(solution)/shard_map/ppermute | solution.py:38
  201.7 9.3 %collective-permute-start.28 = (bf16[7,128,1024]{2,1,0:T(8,128)(2,1)S(1)}, bf16[7,128,1024]{2,1,0:T(8,128)(2,1)S(1)}, u32[]{:S(2)}, u32[]{:S(2)}) collective-permute-start(bf16[7,128,1024]{2,1,0:T(8,128)(2,1)S(1)} %get-tuple-element.128.refs_6_), channel_id=1, source_target_pairs={{0,1},{1,0},{2,3},{3,2},{4,5},{5,4},{6,7},{7,6},{8,9},{9,8},{10,11... | collective-permute-start | bytes 5505032 | tf_op jit(solution)/shard_map/ppermute | solution.py:38
  201.8 34.0 %collective-permute-start.29 = (bf16[7,128,1024]{2,1,0:T(8,128)(2,1)S(1)}, bf16[7,128,1024]{2,1,0:T(8,128)(2,1)S(1)}, u32[]{:S(2)}, u32[]{:S(2)}) collective-permute-start(bf16[7,128,1024]{2,1,0:T(8,128)(2,1)S(1)} %shard_map.275.refs_3_), channel_id=1, source_target_pairs={{0,1},{1,0},{2,3},{3,2},{4,5},{5,4},{6,7},{7,6},{8,9},{9,8},{10,11... | collective-permute-start | bytes 5505032 | tf_op jit(solution)/shard_map/ppermute | solution.py:38
  234.2 39.7 %collective-permute-start.31 = (bf16[2,2,2,128,512]{4,3,2,1,0:T(8,128)(2,1)}, bf16[2,2,2,128,512]{4,3,2,1,0:T(8,128)(2,1)}, u32[]{:S(2)}, u32[]{:S(2)}) collective-permute-start(bf16[2,2,2,128,512]{4,3,2,1,0:T(8,128)(2,1)} %get-tuple-element.137.refs_7_), channel_id=1, source_target_pairs={{0,2},{1,3},{2,0},{3,1},{4,6},{5,7},{6,4},{7,5},{8,10},{9,11},{10,... | collective-permute-start | bytes 3145736 | tf_op jit(solution)/shard_map/ppermute | solution.py:38
  234.9 39.0 %collective-permute-start.32 = (bf16[2,2,2,128,512]{4,3,2,1,0:T(8,128)(2,1)}, bf16[2,2,2,128,512]{4,3,2,1,0:T(8,128)(2,1)S(1)}, u32[]{:S(2)}, u32[]{:S(2)}) collective-permute-start(bf16[2,2,2,128,512]{4,3,2,1,0:T(8,128)(2,1)} %get-tuple-element.145), channel_id=1, source_target_pairs={{0,4},{1,5},{2,6},{3,7},{4,0},{5,1},{6,2},{7,3},{8,12},{9,13},{10,... | collective-permute-start | bytes 3145736 | tf_op jit(solution)/shard_map/ppermute | solution.py:38
  289.6 14.5 %collective-permute-start.33 = (bf16[2,2,4,64,2560]{4,3,2,1,0:T(8,128)(2,1)S(1)}, bf16[2,2,4,64,2560]{4,3,2,1,0:T(8,128)(2,1)S(1)}, u32[]{:S(2)}, u32[]{:S(2)}) collective-permute-start(bf16[2,2,4,64,2560]{4,3,2,1,0:T(8,128)(2,1)S(1)} %shard_map.285.refs_5_), channel_id=1, source_target_pairs={{0,1},{1,0},{2,3},{3,2},{4,5},{5,4},{6,7},{7,6},{8,9},{9,8},{10,11... | collective-permute-start | bytes 15728648 | tf_op jit(solution)/shard_map/ppermute | solution.py:38
  290.4 13.5 %collective-permute-start.34 = (bf16[2,2,128,512]{3,2,1,0:T(8,128)(2,1)S(1)}, bf16[2,2,128,512]{3,2,1,0:T(8,128)(2,1)S(1)}, u32[]{:S(2)}, u32[]{:S(2)}) collective-permute-start(bf16[2,2,128,512]{3,2,1,0:T(8,128)(2,1)S(1)} %get-tuple-element.148), channel_id=1, source_target_pairs={{0,2},{1,3},{2,0},{3,1},{4,6},{5,7},{6,4},{7,5},{8,10},{9,11},{10,... | collective-permute-start | bytes 1572872 | tf_op jit(solution)/shard_map/ppermute | solution.py:38
  337.5 47.9 %collective-permute-start.35 = (bf16[2,2,4,64,1536]{4,3,2,1,0:T(8,128)(2,1)S(1)}, bf16[2,2,4,64,1536]{4,3,2,1,0:T(8,128)(2,1)}, u32[]{:S(2)}, u32[]{:S(2)}) collective-permute-start(bf16[2,2,4,64,1536]{4,3,2,1,0:T(8,128)(2,1)S(1)} %shard_map.290.refs_9_), channel_id=1, source_target_pairs={{0,1},{1,0},{2,3},{3,2},{4,5},{5,4},{6,7},{7,6},{8,9},{9,8},{10,11... | collective-permute-start | bytes 9437192 | tf_op jit(solution)/shard_map/ppermute | solution.py:38
  338.4 42.3 %collective-permute-start.38 = (bf16[2,2,64,2560]{3,2,1,0:T(8,128)(2,1)S(1)}, bf16[2,2,64,2560]{3,2,1,0:T(8,128)(2,1)S(1)}, u32[]{:S(2)}, u32[]{:S(2)}) collective-permute-start(bf16[2,2,64,2560]{3,2,1,0:T(8,128)(2,1)S(1)} %copy-done.98), channel_id=1, source_target_pairs={{0,2},{1,3},{2,0},{3,1},{4,6},{5,7},{6,4},{7,5},{8,10},{9,11},{10,... | collective-permute-start | bytes 3932168 | tf_op jit(solution)/shard_map/ppermute | solution.py:38
  339.5 41.3 %collective-permute-start.39 = (bf16[2,2,64,2560]{3,2,1,0:T(8,128)(2,1)S(1)}, bf16[2,2,64,2560]{3,2,1,0:T(8,128)(2,1)S(1)}, u32[]{:S(2)}, u32[]{:S(2)}) collective-permute-start(bf16[2,2,64,2560]{3,2,1,0:T(8,128)(2,1)S(1)} %copy-done.107), channel_id=1, source_target_pairs={{0,4},{1,5},{2,6},{3,7},{4,0},{5,1},{6,2},{7,3},{8,12},{9,13},{10,... | collective-permute-start | bytes 3932168 | tf_op jit(solution)/shard_map/ppermute | solution.py:38
  339.8 41.0 %collective-permute-start.36 = (bf16[2,2,128,512]{3,2,1,0:T(8,128)(2,1)S(1)}, bf16[2,2,128,512]{3,2,1,0:T(8,128)(2,1)S(1)}, u32[]{:S(2)}, u32[]{:S(2)}) collective-permute-start(bf16[2,2,128,512]{3,2,1,0:T(8,128)(2,1)S(1)} %copy-done.102), channel_id=1, source_target_pairs={{0,4},{1,5},{2,6},{3,7},{4,0},{5,1},{6,2},{7,3},{8,12},{9,13},{10,... | collective-permute-start | bytes 1572872 | tf_op jit(solution)/shard_map/ppermute | solution.py:38
  341.0 39.8 %collective-permute-start.37 = (bf16[2,2,128,512]{3,2,1,0:T(8,128)(2,1)S(1)}, bf16[2,2,128,512]{3,2,1,0:T(8,128)(2,1)S(1)}, u32[]{:S(2)}, u32[]{:S(2)}) collective-permute-start(bf16[2,2,128,512]{3,2,1,0:T(8,128)(2,1)S(1)} %shard_map.287.refs_6_), channel_id=1, source_target_pairs={{0,16},{1,17},{2,18},{3,19},{4,20},{5,21},{6,22},{7,23},{8,24},{9,... | collective-permute-start | bytes 1572872 | tf_op jit(solution)/shard_map/ppermute | solution.py:38
  393.3 31.9 %collective-permute-start.43 = (bf16[2,2,64,1536]{3,2,1,0:T(8,128)(2,1)S(1)}, bf16[2,2,64,1536]{3,2,1,0:T(8,128)(2,1)S(1)}, u32[]{:S(2)}, u32[]{:S(2)}) collective-permute-start(bf16[2,2,64,1536]{3,2,1,0:T(8,128)(2,1)S(1)} %get-tuple-element.160.refs_6_), channel_id=1, source_target_pairs={{0,2},{1,3},{2,0},{3,1},{4,6},{5,7},{6,4},{7,5},{8,10},{9,11},{10,... | collective-permute-start | bytes 2359304 | tf_op jit(solution)/shard_map/ppermute | solution.py:38
  393.7 31.5 %collective-permute-start.44 = (bf16[2,2,64,1536]{3,2,1,0:T(8,128)(2,1)}, bf16[2,2,64,1536]{3,2,1,0:T(8,128)(2,1)S(1)}, u32[]{:S(2)}, u32[]{:S(2)}) collective-permute-start(bf16[2,2,64,1536]{3,2,1,0:T(8,128)(2,1)} %get-tuple-element.165), channel_id=1, source_target_pairs={{0,4},{1,5},{2,6},{3,7},{4,0},{5,1},{6,2},{7,3},{8,12},{9,13},{10,... | collective-permute-start | bytes 2359304 | tf_op jit(solution)/shard_map/ppermute | solution.py:38
  394.3 30.9 %collective-permute-start.42 = (bf16[2,64,2560]{2,1,0:T(8,128)(2,1)}, bf16[2,64,2560]{2,1,0:T(8,128)(2,1)S(1)}, u32[]{:S(2)}, u32[]{:S(2)}) collective-permute-start(bf16[2,64,2560]{2,1,0:T(8,128)(2,1)} %get-tuple-element.162), channel_id=1, source_target_pairs={{0,2},{1,3},{2,0},{3,1},{4,6},{5,7},{6,4},{7,5},{8,10},{9,11},{10,... | collective-permute-start | bytes 1966088 | tf_op jit(solution)/shard_map/ppermute | solution.py:38
  395.0 17.0 %collective-permute-start.41 = (bf16[2,128,512]{2,1,0:T(8,128)(2,1)S(1)}, bf16[2,128,512]{2,1,0:T(8,128)(2,1)S(1)}, u32[]{:S(2)}, u32[]{:S(2)}) collective-permute-start(bf16[2,128,512]{2,1,0:T(8,128)(2,1)S(1)} %get-tuple-element.159.refs_4_), channel_id=1, source_target_pairs={{0,8},{1,9},{2,10},{3,11},{4,12},{5,13},{6,14},{7,15},{8,0},{9,1},... | collective-permute-start | bytes 786440 | tf_op jit(solution)/shard_map/ppermute | solution.py:38
  395.0 60.1 %collective-permute-start.40 = (bf16[2,64,2560]{2,1,0:T(8,128)(2,1)}, bf16[2,64,2560]{2,1,0:T(8,128)(2,1)S(1)}, u32[]{:S(2)}, u32[]{:S(2)}) collective-permute-start(bf16[2,64,2560]{2,1,0:T(8,128)(2,1)} %get-tuple-element.161), channel_id=1, source_target_pairs={{0,4},{1,5},{2,6},{3,7},{4,0},{5,1},{6,2},{7,3},{8,12},{9,13},{10,... | collective-permute-start | bytes 1966088 | tf_op jit(solution)/shard_map/ppermute | solution.py:38
  430.7 44.2 %collective-permute-start.45 = (bf16[2,64,2560]{2,1,0:T(8,128)(2,1)}, bf16[2,64,2560]{2,1,0:T(8,128)(2,1)}, u32[]{:S(2)}, u32[]{:S(2)}) collective-permute-start(bf16[2,64,2560]{2,1,0:T(8,128)(2,1)} %get-tuple-element.166), channel_id=1, source_target_pairs={{0,16},{1,17},{2,18},{3,19},{4,20},{5,21},{6,22},{7,23},{8,24},{9,... | collective-permute-start | bytes 1966088 | tf_op jit(solution)/shard_map/ppermute | solution.py:38
  430.7 8.0 %collective-permute-start.47 = (bf16[2,128,512]{2,1,0:T(8,128)(2,1)}, bf16[2,128,512]{2,1,0:T(8,128)(2,1)}, u32[]{:S(2)}, u32[]{:S(2)}) collective-permute-start(bf16[2,128,512]{2,1,0:T(8,128)(2,1)} %get-tuple-element.168.refs_1_.refs_5_), channel_id=1, source_target_pairs={{0,2},{1,3},{2,0},{3,1},{4,6},{5,7},{6,4},{7,5},{8,10},{9,11},{10,... | collective-permute-start | bytes 786440 | tf_op jit(solution)/shard_map/ppermute | solution.py:38
  431.1 15.6 %collective-permute-start.46 = (bf16[2,64,1536]{2,1,0:T(8,128)(2,1)}, bf16[2,64,1536]{2,1,0:T(8,128)(2,1)}, u32[]{:S(2)}, u32[]{:S(2)}) collective-permute-start(bf16[2,64,1536]{2,1,0:T(8,128)(2,1)} %get-tuple-element.167), channel_id=1, source_target_pairs={{0,2},{1,3},{2,0},{3,1},{4,6},{5,7},{6,4},{7,5},{8,10},{9,11},{10,... | collective-permute-start | bytes 1179656 | tf_op jit(solution)/shard_map/ppermute | solution.py:38
  432.1 47.0 %all-to-all-start = ((f32[32,24,128]{2,1,0:T(8,128)}), f32[32,24,128]{2,1,0:T(8,128)}, u32[]{:S(2)}, u32[]{:S(2)}) async-start(f32[32,24,128]{2,1,0:T(8,128)} %shard_map.294.refs_6_), calls=%async_computation | async-start | bytes 786432 | tf_op jit(solution)/shard_map/all_to_all | solution.py:1259
  438.3 4.1 collective-permute-start.48
  438.7 5.0 collective-permute-start.49
  442.3 40.2 %collective-permute-start.50 = (bf16[2,64,1536]{2,1,0:T(8,128)(2,1)}, bf16[2,64,1536]{2,1,0:T(8,128)(2,1)}, u32[]{:S(2)}, u32[]{:S(2)}) collective-permute-start(bf16[2,64,1536]{2,1,0:T(8,128)(2,1)} %copy-done.108), channel_id=1, source_target_pairs={{0,4},{1,5},{2,6},{3,7},{4,0},{5,1},{6,2},{7,3},{8,12},{9,13},{10,... | collective-permute-start | bytes 1179656 | tf_op jit(solution)/shard_map/ppermute | solution.py:38
  452.5 35.1 %collective-permute-start.51 = (bf16[2,64,1536]{2,1,0:T(8,128)(2,1)}, bf16[2,64,1536]{2,1,0:T(8,128)(2,1)}, u32[]{:S(2)}, u32[]{:S(2)}) collective-permute-start(bf16[2,64,1536]{2,1,0:T(8,128)(2,1)} %shard_map.298.refs_4_), channel_id=1, source_target_pairs={{0,16},{1,17},{2,18},{3,19},{4,20},{5,21},{6,22},{7,23},{8,24},{9,... | collective-permute-start | bytes 1179656 | tf_op jit(solution)/shard_map/ppermute | solution.py:38
  476.9 17.7 %collective-permute-start.52 = (bf16[64,2560]{1,0:T(8,128)(2,1)}, bf16[64,2560]{1,0:T(8,128)(2,1)}, u32[]{:S(2)}, u32[]{:S(2)}) collective-permute-start(bf16[64,2560]{1,0:T(8,128)(2,1)} %shard_map.299.refs_1_), channel_id=1, source_target_pairs={{0,8},{1,9},{2,10},{3,11},{4,12},{5,13},{6,14},{7,15},{8,0},{9,1},... | collective-permute-start | bytes 983048 | tf_op jit(solution)/shard_map/ppermute | solution.py:38
  499.4 8.9 %collective-permute-start.57 = (bf16[64,2560]{1,0:T(8,128)(2,1)S(1)}, bf16[64,2560]{1,0:T(8,128)(2,1)S(1)}, u32[]{:S(2)}, u32[]{:S(2)}) collective-permute-start(bf16[64,2560]{1,0:T(8,128)(2,1)S(1)} %get-tuple-element.173.refs_5_.refs_1_), channel_id=1, source_target_pairs={{0,2},{1,3},{2,0},{3,1},{4,6},{5,7},{6,4},{7,5},{8,10},{9,11},{10,... | collective-permute-start | bytes 983048 | tf_op jit(solution)/shard_map/ppermute | solution.py:38
  499.8 5.7 %collective-permute-start.53 = (bf16[64,1536]{1,0:T(8,128)(2,1)S(1)}, bf16[64,1536]{1,0:T(8,128)(2,1)S(1)}, u32[]{:S(2)}, u32[]{:S(2)}) collective-permute-start(bf16[64,1536]{1,0:T(8,128)(2,1)S(1)} %get-tuple-element.172), channel_id=1, source_target_pairs={{0,8},{1,9},{2,10},{3,11},{4,12},{5,13},{6,14},{7,15},{8,0},{9,1},... | collective-permute-start | bytes 589832 | tf_op jit(solution)/shard_map/ppermute | solution.py:38
  499.9 14.9 %collective-permute-start.58 = (bf16[64,2560]{1,0:T(8,128)(2,1)S(1)}, bf16[64,2560]{1,0:T(8,128)(2,1)S(1)}, u32[]{:S(2)}, u32[]{:S(2)}) collective-permute-start(bf16[64,2560]{1,0:T(8,128)(2,1)S(1)} %get-tuple-element.173.refs_5_.refs_1_), channel_id=1, source_target_pairs={{0,1},{1,0},{2,3},{3,2},{4,5},{5,4},{6,7},{7,6},{8,9},{9,8},{10,11... | collective-permute-start | bytes 983048 | tf_op jit(solution)/shard_map/ppermute | solution.py:38
  506.8 4.6 collective-permute-start.54
  508.2 6.5 %collective-permute-start.59 = (bf16[64,2560]{1,0:T(8,128)(2,1)S(1)}, bf16[64,2560]{1,0:T(8,128)(2,1)S(1)}, u32[]{:S(2)}, u32[]{:S(2)}) collective-permute-start(bf16[64,2560]{1,0:T(8,128)(2,1)S(1)} %collective-permute-done.57.refs_2_), channel_id=1, source_target_pairs={{0,1},{1,0},{2,3},{3,2},{4,5},{5,4},{6,7},{7,6},{8,9},{9,8},{10,11... | collective-permute-start | bytes 983048 | tf_op jit(solution)/shard_map/ppermute | solution.py:38
  510.4 6.6 %collective-permute-start.55 = (bf16[64,1536]{1,0:T(8,128)(2,1)S(1)}, bf16[64,1536]{1,0:T(8,128)(2,1)S(1)}, u32[]{:S(2)}, u32[]{:S(2)}) collective-permute-start(bf16[64,1536]{1,0:T(8,128)(2,1)S(1)} %shard_map.302.refs_5_.refs_1_), channel_id=1, source_target_pairs={{0,1},{1,0},{2,3},{3,2},{4,5},{5,4},{6,7},{7,6},{8,9},{9,8},{10,11... | collective-permute-start | bytes 589832 | tf_op jit(solution)/shard_map/ppermute | solution.py:38
  511.3 5.6 %collective-permute-start.56 = (bf16[64,1536]{1,0:T(8,128)(2,1)S(1)}, bf16[64,1536]{1,0:T(8,128)(2,1)S(1)}, u32[]{:S(2)}, u32[]{:S(2)}) collective-permute-start(bf16[64,1536]{1,0:T(8,128)(2,1)S(1)} %collective-permute-done.54.refs_2_), channel_id=1, source_target_pairs={{0,1},{1,0},{2,3},{3,2},{4,5},{5,4},{6,7},{7,6},{8,9},{9,8},{10,11... | collective-permute-start | bytes 589832 | tf_op jit(solution)/shard_map/ppermute | solution.py:38
  (117 other events, 1225.5 us)
